TPU v7x, 512 devices: a whole 4x4x16 slice. The times are simulated.
512 devices in a mesh: island: 8 (over x, z_hi), fsdp: 8 (over z_lo), tensor: 8 (over y, core).
Axes of the slice: x: 4, y: 4, z: 16 (z_hi: 2, z_lo: 8; z = z_hi * 8 + z_lo), core: 2. Of those that a mesh axis runs over, the one named last changes fastest.
Arguments:
- x_saved: bfloat16 [8, 4096, 8192], P('island', 'fsdp', 'tensor'), may hold values from -6 to 6
- grad_keys: bfloat16 [8, 4096, 1024], P('island', 'fsdp'), may hold values from -0.09375 to 0.09375
- inner_weight: bfloat16 [8, 1024, 8192], P('island', 'fsdp', 'tensor'), may hold values from -0.0625 to 0.0625
- outer_weight: float32 [1024, 8, 8, 128], P('fsdp', 'tensor', 'island'), may hold values from -0.0625 to 0.0625
- outer_momentum: float32 [1024, 8, 8, 128], P('fsdp', 'tensor', 'island'), may hold values from -0.06 to 0.06
- x_next: bfloat16 [8, 4096, 8192], P('island', 'fsdp', 'tensor'), may hold values from -250 to 250
- norm_gain: float32 [8192], P('tensor'), may hold values from 0.1 to 1.9
Outputs:
- keys_next: bfloat16 [8, 4096, 1024], P('island', 'fsdp', 'tensor')
All inputs are finite; a program needn't handle non-finite values.
Results may differ from a plain program's by a relative error of at most 0.029.
Values may be sent and summed in bfloat16 or wider, within the bound.
No kernel may reach another device: no remote copies, remote signals or barrier semaphores. Data moves between devices by JAX's collectives and lax.ppermute only.
A program may use at most 64 MiB of HBM per device.

v0:
```python
import jax
import jax.numpy as jnp
from jax import lax
from jax.sharding import PartitionSpec as P

D = 8192


def per_device(x_saved, grad_keys, inner_weight, outer_weight, outer_momentum, x_next, norm_gain):
    saved = x_saved[0]
    cotangent = grad_keys[0]
    rows_here = inner_weight.shape[1]
    islands = lax.axis_size("island")
    width = outer_weight.shape[3]
    tok_rows = saved.shape[0]
    gradient = lax.psum_scatter(
        lax.dot_general(
            cotangent, saved, (((0,), (0,)), ((), ())), preferred_element_type=jnp.float32
        ).astype(jnp.bfloat16),
        "fsdp",
        scatter_dimension=0,
        tiled=True,
    ).astype(jnp.float32)
    updated = inner_weight[0].astype(jnp.float32) - 0.03 * gradient
    summed = lax.psum_scatter(
        updated.reshape(rows_here, islands, width).astype(jnp.bfloat16),
        "island",
        scatter_dimension=1,
        tiled=True,
    ).astype(jnp.float32)
    replica_total = summed.reshape(rows_here, width)
    theta = outer_weight.reshape(rows_here, width)
    mean_delta = theta - replica_total / islands
    momentum = 0.9 * outer_momentum.reshape(rows_here, width) + mean_delta
    theta_new = theta - 0.7 * (mean_delta + 0.9 * momentum)
    fresh = theta_new.astype(jnp.bfloat16)
    raw = x_next[0].astype(jnp.float32)
    squares = lax.psum(jnp.sum(raw * raw, axis=1), "tensor")
    scale = lax.rsqrt(squares / D + 1e-05)
    normed = (raw * scale[:, None] * norm_gain[None, :]).astype(jnp.bfloat16)
    gathered = lax.all_gather(fresh[None], ("island", "fsdp"), axis=0, tiled=True)
    gathered = gathered.reshape(islands, -1, rows_here, width)
    partial_value = jnp.einsum(
        "tic,ifrc->tfr",
        normed.reshape(tok_rows, islands, width),
        gathered,
        preferred_element_type=jnp.float32,
    )
    partial_value = partial_value.reshape(tok_rows, -1)
    keys_here = lax.psum_scatter(
        partial_value.astype(jnp.bfloat16), "tensor", scatter_dimension=1, tiled=True
    )
    return keys_here[None]


def solution(mesh):
    placed = (
        P("island", "fsdp", "tensor"),
        P("island", "fsdp", None),
        P("island", "fsdp", "tensor"),
        P("fsdp", "tensor", "island", None),
        P("fsdp", "tensor", "island", None),
        P("island", "fsdp", "tensor"),
        P("tensor"),
    )
    return jax.shard_map(
        per_device,
        mesh=mesh,
        in_specs=placed,
        out_specs=P("island", "fsdp", "tensor"),
        check_vma=False,
    )
```

profile of v0, /device:TPU:1, one launch (start us, length us, event | category | flops | bytes accessed | tf_op | source)
XLA Modules:
  0.0 381.4 jit_solution(10115741261189794547)
XLA Ops:
  6.5 0.0 copy-start
  6.5 0.0 reduce-scatter.6.cloned.1.call-start
  6.5 1.2 copy-done
  7.8 3.8 %convolution_convert_fusion = bf16[1024,1024]{1,0:T(8,128)(2,1)} fusion(bf16[1,512,1024]{2,1,0:T(8,128)(2,1)S(1)} %copy-done, bf16[1,512,1024]{2,1,0:T(8,128)(2,1)} %param.8), kind=kOutput, calls=%fused_computation.7 | convolution fusion | flops 1074790400 | bytes 4194304 | tf_op jit(solution)/shard_map/dot_general | solution.py:17
  11.6 0.0 copy-start.2
  11.6 0.0 copy-start.3
  11.6 0.0 copy-start.4
  11.6 0.0 copy-start.1
  11.6 0.0 reduce-scatter.6.cloned.1.call-update
  11.6 0.0 reduce-scatter.8.cloned.1.call-start
  11.7 73.5 %reduce-scatter.6.cloned.1.call-done = bf16[128,1024]{1,0:T(8,128)(2,1)} async-done(((bf16[1024,1024]{1,0:T(8,128)(2,1)}), bf16[128,1024]{1,0:T(8,128)(2,1)}) %reduce-scatter.6.cloned.1.call-update) | async-done | bytes 262160 | tf_op jit(solution)/shard_map/reduce_scatter | solution.py:16
  85.2 0.0 copy-done.2
  85.2 1.7 copy_bitcast_fusion
  87.0 0.0 reduce-scatter.8.cloned.1.call-update
  87.0 0.0 all-gather.2.cloned.1.call-start
  87.0 110.9 %reduce-scatter.8.cloned.1.call-done = bf16[128,1,128]{2,0,1:T(8,128)(2,1)} async-done(((bf16[128,8,128]{2,0,1:T(8,128)(2,1)}), bf16[128,1,128]{2,0,1:T(8,128)(2,1)}) %reduce-scatter.8.cloned.1.call-update) | async-done | bytes 32784 | tf_op jit(solution)/shard_map/reduce_scatter | solution.py:25
  198.0 0.0 copy-done.3
  198.0 0.0 copy-done.4
  198.0 1.4 fusion.14
  199.4 0.0 all-gather.2.cloned.1.call-update
  199.4 0.0 reduce-scatter.10.cloned.1.call-start
  199.4 0.0 copy-done.1
  199.4 0.2 convert_bitcast_fusion
  199.7 0.0 copy-start.5
  199.7 1.8 copy.16
  201.5 0.3 fusion
  201.8 13.5 %psum.7 = f32[512]{0:T(512)S(1)} all-reduce(f32[512]{0:T(512)S(1)} %fusion), channel_id=1, replica_groups=mesh['island'=8,'fsdp'=8,'tensor'=8] {'tensor'}, use_global_device_ids=true, to_apply=%region_1.0 | all-reduce | flops 512 | bytes 4096 | tf_op jit(solution)/shard_map/psum | solution.py:38
  215.2 110.3 %all-gather.2.cloned.1.call-done = bf16[64,128,128]{2,1,0:T(8,128)(2,1)} async-done(((bf16[1,128,128]{2,1,0:T(8,128)(2,1)}), bf16[64,128,128]{2,1,0:T(8,128)(2,1)}) %all-gather.2.cloned.1.call-update) | async-done | bytes 2097168 | tf_op jit(solution)/shard_map/all_gather | solution.py:41
  325.5 0.0 copy-done.5
  325.5 3.5 bitcast_convert_fusion
  329.0 1.3 copy.13
  330.3 0.0 reduce-scatter.10.cloned.1.call-update
  330.4 42.9 %reduce-scatter.10.cloned.1.call-done = bf16[128,512]{1,0:T(8,128)(2,1)} async-done(((bf16[1024,512]{1,0:T(8,128)(2,1)}), bf16[128,512]{1,0:T(8,128)(2,1)}) %reduce-scatter.10.cloned.1.call-update) | async-done | bytes 131088
  373.2 1.7 copy.14
  (1 shorter events, 0.0 us)
Async XLA Ops:
  6.5 1.2 copy-start
  6.5 78.7 %reduce-scatter.6.cloned.1.call-start = ((), (), s32[]{:S(2)}) async-start(), calls=%async_computation.3 | async-start | bytes 2359296 | tf_op jit(solution)/shard_map/reduce_scatter | solution.py:16
  11.6 73.6 %copy-start.2 = (bf16[1,128,1024]{2,1,0:T(8,128)(2,1)S(1)}, bf16[1,128,1024]{2,1,0:T(8,128)(2,1)}, u32[]{:S(2)}) copy-start(bf16[1,128,1024]{2,1,0:T(8,128)(2,1)} %param.9) | copy-start | bytes 786436
  11.6 186.3 %copy-start.3 = (f32[128,1,1,128]{3,2,1,0:T(1,128)S(1)}, f32[128,1,1,128]{3,2,1,0:T(1,128)}, u32[]{:S(2)}) copy-start(f32[128,1,1,128]{3,2,1,0:T(1,128)} %param.10) | copy-start | bytes 196612
  11.6 186.3 %copy-start.4 = (f32[128,1,1,128]{3,2,1,0:T(1,128)S(1)}, f32[128,1,1,128]{3,2,1,0:T(1,128)}, u32[]{:S(2)}) copy-start(f32[128,1,1,128]{3,2,1,0:T(1,128)} %param.11) | copy-start | bytes 196612
  11.6 187.8 %copy-start.1 = (bf16[1,512,1024]{2,1,0:T(8,128)(2,1)S(1)}, bf16[1,512,1024]{2,1,0:T(8,128)(2,1)}, u32[]{:S(2)}) copy-start(bf16[1,512,1024]{2,1,0:T(8,128)(2,1)} %param.12) | copy-start | bytes 3145732
  11.6 186.3 %reduce-scatter.8.cloned.1.call-start = ((), (), s32[]{:S(2)}) async-start(), calls=%async_computation.4 | async-start | bytes 294912 | tf_op jit(solution)/shard_map/reduce_scatter | solution.py:25
  87.0 238.5 %all-gather.2.cloned.1.call-start = ((), (), s32[]{:S(2)}) async-start(), calls=%async_computation.5 | async-start | bytes 2129920 | tf_op jit(solution)/shard_map/all_gather | solution.py:41
  199.4 173.9 %reduce-scatter.10.cloned.1.call-start = ((), (), s32[]{:S(2)}) async-start(), calls=%async_computation.6 | async-start | bytes 1179648
  199.7 125.8 %copy-start.5 = (f32[1024]{0:T(1024)S(1)}, f32[1024]{0:T(1024)}, u32[]{:S(2)}) copy-start(f32[1024]{0:T(1024)} %param.13) | copy-start | bytes 12292
Sparse Core Ops, SparseCore 0:
  11.8 73.4 reduce-scatter.5
  89.7 108.2 reduce-scatter.7
  201.3 124.1 all-gather.1
  330.5 42.7 reduce-scatter.9
where the time goes:
time: 383 us; the launch traced here: 381 us
  waiting for transfers between devices  338 us (88%)
  blocking collectives  13.5 us (4%)
  between operations  13.2 us (3%)
  matrix products  7.37 us (2%)
  local copies, waits for them, and re-layouts  6 us (2%)
    reduce_scatter x1, waiting for transfers between devices, per_device(): lax.psum_scatter(updated.reshape(rows_here, islands, width).astype(jnp.bf...  111 us
    all_gather x1, waiting for transfers between devices, per_device(): lax.all_gather(fresh[None], ('island', 'fsdp'), axis=0, tiled=True)  110 us
    reduce_scatter x1, waiting for transfers between devices, per_device(): lax.psum_scatter(lax.dot_general(cotangent, saved, (((0,), (0,)), ((), ()...  73.5 us
    unnamed x5, waiting for transfers between devices  42.9 us
    psum x1, blocking collectives, per_device(): squares = lax.psum(jnp.sum(raw * raw, axis=1), 'tensor')  13.5 us
  transfers between devices with their start and end apart: 4, of which 4 were waited for; matrix products, arithmetic and copies ran while one was open for 1% of the time, Pallas kernels for 0%

commit v1 on v0

v1 whole, which is shorter than its diff:
```python
import jax
import jax.numpy as jnp
from jax import lax
from jax.sharding import Mesh, PartitionSpec as P

D = 8192
ISLANDS = 8
AXES = ("x", "z3", "z2", "z1", "z0", "y", "c")
NEAR = ("x", "z0")
FAR = ("z3", "z2", "z1")
ISLAND = ("x", "z3")
FSDP = ("z2", "z1", "z0")
TENSOR = ("y", "c")
STEP = 0.7 * 1.9
F32, BF16 = jnp.float32, jnp.bfloat16


def exchange(blocks, axes):
    return lax.all_to_all(blocks, axes, 0, 0)


def total(blocks):
    return jnp.sum(blocks.astype(F32), axis=0)


def spread(block, axes):
    everywhere = jnp.broadcast_to(block[None], (8, *block.shape))
    return exchange(everywhere, axes).reshape(-1, block.shape[-1])


def per_device(x_saved, grad_keys, inner_weight, outer_weight, outer_momentum, x_next, norm_gain):
    rows, width = outer_weight.shape[0], outer_weight.shape[3]
    island, fsdp = lax.axis_index(ISLAND), lax.axis_index(FSDP)
    term = lax.dot_general(
        grad_keys[0], x_saved[0], (((0,), (0,)), ((), ())), preferred_element_type=F32
    )
    share = STEP / ISLANDS
    theta = outer_weight.reshape(rows, width)
    momentum = outer_momentum.reshape(rows, width)
    own = (1.0 - STEP) * theta - 0.7 * 0.9 * 0.9 * momentum
    band = share * inner_weight[0].astype(F32)
    place = island * width
    band = lax.dynamic_update_slice(
        band, lax.dynamic_slice(band, (0, place), (rows, width)) + own, (0, place)
    )
    term = (-0.03 * share) * term
    start = fsdp * rows
    term = lax.dynamic_update_slice(
        term, lax.dynamic_slice(term, (start, 0), band.shape) + band, (start, 0)
    )
    features = term.shape[1]
    sums = total(exchange(term.astype(BF16).reshape(8, -1, features), NEAR)).astype(BF16)
    fresh = total(exchange(sums.reshape(8, -1, features), FAR)).astype(BF16)
    weight = spread(spread(fresh, FAR), NEAR)

    raw = x_next[0].astype(F32)
    squares = total(lax.all_gather(jnp.sum(raw * raw, axis=1), TENSOR, axis=0))
    scale = lax.rsqrt(squares / D + 1e-05)
    gained = (raw * norm_gain[None, :]).astype(BF16)
    partial = lax.dot_general(
        weight, gained, (((1,), (1,)), ((), ())), preferred_element_type=F32
    )
    tokens = partial.shape[1]
    keys = total(exchange(partial.astype(BF16).reshape(8, -1, tokens), TENSOR))
    return (keys * scale[None, :]).T.astype(BF16)[None]


def solution(mesh):
    fine = Mesh(mesh.devices.reshape(4, 2, 2, 2, 2, 4, 2), AXES)
    placed = (
        P(ISLAND, FSDP, TENSOR),
        P(ISLAND, FSDP, None),
        P(ISLAND, FSDP, TENSOR),
        P(FSDP, TENSOR, ISLAND, None),
        P(FSDP, TENSOR, ISLAND, None),
        P(ISLAND, FSDP, TENSOR),
        P(TENSOR),
    )
    return jax.shard_map(
        per_device,
        mesh=fine,
        in_specs=placed,
        out_specs=P(ISLAND, FSDP, TENSOR),
        check_vma=False,
    )
```

time: 383 us -> 153 us (0.40)
  waiting for transfers between devices: 338 us -> 0.01 us
  blocking collectives: 13.5 us -> 133 us
  between operations: 13.2 us -> 0.12 us
  starting transfers between devices: 0.13 us -> 8.71 us
  local copies, waits for them, and re-layouts: 6 us -> 1.19 us
    reduce_scatter x2 -> x0, waiting for transfers between devices: 184 us -> none  [the longest x1 111 us: per_device(): lax.psum_scatter(updated.reshape(rows_here, islands, width).astype(jnp.bf...]
    all_to_all x0 -> x4, blocking collectives: none -> 113 us  [exchange(): return lax.all_to_all(blocks, axes, 0, 0)]
    all_gather x1 -> x0, waiting for transfers between devices: 110 us -> none  [per_device(): lax.all_gather(fresh[None], ('island', 'fsdp'), axis=0, tiled=True)]
    unnamed x5 -> x0, waiting for transfers between devices: 42.9 us -> none
    all_gather x0 -> x1, blocking collectives: none -> 20.1 us  [per_device(): squares = total(lax.all_gather(jnp.sum(raw * raw, axis=1), TENSOR, axis=0))]
    psum x1 -> x0, blocking collectives: 13.5 us -> none  [per_device(): squares = lax.psum(jnp.sum(raw * raw, axis=1), 'tensor')]
    all_to_all x0 -> x1, starting transfers between devices: none -> 8.71 us  [exchange(): return lax.all_to_all(blocks, axes, 0, 0)]
    unnamed x15 -> x10, local copies, waits for them, and re-layouts: 6 us -> 0.16 us
  transfers between devices with their start and end apart: 4 -> 1, of which waited for: 4 -> 0; matrix products, arithmetic and copies ran while one was open for 1% -> 0% of each run, Pallas kernels for 0% -> 0%
where the time goes in v1:
time: 153 us; the launch traced here: 151 us
  blocking collectives  133 us (87%)
  starting transfers between devices  8.71 us (6%)
  matrix products  4.83 us (3%)
  other arithmetic  2.49 us (2%)
    all_to_all x4, blocking collectives, exchange(): return lax.all_to_all(blocks, axes, 0, 0)  113 us
    all_gather x1, blocking collectives, per_device(): squares = total(lax.all_gather(jnp.sum(raw * raw, axis=1), TENSOR, axis=0))  20.1 us
    all_to_all x1, starting transfers between devices, exchange(): return lax.all_to_all(blocks, axes, 0, 0)  8.71 us
  transfers between devices with their start and end apart: 1, of which 0 were waited for; matrix products, arithmetic and copies ran while one was open for 0% of the time, Pallas kernels for 0%

profile of v1, /device:TPU:1, one launch (start us, length us, event | category | flops | bytes accessed | tf_op | source)
XLA Modules:
  0.0 150.6 jit_solution(16985203247626157714)
XLA Ops:
  0.0 0.0 copy-start
  0.0 1.2 convert_multiply_fusion.2
  1.2 0.1 copy-done
  1.3 0.0 copy-start.2
  1.3 0.0 copy-start.3
  1.3 2.5 %convolution_multiply_fusion = f32[1024,1024]{1,0:T(8,128)S(1)} fusion(bf16[1,512,1024]{2,1,0:T(8,128)(2,1)S(1)} %copy-done, bf16[1,512,1024]{2,1,0:T(8,128)(2,1)} %param.8), kind=kOutput, calls=%fused_computation.2 | convolution fusion | flops 1074790400 | bytes 6291456 | tf_op jit(solution)/shard_map/dot_general | solution.py:34
  3.9 0.0 copy-done.2
  3.9 0.0 copy-done.3
  3.9 0.1 add_dynamic-update-slice_fusion
  4.0 0.3 convert_element_type.35
  4.4 29.6 %all_to_all.25 = bf16[8,128,1024]{2,1,0:T(8,128)(2,1)S(1)} all-to-all(bf16[8,128,1024]{2,1,0:T(8,128)(2,1)S(1)} %bitcast.30), channel_id=1, replica_groups=mesh['x'=4,'z3'=2,'z2'=2,'z1'=2,'z0'=2,'y'=4,'c'=2] {'x','z0'}, dimensions={0} | all-to-all | bytes 4194304 | tf_op jit(solution)/shard_map/all_to_all | solution.py:19
  34.0 0.4 reduce_sum.51
  34.4 34.1 %all_to_all.26 = bf16[8,16,1024]{2,1,0:T(8,128)(2,1)S(1)} all-to-all(bf16[8,16,1024]{2,1,0:T(8,128)(2,1)S(1)} %bitcast.32), channel_id=1, replica_groups=mesh['x'=4,'z3'=2,'z2'=2,'z1'=2,'z0'=2,'y'=4,'c'=2] {'z3','z2','z1'}, dimensions={0} | all-to-all | bytes 524288 | tf_op jit(solution)/shard_map/all_to_all | solution.py:19
  68.5 23.3 %all_to_all.27 = bf16[8,16,1024]{2,1,0:T(8,128)(2,1)S(1)} all-to-all(bf16[8,16,1024]{2,1,0:T(8,128)(2,1)S(1)} %broadcast_in_dim.8), channel_id=1, replica_groups=mesh['x'=4,'z3'=2,'z2'=2,'z1'=2,'z0'=2,'y'=4,'c'=2] {'z3','z2','z1'}, dimensions={0} | all-to-all | bytes 524288 | tf_op jit(solution)/shard_map/all_to_all | solution.py:19
  91.8 0.3 broadcast_in_dim.20
  92.0 0.0 copy-start.1
  92.0 0.0 copy-start.4
  92.0 26.2 %all_to_all.28 = bf16[8,128,1024]{2,1,0:T(8,128)(2,1)S(1)} all-to-all(bf16[8,128,1024]{2,1,0:T(8,128)(2,1)S(1)} %broadcast_in_dim.20), channel_id=1, replica_groups=mesh['x'=4,'z3'=2,'z2'=2,'z1'=2,'z0'=2,'y'=4,'c'=2] {'x','z0'}, dimensions={0} | all-to-all | bytes 4194304 | tf_op jit(solution)/shard_map/all_to_all | solution.py:19
  118.3 0.0 copy-done.1
  118.3 0.0 copy-done.4
  118.3 2.3 %convolution_convert_fusion = bf16[1024,512]{1,0:T(8,128)(2,1)} fusion(bf16[1024,1024]{1,0:T(8,128)(2,1)S(1)} %bitcast.31, bf16[1,512,1024]{2,1,0:T(8,128)(2,1)S(1)} %copy-done.1, f32[1024]{0:T(1024)S(1)} %copy-done.4), kind=kOutput, calls=%fused_computation.6 | convolution fusion | flops 1075838976 | bytes 4198400 | tf_op jit(solution)/shard_map/dot_general | solution.py:60
  120.6 8.7 %all-to-all-start.4 = ((bf16[8,128,512]{2,1,0:T(8,128)(2,1)}), bf16[8,128,512]{2,1,0:T(8,128)(2,1)S(1)}, u32[]{:S(2)}, u32[]{:S(2)}) async-start(bf16[8,128,512]{2,1,0:T(8,128)(2,1)} %bitcast.34), calls=%async_computation.4 | async-start | bytes 2097152 | tf_op jit(solution)/shard_map/all_to_all | solution.py:19
  129.3 0.3 fusion.1
  129.6 20.1 %all-gather.1 = f32[8,1,512]{2,1,0:T(1,128)S(1)} all-gather(f32[1,1,512]{2,1,0:T(1,128)S(1)} %bitcast.37), channel_id=2, replica_groups=mesh['x'=4,'z3'=2,'z2'=2,'z1'=2,'z0'=2,'y'=4,'c'=2] {'y','c'}, dimensions={0}, use_global_device_ids=true | all-gather | bytes 18432 | tf_op jit(solution)/shard_map/all_gather | solution.py:57
  149.7 0.0 all-to-all-done.4
  149.7 0.1 convert_reduce_fusion
  149.9 0.8 copy.15
  (6 shorter events, 0.1 us)
Async XLA Ops:
  0.0 1.3 copy-start
  1.3 2.6 %copy-start.2 = (f32[128,1,1,128]{3,2,1,0:T(1,128)S(1)}, f32[128,1,1,128]{3,2,1,0:T(1,128)}, u32[]{:S(2)}) copy-start(f32[128,1,1,128]{3,2,1,0:T(1,128)} %param.11) | copy-start | bytes 196612
  1.3 2.6 %copy-start.3 = (f32[128,1,1,128]{3,2,1,0:T(1,128)S(1)}, f32[128,1,1,128]{3,2,1,0:T(1,128)}, u32[]{:S(2)}) copy-start(f32[128,1,1,128]{3,2,1,0:T(1,128)} %param.10) | copy-start | bytes 196612
  92.0 26.3 %copy-start.1 = (bf16[1,512,1024]{2,1,0:T(8,128)(2,1)S(1)}, bf16[1,512,1024]{2,1,0:T(8,128)(2,1)}, u32[]{:S(2)}) copy-start(bf16[1,512,1024]{2,1,0:T(8,128)(2,1)} %param.12) | copy-start | bytes 3145732
  92.0 26.3 %copy-start.4 = (f32[1024]{0:T(1024)S(1)}, f32[1024]{0:T(1024)}, u32[]{:S(2)}) copy-start(f32[1024]{0:T(1024)} %param.13) | copy-start | bytes 12292
  120.6 29.1 %all-to-all-start.4 = ((bf16[8,128,512]{2,1,0:T(8,128)(2,1)}), bf16[8,128,512]{2,1,0:T(8,128)(2,1)S(1)}, u32[]{:S(2)}, u32[]{:S(2)}) async-start(bf16[8,128,512]{2,1,0:T(8,128)(2,1)} %bitcast.34), calls=%async_computation.4 | async-start | bytes 2097152 | tf_op jit(solution)/shard_map/all_to_all | solution.py:19

commit v2 on v1

v2 whole, which is shorter than its diff:
```python
import jax
import jax.numpy as jnp
from jax import lax
from jax.experimental import pallas as pl
from jax.experimental.pallas import tpu as pltpu
from jax.sharding import Mesh, PartitionSpec as P

D = 8192
ISLANDS = 8
R = 128
AXES = ("x", "z3", "z2", "z1", "z0", "y", "c")
NEAR = ("x", "z0")
FAR = ("z3", "z2", "z1")
ISLAND = ("x", "z3")
FSDP = ("z2", "z1", "z0")
TENSOR = ("y", "c")
STEP = 0.7 * 1.9
SHARE = STEP / ISLANDS
F32, BF16 = jnp.float32, jnp.bfloat16


def exchange(blocks, axes):
    return lax.all_to_all(blocks, axes, 0, 0)


def total(blocks):
    return jnp.sum(blocks.astype(F32), axis=0)


def project_kernel(x_ref, w_ref, out_ref, acc_ref, squares_ref):
    step = pl.program_id(0)

    @pl.when(step == 0)
    def _():
        acc_ref[...] = jnp.zeros_like(acc_ref)
        squares_ref[...] = jnp.zeros_like(squares_ref)

    x = x_ref[0]
    weight = w_ref[...].reshape(-1, R)
    acc_ref[...] += jnp.dot(x, weight, preferred_element_type=F32)
    squares = squares_ref[...]
    for j in range(x.shape[1] // R):
        part = x[:, j * R : (j + 1) * R].astype(F32)
        squares += part * part
    squares_ref[...] = squares

    @pl.when(step == pl.num_programs(0) - 1)
    def _():
        mean = jnp.sum(squares_ref[...], axis=1, keepdims=True) / D
        out_ref[...] = (acc_ref[...] * lax.rsqrt(mean + 1e-05)).astype(BF16)


def project(x_all, weight):
    blocks, tokens, features = x_all.shape
    return pl.pallas_call(
        project_kernel,
        grid=(blocks,),
        in_specs=[
            pl.BlockSpec((1, tokens, features), lambda s: (s, 0, 0)),
            pl.BlockSpec((8, 1, R, R), lambda s: (0, s, 0, 0)),
        ],
        out_specs=pl.BlockSpec((tokens, R), lambda s: (0, 0)),
        out_shape=jax.ShapeDtypeStruct((tokens, R), BF16),
        scratch_shapes=[pltpu.VMEM((tokens, R), F32), pltpu.VMEM((tokens, R), F32)],
        compiler_params=pltpu.CompilerParams(vmem_limit_bytes=24 * 2**20),
        cost_estimate=pl.CostEstimate(
            flops=2 * blocks * tokens * features * R,
            bytes_accessed=2 * blocks * (tokens * features + features * R),
            transcendentals=tokens,
        ),
    )(x_all, weight)


def per_device(x_saved, grad_keys, inner_weight, outer_weight, outer_momentum, x_next, norm_gain):
    rows, width = outer_weight.shape[0], outer_weight.shape[3]
    island, fsdp = lax.axis_index(ISLAND), lax.axis_index(FSDP)
    x_all = lax.all_gather(x_next[0], TENSOR, axis=0)

    term = lax.dot_general(
        x_saved[0], grad_keys[0], (((0,), (0,)), ((), ())), preferred_element_type=F32
    )
    theta = outer_weight.reshape(rows, width)
    momentum = outer_momentum.reshape(rows, width)
    own = (1.0 - STEP) * theta - 0.7 * 0.9 * 0.9 * momentum
    band = SHARE * inner_weight[0].astype(F32)
    place = island * width
    band = lax.dynamic_update_slice(
        band, lax.dynamic_slice(band, (0, place), (rows, width)) + own, (0, place)
    )
    band = band.T
    term = (-0.03 * SHARE) * term
    start = fsdp * rows
    term = lax.dynamic_update_slice(
        term, lax.dynamic_slice(term, (0, start), band.shape) + band, (0, start)
    )
    term = (term * norm_gain[:, None]).astype(BF16)
    keys = term.shape[1]
    sums = total(exchange(term.reshape(8, -1, keys), NEAR)).astype(BF16)
    fresh = total(exchange(sums.reshape(8, -1, keys), FAR)).astype(BF16)
    depth = fresh.shape[0]
    pieces = fresh.reshape(depth, 8, R).transpose(1, 0, 2)
    pieces = jnp.broadcast_to(pieces[:, None], (8, 8, depth, R)).reshape(64, depth, R)
    mine = exchange(pieces, TENSOR + FAR).reshape(8, 8 * depth, R)
    mine, x_all = lax.optimization_barrier((mine, x_all))
    weight = exchange(jnp.broadcast_to(mine[None], (8, *mine.shape)), NEAR)
    return project(x_all, weight)[None]


def solution(mesh):
    fine = Mesh(mesh.devices.reshape(4, 2, 2, 2, 2, 4, 2), AXES)
    placed = (
        P(ISLAND, FSDP, TENSOR),
        P(ISLAND, FSDP, None),
        P(ISLAND, FSDP, TENSOR),
        P(FSDP, TENSOR, ISLAND, None),
        P(FSDP, TENSOR, ISLAND, None),
        P(ISLAND, FSDP, TENSOR),
        P(TENSOR),
    )
    return jax.shard_map(
        per_device,
        mesh=fine,
        in_specs=placed,
        out_specs=P(ISLAND, FSDP, TENSOR),
        check_vma=False,
    )
```

time: 153 us -> 154 us (level); the launches traced: 151 us -> 153 us
  between operations: 0.12 us -> 13.5 us
  blocking collectives: 133 us -> 124 us
  starting transfers between devices: 8.71 us -> 0.01 us
  local copies, waits for them, and re-layouts: 1.19 us -> 6.92 us
  Pallas kernels: 0 us -> 4.74 us
  matrix products: 4.83 us -> 2.52 us
  other arithmetic: 2.49 us -> 0.95 us
    all_gather x1 -> x0, blocking collectives: 20.1 us -> none  [per_device(): squares = total(lax.all_gather(jnp.sum(raw * raw, axis=1), TENSOR, axis=0))]
    all_to_all x4, blocking collectives: 113 us -> 124 us  [exchange(): return lax.all_to_all(blocks, axes, 0, 0)]
    all_to_all x1 -> x0, starting transfers between devices: 8.71 us -> none  [exchange(): return lax.all_to_all(blocks, axes, 0, 0)]
    unnamed x10, local copies, waits for them, and re-layouts: 0.16 us -> 6.38 us
    pallas_call x0 -> x1, Pallas kernels: none -> 4.74 us  [project(): pl.pallas_call(project_kernel, grid=(blocks,), in_specs=[pl.BlockSpec((1,...]
    dot_general x2 -> x1, matrix products: 4.83 us -> 2.52 us  [per_device(): lax.dot_general(x_saved[0], grad_keys[0], (((0,), (0,)), ((), ())), prefe...]
  transfers between devices with their start and end apart: 1 -> 1, of which waited for: 0 -> 0; matrix products, arithmetic and copies ran while one was open for 0% -> 4% of each run, Pallas kernels for 0% -> 0%
where the time goes in v2:
time: 154 us; the launch traced here: 153 us
  blocking collectives  124 us (81%)
  between operations  13.5 us (9%)
  local copies, waits for them, and re-layouts  6.92 us (4%)
  Pallas kernels  4.74 us (3%)
  matrix products  2.52 us (2%)
    all_to_all x4, blocking collectives, exchange(): return lax.all_to_all(blocks, axes, 0, 0)  124 us
    unnamed x10, local copies, waits for them, and re-layouts  6.38 us
    pallas_call x1, Pallas kernels, project(): pl.pallas_call(project_kernel, grid=(blocks,), in_specs=[pl.BlockSpec((1,...  4.74 us
  transfers between devices with their start and end apart: 1, of which 0 were waited for; matrix products, arithmetic and copies ran while one was open for 4% of the time, Pallas kernels for 0%

profile of v2, /device:TPU:1, one launch (start us, length us, event | category | flops | bytes accessed | tf_op | source)
XLA Modules:
  0.0 153.2 jit_solution(3540423882991218122)
XLA Ops:
  6.5 0.0 copy-start
  6.5 0.0 all-gather.2.cloned.1.call-start
  6.5 0.7 all-gather.2.cloned.1.call-update
  7.3 1.1 copy.19
  8.4 0.9 copy.21
  9.3 0.9 copy.20
  10.3 0.1 convert_multiply_fusion
  10.4 0.0 copy-done
  10.4 0.0 copy-start.2
  10.4 2.5 %convolution_multiply_fusion = f32[1024,1024]{1,0:T(8,128)S(1)} fusion(bf16[1,512,1024]{2,1,0:T(8,128)(2,1)S(1)} %copy-done, bf16[1,512,1024]{2,1,0:T(8,128)(2,1)} %param.7), kind=kOutput, calls=%fused_computation.1 | convolution fusion | flops 1074790400 | bytes 6291456 | tf_op jit(solution)/shard_map/dot_general | solution.py:79
  12.9 0.2 fusion.2
  13.1 0.0 copy-done.2
  13.1 0.3 multiply_convert_fusion
  13.4 29.6 %all_to_all.20 = bf16[8,128,1024]{2,1,0:T(8,128)(2,1)S(1)} all-to-all(bf16[8,128,1024]{2,1,0:T(8,128)(2,1)S(1)} %bitcast.27), channel_id=1, replica_groups=mesh['x'=4,'z3'=2,'z2'=2,'z1'=2,'z0'=2,'y'=4,'c'=2] {'x','z0'}, dimensions={0} | all-to-all | bytes 4194304 | tf_op jit(solution)/shard_map/all_to_all | solution.py:23
  43.1 0.4 reduce_sum.24
  43.4 34.1 %all_to_all.21 = bf16[8,16,1024]{2,1,0:T(8,128)(2,1)S(1)} all-to-all(bf16[8,16,1024]{2,1,0:T(8,128)(2,1)S(1)} %bitcast.29), channel_id=1, replica_groups=mesh['x'=4,'z3'=2,'z2'=2,'z1'=2,'z0'=2,'y'=4,'c'=2] {'z3','z2','z1'}, dimensions={0} | all-to-all | bytes 524288 | tf_op jit(solution)/shard_map/all_to_all | solution.py:23
  77.6 30.7 %all_to_all.22 = bf16[64,16,128]{2,1,0:T(8,128)(2,1)S(1)} all-to-all(bf16[64,16,128]{2,1,0:T(8,128)(2,1)S(1)} %bitcast.30), channel_id=1, replica_groups=mesh['x'=4,'z3'=2,'z2'=2,'z1'=2,'z0'=2,'y'=4,'c'=2] {'y','c','z3','z2','..., dimensions={0} | all-to-all | bytes 524288 | tf_op jit(solution)/shard_map/all_to_all | solution.py:23
  108.3 0.0 all-gather.2.cloned.1.call-done.x_ref
  108.3 0.5 broadcast_in_dim.7
  108.8 29.4 %all_to_all.23.w_ref = bf16[8,8,128,128]{3,2,1,0:T(8,128)(2,1)S(1)} all-to-all(bf16[8,8,128,128]{3,2,1,0:T(8,128)(2,1)S(1)} %broadcast_in_dim.7), channel_id=1, replica_groups=mesh['x'=4,'z3'=2,'z2'=2,'z1'=2,'z0'=2,'y'=4,'c'=2] {'x','z0'}, dimensions={0} | all-to-all | bytes 4194304 | tf_op jit(solution)/shard_map/all_to_all | solution.py:23
  138.3 0.0 copy-start.1
  138.3 3.4 %copy-done.1 = bf16[8,512,1024]{2,1,0:T(8,128)(2,1)S(1)} copy-done((bf16[8,512,1024]{2,1,0:T(8,128)(2,1)S(1)}, bf16[8,512,1024]{2,1,0:T(8,128)(2,1)}, u32[]{:S(2)}) %copy-start.1) | copy-done | bytes 8388632
  141.7 4.7 %shard_map.73 = bf16[512,128]{1,0:T(8,128)(2,1)} custom-call(bf16[8,512,1024]{2,1,0:T(8,128)(2,1)S(1)} %copy-done.1, bf16[8,8,128,128]{3,2,1,0:T(8,128)(2,1)S(1)} %all_to_all.23.w_ref), custom_call_target="tpu_custom_call" | custom-call | flops 1073741824 | bytes 10485760 | tf_op jit(solution)/shard_map/pallas_call | solution.py:55
  (5 shorter events, 0.1 us)
Async XLA Ops:
  6.5 3.9 %copy-start = (bf16[1,512,1024]{2,1,0:T(8,128)(2,1)S(1)}, bf16[1,512,1024]{2,1,0:T(8,128)(2,1)}, u32[]{:S(2)}) copy-start(bf16[1,512,1024]{2,1,0:T(8,128)(2,1)} %param.8) | copy-start | bytes 3145732
  6.5 101.8 %all-gather.2.cloned.1.call-start = ((), (), s32[]{:S(2)}) async-start(), calls=%async_computation.4 | async-start | bytes 9437184 | tf_op jit(solution)/shard_map/all_gather | solution.py:77
  10.4 2.7 %copy-start.2 = (f32[1024]{0:T(1024)S(1)}, f32[1024]{0:T(1024)}, u32[]{:S(2)}) copy-start(f32[1024]{0:T(1024)} %param.13) | copy-start | bytes 12292
  138.3 3.4 %copy-start.1 = (bf16[8,512,1024]{2,1,0:T(8,128)(2,1)S(1)}, bf16[8,512,1024]{2,1,0:T(8,128)(2,1)}, u32[]{:S(2)}) copy-start(bf16[8,512,1024]{2,1,0:T(8,128)(2,1)} %all-gather.2.cloned.1.call-done.x_ref) | copy-start | bytes 25165828
Sparse Core Ops, SparseCore 0:
  9.5 63.1 all-gather.1

commit v3 on v1

v3 whole, which is shorter than its diff:
```python
import jax
import jax.numpy as jnp
from jax import lax
from jax.experimental import pallas as pl
from jax.experimental.pallas import tpu as pltpu
from jax.sharding import Mesh, PartitionSpec as P

D = 8192
ISLANDS = 8
R = 128
AXES = ("x", "z3", "z2", "z1", "z0", "y", "c")
NEAR = ("x", "z0")
FAR = ("z3", "z2", "z1")
ISLAND = ("x", "z3")
FSDP = ("z2", "z1", "z0")
TENSOR = ("y", "c")
STEP = 0.7 * 1.9
SHARE = STEP / ISLANDS
F32, BF16 = jnp.float32, jnp.bfloat16
VMEM = 16 * 2**20


def exchange(blocks, axes):
    return lax.all_to_all(blocks, axes, 0, 0)


def total(blocks):
    return jnp.sum(blocks.astype(F32), axis=0)


def share_kernel(place_ref, x_ref, g_ref, w_ref, theta_ref, momentum_ref, gain_ref, out_ref):
    step = pl.program_id(0)
    width = x_ref.shape[1]
    term = lax.dot_general(
        x_ref[...], g_ref[...], (((0,), (0,)), ((), ())), preferred_element_type=F32
    )
    own = (1.0 - STEP) * theta_ref[...] - 0.7 * 0.9 * 0.9 * momentum_ref[...]
    band = []
    for j in range(width // R):
        here = place_ref[0] == step * (width // R) + j
        band.append(SHARE * w_ref[:, j * R : (j + 1) * R].astype(F32) + jnp.where(here, own, 0.0))
    band = jnp.concatenate(band, axis=1).T
    gain = jnp.broadcast_to(gain_ref[...], (R, width)).T
    for j in range(out_ref.shape[1] // R):
        piece = (-0.03 * SHARE) * term[:, j * R : (j + 1) * R]
        piece += jnp.where(place_ref[1] == j, band, 0.0)
        out_ref[:, j * R : (j + 1) * R] = (piece * gain).astype(BF16)


def share(place, x, g, weight, theta, momentum, gain):
    tokens, features = x.shape
    keys = g.shape[1]
    width = 4 * R
    whole = lambda *shape: pl.BlockSpec(shape, lambda i: (0, 0))
    return pl.pallas_call(
        share_kernel,
        grid=(features // width,),
        in_specs=[
            pl.BlockSpec(memory_space=pltpu.SMEM),
            pl.BlockSpec((tokens, width), lambda i: (0, i)),
            whole(tokens, keys),
            pl.BlockSpec((R, width), lambda i: (0, i)),
            whole(R, R),
            whole(R, R),
            pl.BlockSpec((1, width), lambda i: (0, i)),
        ],
        out_specs=pl.BlockSpec((width, keys), lambda i: (i, 0)),
        out_shape=jax.ShapeDtypeStruct((features, keys), BF16),
        compiler_params=pltpu.CompilerParams(vmem_limit_bytes=60 * 2**20),
        cost_estimate=pl.CostEstimate(
            flops=2 * tokens * features * keys, bytes_accessed=6 * 2**20, transcendentals=0
        ),
    )(place, x, g, weight, theta, momentum, gain)


def scale_kernel(*refs):
    x_refs, out_ref, x_all, sems = refs[:8], *refs[8:]
    copies = [
        pltpu.make_async_copy(x_ref, x_all.at[block], sems.at[block])
        for block, x_ref in enumerate(x_refs)
    ]
    for copy in copies:
        copy.start()
    for copy in copies:
        copy.wait()

    @pl.loop(0, out_ref.shape[0] // 64)
    def _(i):
        rows = pl.ds(pl.multiple_of(i * 64, 64), 64)
        squares = jnp.zeros((64, R), F32)
        for block in range(8):
            for j in range(x_all.shape[2] // R):
                part = x_all[block, rows, j * R : (j + 1) * R].astype(F32)
                squares += part * part
        mean = jnp.sum(squares, axis=1, keepdims=True) / D
        out_ref[rows, :] = jnp.broadcast_to(lax.rsqrt(mean + 1e-05), (64, R))


def scales(blocks):
    tokens, features = blocks[0].shape
    vmem = pl.BlockSpec(memory_space=pltpu.VMEM)
    return pl.pallas_call(
        scale_kernel,
        in_specs=[pl.BlockSpec(memory_space=pl.ANY)] * 8,
        out_specs=(vmem, vmem),
        out_shape=(
            jax.ShapeDtypeStruct((tokens, R), F32),
            jax.ShapeDtypeStruct((8, tokens, features), BF16),
        ),
        scratch_shapes=[pltpu.SemaphoreType.DMA((8,))],
        compiler_params=pltpu.CompilerParams(vmem_limit_bytes=VMEM),
        cost_estimate=pl.CostEstimate(
            flops=16 * tokens * features,
            bytes_accessed=32 * tokens * features,
            transcendentals=tokens,
        ),
    )(*blocks)


def project_kernel(own_ref, scale_ref, w_ref, x_ref, out_ref):
    acc = jnp.zeros(out_ref.shape, F32)
    for block in range(8):
        weight = w_ref[:, pl.ds(own_ref[0] ^ block, 1)].reshape(-1, R)
        acc += jnp.dot(x_ref[block], weight, preferred_element_type=F32)
    out_ref[...] = (acc * scale_ref[...]).astype(BF16)


def project(own, scale, weight, x_all):
    tokens, features = x_all.shape[1:]
    vmem = pl.BlockSpec(memory_space=pltpu.VMEM)
    return pl.pallas_call(
        project_kernel,
        in_specs=[pl.BlockSpec(memory_space=pltpu.SMEM)] + [vmem] * 3,
        out_specs=vmem,
        out_shape=jax.ShapeDtypeStruct((tokens, R), BF16),
        compiler_params=pltpu.CompilerParams(vmem_limit_bytes=VMEM),
        cost_estimate=pl.CostEstimate(
            flops=16 * tokens * features * R,
            bytes_accessed=16 * (tokens * features + features * R),
            transcendentals=0,
        ),
    )(own, scale, weight, x_all)


def swap(block, bits):
    return lax.ppermute(block, TENSOR, [(t, t ^ bits) for t in range(8)])


def per_device(x_saved, grad_keys, inner_weight, outer_weight, outer_momentum, x_next, norm_gain):
    rows, width = outer_weight.shape[0], outer_weight.shape[3]
    place = jnp.stack([lax.axis_index(ISLAND), lax.axis_index(FSDP)]).astype(jnp.int32)
    term = share(
        place,
        x_saved[0],
        grad_keys[0],
        inner_weight[0],
        outer_weight.reshape(rows, width),
        outer_momentum.reshape(rows, width),
        norm_gain[None],
    )
    keys = term.shape[1]
    x_own = x_next[0]
    x_core, x_up, x_down, x_far = (swap(x_own, bits) for bits in (1, 2, 6, 4))
    sums = exchange(term.reshape(8, -1, keys), NEAR)
    sums, x_core = lax.optimization_barrier((sums, x_core))
    fresh = exchange(total(sums).astype(BF16).reshape(8, -1, keys), FAR)
    fresh, x_up, x_down, x_far = lax.optimization_barrier((fresh, x_up, x_down, x_far))
    fresh = total(fresh).astype(BF16)
    depth = fresh.shape[0]
    pieces = fresh.reshape(depth, 8, R).transpose(1, 0, 2)
    pieces = jnp.broadcast_to(pieces[:, None], (8, 8, depth, R)).reshape(64, depth, R)
    mine = exchange(pieces, TENSOR + FAR).reshape(8, 8 * depth, R)
    mine, x_up, x_down, x_far = lax.optimization_barrier((mine, x_up, x_down, x_far))
    x_up_core, x_down_core, x_far_core = swap(x_up, 1), swap(x_down, 1), swap(x_far, 1)
    blocks = (x_own, x_core, x_up, x_up_core, x_far, x_far_core, x_down, x_down_core)
    scale, x_all = scales(blocks)
    weight = exchange(jnp.broadcast_to(mine[None], (8, *mine.shape)), NEAR)
    own = lax.axis_index(TENSOR).astype(jnp.int32)[None]
    return project(own, scale, weight, x_all)[None]


def solution(mesh):
    fine = Mesh(mesh.devices.reshape(4, 2, 2, 2, 2, 4, 2), AXES)
    placed = (
        P(ISLAND, FSDP, TENSOR),
        P(ISLAND, FSDP, None),
        P(ISLAND, FSDP, TENSOR),
        P(FSDP, TENSOR, ISLAND, None),
        P(FSDP, TENSOR, ISLAND, None),
        P(ISLAND, FSDP, TENSOR),
        P(TENSOR),
    )
    return jax.shard_map(
        per_device,
        mesh=fine,
        in_specs=placed,
        out_specs=P(ISLAND, FSDP, TENSOR),
        check_vma=False,
    )
```

time: 153 us -> 145 us (0.948); the launches traced: 151 us -> 144 us
  blocking collectives: 133 us -> 31.3 us
  starting transfers between devices: 8.71 us -> 54.1 us
  waiting for transfers between devices: 0.01 us -> 30.1 us
  Pallas kernels: 0 us -> 12.2 us
  local copies, waits for them, and re-layouts: 1.19 us -> 13.2 us
  matrix products: 4.83 us -> 0 us
    all_to_all x4 -> x1, blocking collectives: 113 us -> 31.3 us  [exchange(): return lax.all_to_all(blocks, axes, 0, 0)]
    all_to_all x1 -> x3, starting transfers between devices: 8.71 us -> 31.5 us  [exchange(): return lax.all_to_all(blocks, axes, 0, 0)]
    ppermute x0 -> x7, starting transfers between devices: none -> 22.6 us  [swap(): return lax.ppermute(block, TENSOR, [(t, t ^ bits) for t in range(8)])]
    all_gather x1 -> x0, blocking collectives: 20.1 us -> none  [per_device(): squares = total(lax.all_gather(jnp.sum(raw * raw, axis=1), TENSOR, axis=0))]
    ppermute x0 -> x7, waiting for transfers between devices: none -> 17.7 us  [swap(): return lax.ppermute(block, TENSOR, [(t, t ^ bits) for t in range(8)])]
    all_to_all x1 -> x3, waiting for transfers between devices: 0.01 us -> 12.4 us  [exchange(): return lax.all_to_all(blocks, axes, 0, 0)]
    pallas_call x0 -> x3, Pallas kernels: none -> 12.2 us  [the longest x1 4.95 us: scales(): pl.pallas_call(scale_kernel, in_specs=[pl.BlockSpec(memory_space=pl.ANY)]...]
    unnamed x10 -> x19, local copies, waits for them, and re-layouts: 0.16 us -> 11.3 us
  transfers between devices with their start and end apart: 1 -> 10, of which waited for: 0 -> 6; matrix products, arithmetic and copies ran while one was open for 0% -> 2% of each run, Pallas kernels for 0% -> 3%
where the time goes in v3:
time: 145 us; the launch traced here: 144 us
  starting transfers between devices  54.1 us (37%)
  blocking collectives  31.3 us (22%)
  waiting for transfers between devices  30.1 us (21%)
  local copies, waits for them, and re-layouts  13.2 us (9%)
  Pallas kernels  12.2 us (8%)
  other arithmetic  3.33 us (2%)
    all_to_all x3, starting transfers between devices, exchange(): return lax.all_to_all(blocks, axes, 0, 0)  31.5 us
    all_to_all x1, blocking collectives, exchange(): return lax.all_to_all(blocks, axes, 0, 0)  31.3 us
    ppermute x7, starting transfers between devices, swap(): return lax.ppermute(block, TENSOR, [(t, t ^ bits) for t in range(8)])  22.6 us
    ppermute x7, waiting for transfers between devices, swap(): return lax.ppermute(block, TENSOR, [(t, t ^ bits) for t in range(8)])  17.7 us
    all_to_all x3, waiting for transfers between devices, exchange(): return lax.all_to_all(blocks, axes, 0, 0)  12.4 us
    unnamed x19, local copies, waits for them, and re-layouts  11.3 us
    pallas_call x1, Pallas kernels, scales(): pl.pallas_call(scale_kernel, in_specs=[pl.BlockSpec(memory_space=pl.ANY)]...  4.95 us
    pallas_call x1, Pallas kernels, share(): pl.pallas_call(share_kernel, grid=(features // width,), in_specs=[pl.Bloc...  4.28 us
  transfers between devices with their start and end apart: 10, of which 6 were waited for; matrix products, arithmetic and copies ran while one was open for 2% of the time, Pallas kernels for 3%

profile of v3, /device:TPU:1, one launch (start us, length us, event | category | flops | bytes accessed | tf_op | source)
XLA Modules:
  0.0 144.4 jit_solution(10218875843977148145)
XLA Ops:
  0.0 0.6 pad_add_fusion.place_ref
  0.6 4.3 %shard_map.73 = bf16[1024,1024]{1,0:T(8,128)(2,1)} custom-call(s32[2]{0:T(128)} %pad_add_fusion.place_ref, bf16[512,1024]{1,0:T(8,128)(2,1)} %bitcast.27, bf16[512,1024]{1,0:T(8,128)(2,1)} %bitcast.28, bf16[128,1024]{1,0:T(8,128)(2,1)} %bitcast.29, f32[128,128]{1,0:T(8,128)} %bitcast.32, f32[128,128]{1,0:T(8,128)} %bitcast.33, f32[1,1024]{1,0:T(1,128)} %bitcast.34), custom_call_target="tpu_custom_call" | custom-call | flops 1073741824 | bytes 6291456 | tf_op jit(solution)/shard_map/pallas_call | solution.py:55
  4.8 0.0 copy-start.2
  4.8 6.3 %all-to-all-start = ((bf16[8,128,1024]{2,1,0:T(8,128)(2,1)}), bf16[8,128,1024]{2,1,0:T(8,128)(2,1)}, u32[]{:S(2)}, u32[]{:S(2)}) async-start(bf16[8,128,1024]{2,1,0:T(8,128)(2,1)} %bitcast.24), calls=%async_computation | async-start | bytes 4194304 | tf_op jit(solution)/shard_map/all_to_all | solution.py:24
  11.2 0.0 copy-done.2
  11.2 6.9 %collective-permute-start = (bf16[512,1024]{1,0:T(8,128)(2,1)S(1)}, bf16[512,1024]{1,0:T(8,128)(2,1)S(1)}, u32[]{:S(2)}, u32[]{:S(2)}) collective-permute-start(bf16[512,1024]{1,0:T(8,128)(2,1)S(1)} %bitcast.19), channel_id=1, source_target_pairs={{0,1},{1,0},{2,3},{3,2},{4,5},{5,4},{6,7},{7,6},{8,9},{9,8},{10,11... | collective-permute-start | bytes 3145736 | tf_op jit(solution)/shard_map/ppermute | solution.py:146
  18.1 1.9 %collective-permute-start.3 = (bf16[512,1024]{1,0:T(8,128)(2,1)S(1)}, bf16[512,1024]{1,0:T(8,128)(2,1)S(1)}, u32[]{:S(2)}, u32[]{:S(2)}) collective-permute-start(bf16[512,1024]{1,0:T(8,128)(2,1)S(1)} %bitcast.20), channel_id=1, source_target_pairs={{0,4},{1,5},{2,6},{3,7},{4,0},{5,1},{6,2},{7,3},{8,12},{9,13},{10,... | collective-permute-start | bytes 3145736 | tf_op jit(solution)/shard_map/ppermute | solution.py:146
  20.0 1.9 %collective-permute-start.2 = (bf16[512,1024]{1,0:T(8,128)(2,1)S(1)}, bf16[512,1024]{1,0:T(8,128)(2,1)S(1)}, u32[]{:S(2)}, u32[]{:S(2)}) collective-permute-start(bf16[512,1024]{1,0:T(8,128)(2,1)S(1)} %bitcast.21), channel_id=1, source_target_pairs={{0,6},{1,7},{2,4},{3,5},{4,2},{5,3},{6,0},{7,1},{8,14},{9,15},{10,... | collective-permute-start | bytes 3145736 | tf_op jit(solution)/shard_map/ppermute | solution.py:146
  22.0 4.5 %collective-permute-start.1 = (bf16[512,1024]{1,0:T(8,128)(2,1)S(1)}, bf16[512,1024]{1,0:T(8,128)(2,1)}, u32[]{:S(2)}, u32[]{:S(2)}) collective-permute-start(bf16[512,1024]{1,0:T(8,128)(2,1)S(1)} %bitcast.22), channel_id=1, source_target_pairs={{0,2},{1,3},{2,0},{3,1},{4,6},{5,7},{6,4},{7,5},{8,10},{9,11},{10,... | collective-permute-start | bytes 3145736 | tf_op jit(solution)/shard_map/ppermute | solution.py:146
  26.5 0.0 collective-permute-done.refs_1_
  26.5 0.0 copy-start.3
  26.5 1.0 copy-done.3
  27.5 5.9 %all-to-all-done = bf16[8,128,1024]{2,1,0:T(8,128)(2,1)} async-done(((bf16[8,128,1024]{2,1,0:T(8,128)(2,1)}), bf16[8,128,1024]{2,1,0:T(8,128)(2,1)}, u32[]{:S(2)}, u32[]{:S(2)}) %all-to-all-start) | async-done | bytes 2097184 | tf_op jit(solution)/shard_map/all_to_all | solution.py:24
  33.4 2.7 %reduce_sum.24 = bf16[128,1024]{1,0:T(8,128)(2,1)} reduce(bf16[8,128,1024]{2,1,0:T(8,128)(2,1)} %all-to-all-done, bf16[]{:T(256)} %constant.34.clone.1), dimensions={0}, to_apply=%region_0.0 | reduce | flops 917504 | bytes 2359298 | tf_op jit(solution)/shard_map/reduce_sum | solution.py:28
  36.2 17.9 %all-to-all-start.1 = ((bf16[8,16,1024]{2,1,0:T(8,128)(2,1)}), bf16[8,16,1024]{2,1,0:T(8,128)(2,1)S(1)}, u32[]{:S(2)}, u32[]{:S(2)}) async-start(bf16[8,16,1024]{2,1,0:T(8,128)(2,1)} %bitcast.11), calls=%async_computation.1 | async-start | bytes 524288 | tf_op jit(solution)/shard_map/all_to_all | solution.py:24
  54.0 0.0 collective-permute-done.3.refs_4_
  54.0 0.0 copy-start.5
  54.0 15.1 %collective-permute-done.2.refs_6_ = bf16[512,1024]{1,0:T(8,128)(2,1)S(1)} collective-permute-done((bf16[512,1024]{1,0:T(8,128)(2,1)S(1)}, bf16[512,1024]{1,0:T(8,128)(2,1)S(1)}, u32[]{:S(2)}, u32[]{:S(2)}) %collective-permute-start.2) | collective-permute-done | bytes 1048608 | tf_op jit(solution)/shard_map/ppermute | solution.py:146
  69.1 0.0 copy-start.7
  69.1 0.0 collective-permute-done.1.refs_2_
  69.1 2.5 %all-to-all-done.1 = bf16[8,16,1024]{2,1,0:T(8,128)(2,1)S(1)} async-done(((bf16[8,16,1024]{2,1,0:T(8,128)(2,1)}), bf16[8,16,1024]{2,1,0:T(8,128)(2,1)S(1)}, u32[]{:S(2)}, u32[]{:S(2)}) %all-to-all-start.1) | async-done | bytes 262176 | tf_op jit(solution)/shard_map/all_to_all | solution.py:24
  71.7 31.3 %all_to_all.20 = bf16[64,16,128]{2,1,0:T(8,128)(2,1)S(1)} all-to-all(bf16[64,16,128]{2,1,0:T(8,128)(2,1)S(1)} %bitcast.26), channel_id=1, replica_groups=mesh['x'=4,'z3'=2,'z2'=2,'z1'=2,'z0'=2,'y'=4,'c'=2] {'y','c','z3','z2','..., dimensions={0} | all-to-all | bytes 524288 | tf_op jit(solution)/shard_map/all_to_all | solution.py:24
  103.0 1.9 %broadcast_in_dim.24 = bf16[8,8,128,128]{3,2,1,0:T(8,128)(2,1)} broadcast(bf16[8,128,128]{2,1,0:T(8,128)(2,1)S(1)} %bitcast.25), dimensions={1,2,3} | broadcast | bytes 2359296 | tf_op jit(solution)/shard_map/broadcast_in_dim | solution.py:177
  104.9 0.0 copy-done.5
  104.9 0.0 copy-done.7
  104.9 7.3 %all-to-all-start.3 = ((bf16[8,8,128,128]{3,2,1,0:T(8,128)(2,1)}), bf16[8,8,128,128]{3,2,1,0:T(8,128)(2,1)S(1)}, u32[]{:S(2)}, u32[]{:S(2)}) async-start(bf16[8,8,128,128]{3,2,1,0:T(8,128)(2,1)} %broadcast_in_dim.24), calls=%async_computation.3 | async-start | bytes 4194304 | tf_op jit(solution)/shard_map/all_to_all | solution.py:24
  112.1 3.0 %collective-permute-start.4 = (bf16[512,1024]{1,0:T(8,128)(2,1)}, bf16[512,1024]{1,0:T(8,128)(2,1)}, u32[]{:S(2)}, u32[]{:S(2)}) collective-permute-start(bf16[512,1024]{1,0:T(8,128)(2,1)} %collective-permute-done.1.refs_2_), channel_id=1, source_target_pairs={{0,1},{1,0},{2,3},{3,2},{4,5},{5,4},{6,7},{7,6},{8,9},{9,8},{10,11... | collective-permute-start | bytes 3145736 | tf_op jit(solution)/shard_map/ppermute | solution.py:146
  115.1 1.9 %collective-permute-start.5 = (bf16[512,1024]{1,0:T(8,128)(2,1)}, bf16[512,1024]{1,0:T(8,128)(2,1)}, u32[]{:S(2)}, u32[]{:S(2)}) collective-permute-start(bf16[512,1024]{1,0:T(8,128)(2,1)} %copy-done.5), channel_id=1, source_target_pairs={{0,1},{1,0},{2,3},{3,2},{4,5},{5,4},{6,7},{7,6},{8,9},{9,8},{10,11... | collective-permute-start | bytes 3145736 | tf_op jit(solution)/shard_map/ppermute | solution.py:146
  117.0 2.4 %collective-permute-start.6 = (bf16[512,1024]{1,0:T(8,128)(2,1)}, bf16[512,1024]{1,0:T(8,128)(2,1)}, u32[]{:S(2)}, u32[]{:S(2)}) collective-permute-start(bf16[512,1024]{1,0:T(8,128)(2,1)} %copy-done.7), channel_id=1, source_target_pairs={{0,1},{1,0},{2,3},{3,2},{4,5},{5,4},{6,7},{7,6},{8,9},{9,8},{10,11... | collective-permute-start | bytes 3145736 | tf_op jit(solution)/shard_map/ppermute | solution.py:146
  119.5 0.0 collective-permute-done.4.refs_3_
  119.5 0.5 collective-permute-done.5.refs_5_
  120.0 2.1 %collective-permute-done.6.refs_7_ = bf16[512,1024]{1,0:T(8,128)(2,1)} collective-permute-done((bf16[512,1024]{1,0:T(8,128)(2,1)}, bf16[512,1024]{1,0:T(8,128)(2,1)}, u32[]{:S(2)}, u32[]{:S(2)}) %collective-permute-start.6) | collective-permute-done | bytes 1048608 | tf_op jit(solution)/shard_map/ppermute | solution.py:146
  122.1 0.0 copy-start.4
  122.1 1.2 copy-done.4
  123.3 0.0 copy-start.6
  123.3 1.2 copy-done.6
  124.5 0.0 copy-start.8
  124.5 1.2 copy-done.8
  125.7 5.0 %shard_map.74 = (f32[512,128]{1,0:T(8,128)S(1)}, bf16[8,512,1024]{2,1,0:T(8,128)(2,1)S(1)}) custom-call(bf16[512,1024]{1,0:T(8,128)(2,1)S(1)} %bitcast.23, bf16[512,1024]{1,0:T(8,128)(2,1)S(1)} %copy-done.4, bf16[512,1024]{1,0:T(8,128)(2,1)} %collective-permute-done.1.refs_2_, bf16[512,1024]{1,0:T(8,128)(2,1)} %collective-permute-done.4.refs_3_, ...), custom_call_target="tpu_custom_call" | custom-call | flops 8388608 | bytes 16777216 | tf_op jit(solution)/shard_map/pallas_call | solution.py:102
  130.7 0.0 copy-start
  130.7 3.2 %copy-done = bf16[8,512,1024]{2,1,0:T(8,128)(2,1)} copy-done((bf16[8,512,1024]{2,1,0:T(8,128)(2,1)}, bf16[8,512,1024]{2,1,0:T(8,128)(2,1)S(1)}, u32[]{:S(2)}) %copy-start) | copy-done | bytes 8388632
  133.9 4.1 %all-to-all-done.3.w_ref = bf16[8,8,128,128]{3,2,1,0:T(8,128)(2,1)S(1)} async-done(((bf16[8,8,128,128]{3,2,1,0:T(8,128)(2,1)}), bf16[8,8,128,128]{3,2,1,0:T(8,128)(2,1)S(1)}, u32[]{:S(2)}, u32[]{:S(2)}) %all-to-all-start.3) | async-done | bytes 2097184 | tf_op jit(solution)/shard_map/all_to_all | solution.py:24
  138.0 0.0 copy-start.1
  138.0 3.4 %copy-done.1 = bf16[8,512,1024]{2,1,0:T(8,128)(2,1)S(1)} copy-done((bf16[8,512,1024]{2,1,0:T(8,128)(2,1)S(1)}, bf16[8,512,1024]{2,1,0:T(8,128)(2,1)}, u32[]{:S(2)}) %copy-start.1) | copy-done | bytes 8388632
  141.4 3.0 %shard_map.75 = bf16[512,128]{1,0:T(8,128)(2,1)} custom-call(s32[1]{0:T(128)} %bitcast.own_ref, f32[512,128]{1,0:T(8,128)S(1)} %get-tuple-element.26.scale_ref, bf16[8,8,128,128]{3,2,1,0:T(8,128)(2,1)S(1)} %all-to-all-done.3.w_ref, bf16[8,512,1024]{2,1,0:T(8,128)(2,1)S(1)} %copy-done.1), custom_call_target="tpu_custom_call" | custom-call | flops 1073741824 | bytes 10485760 | tf_op jit(solution)/shard_map/pallas_call | solution.py:131
  (4 shorter events, 0.1 us)
Async XLA Ops:
  4.8 6.3 %copy-start.2 = (bf16[1,512,1024]{2,1,0:T(8,128)(2,1)S(1)}, bf16[1,512,1024]{2,1,0:T(8,128)(2,1)}, u32[]{:S(2)}) copy-start(bf16[1,512,1024]{2,1,0:T(8,128)(2,1)} %param.12) | copy-start | bytes 3145732
  4.8 28.6 %all-to-all-start = ((bf16[8,128,1024]{2,1,0:T(8,128)(2,1)}), bf16[8,128,1024]{2,1,0:T(8,128)(2,1)}, u32[]{:S(2)}, u32[]{:S(2)}) async-start(bf16[8,128,1024]{2,1,0:T(8,128)(2,1)} %bitcast.24), calls=%async_computation | async-start | bytes 4194304 | tf_op jit(solution)/shard_map/all_to_all | solution.py:24
  11.2 15.3 %collective-permute-start = (bf16[512,1024]{1,0:T(8,128)(2,1)S(1)}, bf16[512,1024]{1,0:T(8,128)(2,1)S(1)}, u32[]{:S(2)}, u32[]{:S(2)}) collective-permute-start(bf16[512,1024]{1,0:T(8,128)(2,1)S(1)} %bitcast.19), channel_id=1, source_target_pairs={{0,1},{1,0},{2,3},{3,2},{4,5},{5,4},{6,7},{7,6},{8,9},{9,8},{10,11... | collective-permute-start | bytes 3145736 | tf_op jit(solution)/shard_map/ppermute | solution.py:146
  18.1 35.9 %collective-permute-start.3 = (bf16[512,1024]{1,0:T(8,128)(2,1)S(1)}, bf16[512,1024]{1,0:T(8,128)(2,1)S(1)}, u32[]{:S(2)}, u32[]{:S(2)}) collective-permute-start(bf16[512,1024]{1,0:T(8,128)(2,1)S(1)} %bitcast.20), channel_id=1, source_target_pairs={{0,4},{1,5},{2,6},{3,7},{4,0},{5,1},{6,2},{7,3},{8,12},{9,13},{10,... | collective-permute-start | bytes 3145736 | tf_op jit(solution)/shard_map/ppermute | solution.py:146
  20.0 49.1 %collective-permute-start.2 = (bf16[512,1024]{1,0:T(8,128)(2,1)S(1)}, bf16[512,1024]{1,0:T(8,128)(2,1)S(1)}, u32[]{:S(2)}, u32[]{:S(2)}) collective-permute-start(bf16[512,1024]{1,0:T(8,128)(2,1)S(1)} %bitcast.21), channel_id=1, source_target_pairs={{0,6},{1,7},{2,4},{3,5},{4,2},{5,3},{6,0},{7,1},{8,14},{9,15},{10,... | collective-permute-start | bytes 3145736 | tf_op jit(solution)/shard_map/ppermute | solution.py:146
  22.0 47.2 %collective-permute-start.1 = (bf16[512,1024]{1,0:T(8,128)(2,1)S(1)}, bf16[512,1024]{1,0:T(8,128)(2,1)}, u32[]{:S(2)}, u32[]{:S(2)}) collective-permute-start(bf16[512,1024]{1,0:T(8,128)(2,1)S(1)} %bitcast.22), channel_id=1, source_target_pairs={{0,2},{1,3},{2,0},{3,1},{4,6},{5,7},{6,4},{7,5},{8,10},{9,11},{10,... | collective-permute-start | bytes 3145736 | tf_op jit(solution)/shard_map/ppermute | solution.py:146
  26.5 1.0 copy-start.3
  36.2 35.4 %all-to-all-start.1 = ((bf16[8,16,1024]{2,1,0:T(8,128)(2,1)}), bf16[8,16,1024]{2,1,0:T(8,128)(2,1)S(1)}, u32[]{:S(2)}, u32[]{:S(2)}) async-start(bf16[8,16,1024]{2,1,0:T(8,128)(2,1)} %bitcast.11), calls=%async_computation.1 | async-start | bytes 524288 | tf_op jit(solution)/shard_map/all_to_all | solution.py:24
  54.0 50.8 %copy-start.5 = (bf16[512,1024]{1,0:T(8,128)(2,1)}, bf16[512,1024]{1,0:T(8,128)(2,1)S(1)}, u32[]{:S(2)}) copy-start(bf16[512,1024]{1,0:T(8,128)(2,1)S(1)} %collective-permute-done.3.refs_4_) | copy-start | bytes 3145732
  69.1 35.7 %copy-start.7 = (bf16[512,1024]{1,0:T(8,128)(2,1)}, bf16[512,1024]{1,0:T(8,128)(2,1)S(1)}, u32[]{:S(2)}) copy-start(bf16[512,1024]{1,0:T(8,128)(2,1)S(1)} %collective-permute-done.2.refs_6_) | copy-start | bytes 3145732
  104.9 33.2 %all-to-all-start.3 = ((bf16[8,8,128,128]{3,2,1,0:T(8,128)(2,1)}), bf16[8,8,128,128]{3,2,1,0:T(8,128)(2,1)S(1)}, u32[]{:S(2)}, u32[]{:S(2)}) async-start(bf16[8,8,128,128]{3,2,1,0:T(8,128)(2,1)} %broadcast_in_dim.24), calls=%async_computation.3 | async-start | bytes 4194304 | tf_op jit(solution)/shard_map/all_to_all | solution.py:24
  112.1 7.4 %collective-permute-start.4 = (bf16[512,1024]{1,0:T(8,128)(2,1)}, bf16[512,1024]{1,0:T(8,128)(2,1)}, u32[]{:S(2)}, u32[]{:S(2)}) collective-permute-start(bf16[512,1024]{1,0:T(8,128)(2,1)} %collective-permute-done.1.refs_2_), channel_id=1, source_target_pairs={{0,1},{1,0},{2,3},{3,2},{4,5},{5,4},{6,7},{7,6},{8,9},{9,8},{10,11... | collective-permute-start | bytes 3145736 | tf_op jit(solution)/shard_map/ppermute | solution.py:146
  115.1 4.9 %collective-permute-start.5 = (bf16[512,1024]{1,0:T(8,128)(2,1)}, bf16[512,1024]{1,0:T(8,128)(2,1)}, u32[]{:S(2)}, u32[]{:S(2)}) collective-permute-start(bf16[512,1024]{1,0:T(8,128)(2,1)} %copy-done.5), channel_id=1, source_target_pairs={{0,1},{1,0},{2,3},{3,2},{4,5},{5,4},{6,7},{7,6},{8,9},{9,8},{10,11... | collective-permute-start | bytes 3145736 | tf_op jit(solution)/shard_map/ppermute | solution.py:146
  117.0 5.0 %collective-permute-start.6 = (bf16[512,1024]{1,0:T(8,128)(2,1)}, bf16[512,1024]{1,0:T(8,128)(2,1)}, u32[]{:S(2)}, u32[]{:S(2)}) collective-permute-start(bf16[512,1024]{1,0:T(8,128)(2,1)} %copy-done.7), channel_id=1, source_target_pairs={{0,1},{1,0},{2,3},{3,2},{4,5},{5,4},{6,7},{7,6},{8,9},{9,8},{10,11... | collective-permute-start | bytes 3145736 | tf_op jit(solution)/shard_map/ppermute | solution.py:146
  122.1 1.2 copy-start.4
  123.3 1.2 copy-start.6
  124.5 1.2 copy-start.8
  130.7 3.2 %copy-start = (bf16[8,512,1024]{2,1,0:T(8,128)(2,1)}, bf16[8,512,1024]{2,1,0:T(8,128)(2,1)S(1)}, u32[]{:S(2)}) copy-start(bf16[8,512,1024]{2,1,0:T(8,128)(2,1)S(1)} %get-tuple-element.28.x_ref) | copy-start | bytes 25165828
  138.0 3.4 %copy-start.1 = (bf16[8,512,1024]{2,1,0:T(8,128)(2,1)S(1)}, bf16[8,512,1024]{2,1,0:T(8,128)(2,1)}, u32[]{:S(2)}) copy-start(bf16[8,512,1024]{2,1,0:T(8,128)(2,1)} %copy-done) | copy-start | bytes 25165828

commit v4 on v3

--- a/solution.py
+++ b/solution.py
@@ -73,73 +73,66 @@
     )(place, x, g, weight, theta, momentum, gain)
 
 
-def scale_kernel(*refs):
-    x_refs, out_ref, x_all, sems = refs[:8], *refs[8:]
-    copies = [
-        pltpu.make_async_copy(x_ref, x_all.at[block], sems.at[block])
-        for block, x_ref in enumerate(x_refs)
-    ]
-    for copy in copies:
-        copy.start()
-    for copy in copies:
-        copy.wait()
-
-    @pl.loop(0, out_ref.shape[0] // 64)
-    def _(i):
-        rows = pl.ds(pl.multiple_of(i * 64, 64), 64)
-        squares = jnp.zeros((64, R), F32)
-        for block in range(8):
-            for j in range(x_all.shape[2] // R):
-                part = x_all[block, rows, j * R : (j + 1) * R].astype(F32)
-                squares += part * part
-        mean = jnp.sum(squares, axis=1, keepdims=True) / D
-        out_ref[rows, :] = jnp.broadcast_to(lax.rsqrt(mean + 1e-05), (64, R))
+def project_kernel(place_ref, w_ref, *refs):
+    x_refs, (keep_ref, squares_ref, send_ref) = refs[:4], refs[4:]
+    tokens = keep_ref.shape[0]
+    acc = jnp.zeros((tokens, 2 * R), F32)
+    for block, x_ref in enumerate(x_refs):
+        weight = w_ref[:, pl.ds(place_ref[2] ^ block, 1)].reshape(-1, 2 * R)
+        acc += jnp.dot(x_ref[...], weight, preferred_element_type=F32)
+    squares = jnp.zeros((tokens, R), F32)
+    for x_ref in x_refs:
+        for j in range(x_ref.shape[1] // R):
+            part = x_ref[:, j * R : (j + 1) * R].astype(F32)
+            squares += part * part
+    squares = jnp.broadcast_to(jnp.sum(squares, axis=1, keepdims=True), (tokens, R))
+    first = place_ref[3] == 0
+    keep_ref[...] = jnp.where(first, acc[:, :R], acc[:, R:])
+    squares_ref[...] = squares
+    high = squares.astype(BF16)
+    low = (squares - high.astype(F32)).astype(BF16)
+    lane = lax.broadcasted_iota(jnp.int32, (tokens, R), 1)
+    send_ref[:, :R] = jnp.where(first, acc[:, R:], acc[:, :R]).astype(BF16)
+    send_ref[:, R:] = jnp.where(lane < R // 2, high.astype(F32), low.astype(F32)).astype(BF16)
 
 
-def scales(blocks):
+def project(place, weight, blocks):
     tokens, features = blocks[0].shape
     vmem = pl.BlockSpec(memory_space=pltpu.VMEM)
     return pl.pallas_call(
-        scale_kernel,
-        in_specs=[pl.BlockSpec(memory_space=pl.ANY)] * 8,
-        out_specs=(vmem, vmem),
+        project_kernel,
+        in_specs=[pl.BlockSpec(memory_space=pltpu.SMEM)] + [vmem] * 5,
+        out_specs=(vmem,) * 3,
         out_shape=(
             jax.ShapeDtypeStruct((tokens, R), F32),
-            jax.ShapeDtypeStruct((8, tokens, features), BF16),
+            jax.ShapeDtypeStruct((tokens, R), F32),
+            jax.ShapeDtypeStruct((tokens, 2 * R), BF16),
         ),
-        scratch_shapes=[pltpu.SemaphoreType.DMA((8,))],
-        compiler_params=pltpu.CompilerParams(vmem_limit_bytes=VMEM),
-        cost_estimate=pl.CostEstimate(
-            flops=16 * tokens * features,
-            bytes_accessed=32 * tokens * features,
-            transcendentals=tokens,
-        ),
-    )(*blocks)
-
-
-def project_kernel(own_ref, scale_ref, w_ref, x_ref, out_ref):
-    acc = jnp.zeros(out_ref.shape, F32)
-    for block in range(8):
-        weight = w_ref[:, pl.ds(own_ref[0] ^ block, 1)].reshape(-1, R)
-        acc += jnp.dot(x_ref[block], weight, preferred_element_type=F32)
-    out_ref[...] = (acc * scale_ref[...]).astype(BF16)
-
-
-def project(own, scale, weight, x_all):
-    tokens, features = x_all.shape[1:]
-    vmem = pl.BlockSpec(memory_space=pltpu.VMEM)
-    return pl.pallas_call(
-        project_kernel,
-        in_specs=[pl.BlockSpec(memory_space=pltpu.SMEM)] + [vmem] * 3,
-        out_specs=vmem,
-        out_shape=jax.ShapeDtypeStruct((tokens, R), BF16),
         compiler_params=pltpu.CompilerParams(vmem_limit_bytes=VMEM),
         cost_estimate=pl.CostEstimate(
             flops=16 * tokens * features * R,
-            bytes_accessed=16 * (tokens * features + features * R),
+            bytes_accessed=8 * (tokens * features + 2 * features * R),
             transcendentals=0,
         ),
-    )(own, scale, weight, x_all)
+    )(place, weight, *blocks)
+
+
+def finish_kernel(keep_ref, squares_ref, got_ref, out_ref):
+    other = got_ref[:, R:].astype(F32)
+    other = other[:, :1] + other[:, R // 2 : R // 2 + 1]
+    scale = lax.rsqrt((squares_ref[...] + other) / D + 1e-05)
+    out_ref[...] = ((keep_ref[...] + got_ref[:, :R].astype(F32)) * scale).astype(BF16)
+
+
+def finish(keep, squares, got):
+    vmem = pl.BlockSpec(memory_space=pltpu.VMEM)
+    return pl.pallas_call(
+        finish_kernel,
+        in_specs=[vmem] * 3,
+        out_specs=vmem,
+        out_shape=jax.ShapeDtypeStruct(keep.shape, BF16),
+        compiler_params=pltpu.CompilerParams(vmem_limit_bytes=VMEM),
+    )(keep, squares, got)
 
 
 def swap(block, bits):
@@ -148,7 +141,8 @@
 
 def per_device(x_saved, grad_keys, inner_weight, outer_weight, outer_momentum, x_next, norm_gain):
     rows, width = outer_weight.shape[0], outer_weight.shape[3]
-    place = jnp.stack([lax.axis_index(ISLAND), lax.axis_index(FSDP)]).astype(jnp.int32)
+    place = jnp.stack([lax.axis_index(axis) for axis in (ISLAND, FSDP, "y", "c")])
+    place = place.astype(jnp.int32)
     term = share(
         place,
         x_saved[0],
@@ -160,23 +154,18 @@
     )
     keys = term.shape[1]
     x_own = x_next[0]
-    x_core, x_up, x_down, x_far = (swap(x_own, bits) for bits in (1, 2, 6, 4))
+    x_up, x_down, x_far = (swap(x_own, bits) for bits in (2, 6, 4))
     sums = exchange(term.reshape(8, -1, keys), NEAR)
-    sums, x_core = lax.optimization_barrier((sums, x_core))
     fresh = exchange(total(sums).astype(BF16).reshape(8, -1, keys), FAR)
     fresh, x_up, x_down, x_far = lax.optimization_barrier((fresh, x_up, x_down, x_far))
     fresh = total(fresh).astype(BF16)
     depth = fresh.shape[0]
-    pieces = fresh.reshape(depth, 8, R).transpose(1, 0, 2)
-    pieces = jnp.broadcast_to(pieces[:, None], (8, 8, depth, R)).reshape(64, depth, R)
-    mine = exchange(pieces, TENSOR + FAR).reshape(8, 8 * depth, R)
-    mine, x_up, x_down, x_far = lax.optimization_barrier((mine, x_up, x_down, x_far))
-    x_up_core, x_down_core, x_far_core = swap(x_up, 1), swap(x_down, 1), swap(x_far, 1)
-    blocks = (x_own, x_core, x_up, x_up_core, x_far, x_far_core, x_down, x_down_core)
-    scale, x_all = scales(blocks)
+    pieces = fresh.reshape(depth, 4, 2 * R).transpose(1, 0, 2)
+    pieces = jnp.broadcast_to(pieces[:, None], (4, 8, depth, 2 * R)).reshape(32, depth, 2 * R)
+    mine = exchange(pieces, ("y",) + FAR).reshape(4, 8 * depth, 2 * R)
     weight = exchange(jnp.broadcast_to(mine[None], (8, *mine.shape)), NEAR)
-    own = lax.axis_index(TENSOR).astype(jnp.int32)[None]
-    return project(own, scale, weight, x_all)[None]
+    keep, squares, send = project(place, weight, (x_own, x_up, x_far, x_down))
+    return finish(keep, squares, swap(send, 1))[None]
 
 
 def solution(mesh):

time: 145 us -> 141 us (0.972)
  blocking collectives: 31.3 us -> 59.3 us
  starting transfers between devices: 54.1 us -> 37.6 us
  local copies, waits for them, and re-layouts: 13.2 us -> 0.28 us
  Pallas kernels: 12.2 us -> 8.29 us
    all_to_all x1 -> x2, blocking collectives: 31.3 us -> 59.3 us  [exchange(): return lax.all_to_all(blocks, axes, 0, 0)]
    unnamed x19 -> x4, local copies, waits for them, and re-layouts: 11.3 us -> 0.01 us
    all_to_all x3 -> x2, waiting for transfers between devices: 12.4 us -> 22.2 us  [exchange(): return lax.all_to_all(blocks, axes, 0, 0)]
    ppermute x7 -> x4, starting transfers between devices: 22.6 us -> 13.4 us  [swap(): return lax.ppermute(block, TENSOR, [(t, t ^ bits) for t in range(8)])]
    ppermute x7 -> x4, waiting for transfers between devices: 17.7 us -> 9.28 us  [swap(): return lax.ppermute(block, TENSOR, [(t, t ^ bits) for t in range(8)])]
    all_to_all x3 -> x2, starting transfers between devices: 31.5 us -> 24.2 us  [exchange(): return lax.all_to_all(blocks, axes, 0, 0)]
    pallas_call x1, Pallas kernels: 4.95 us -> 0.87 us  [finish(): pl.pallas_call(finish_kernel, in_specs=[vmem] * 3, out_specs=vmem, out_sh...]
    broadcast_in_dim x1, local copies, waits for them, and re-layouts: 1.89 us -> 0.23 us  [per_device(): weight = exchange(jnp.broadcast_to(mine[None], (8, *mine.shape)), NEAR)]
  transfers between devices with their start and end apart: 10 -> 6, of which waited for: 6 -> 4; matrix products, arithmetic and copies ran while one was open for 2% -> 2% of each run, Pallas kernels for 3% -> 0%
where the time goes in v4:
time: 141 us; the launch traced here: 140 us
  blocking collectives  59.3 us (42%)
  starting transfers between devices  37.6 us (27%)
  waiting for transfers between devices  31.5 us (22%)
  Pallas kernels  8.29 us (6%)
  other arithmetic  3.36 us (2%)
    all_to_all x2, blocking collectives, exchange(): return lax.all_to_all(blocks, axes, 0, 0)  59.3 us
    all_to_all x2, starting transfers between devices, exchange(): return lax.all_to_all(blocks, axes, 0, 0)  24.2 us
    all_to_all x2, waiting for transfers between devices, exchange(): return lax.all_to_all(blocks, axes, 0, 0)  22.2 us
    ppermute x4, starting transfers between devices, swap(): return lax.ppermute(block, TENSOR, [(t, t ^ bits) for t in range(8)])  13.4 us
    ppermute x4, waiting for transfers between devices, swap(): return lax.ppermute(block, TENSOR, [(t, t ^ bits) for t in range(8)])  9.28 us
    pallas_call x1, Pallas kernels, share(): pl.pallas_call(share_kernel, grid=(features // width,), in_specs=[pl.Bloc...  4.25 us
    pallas_call x1, Pallas kernels, project(): pl.pallas_call(project_kernel, in_specs=[pl.BlockSpec(memory_space=pltpu....  3.17 us
  transfers between devices with their start and end apart: 6, of which 4 were waited for; matrix products, arithmetic and copies ran while one was open for 2% of the time, Pallas kernels for 0%

profile of v4, /device:TPU:1, one launch (start us, length us, event | category | flops | bytes accessed | tf_op | source)
XLA Modules:
  0.0 140.4 jit_solution(15009817199850182269)
XLA Ops:
  0.0 0.6 pad_add_fusion.place_ref
  0.6 4.2 %shard_map.73 = bf16[1024,1024]{1,0:T(8,128)(2,1)} custom-call(s32[4]{0:T(128)} %pad_add_fusion.place_ref, bf16[512,1024]{1,0:T(8,128)(2,1)} %bitcast.24, bf16[512,1024]{1,0:T(8,128)(2,1)} %bitcast.25, bf16[128,1024]{1,0:T(8,128)(2,1)} %bitcast.26, f32[128,128]{1,0:T(8,128)} %bitcast.28, f32[128,128]{1,0:T(8,128)} %bitcast.29, f32[1,1024]{1,0:T(1,128)} %bitcast.30), custom_call_target="tpu_custom_call" | custom-call | flops 1073741824 | bytes 6291456 | tf_op jit(solution)/shard_map/pallas_call | solution.py:55
  4.8 0.0 copy-start
  4.8 6.3 %all-to-all-start = ((bf16[8,128,1024]{2,1,0:T(8,128)(2,1)}), bf16[8,128,1024]{2,1,0:T(8,128)(2,1)}, u32[]{:S(2)}, u32[]{:S(2)}) async-start(bf16[8,128,1024]{2,1,0:T(8,128)(2,1)} %bitcast.21), calls=%async_computation | async-start | bytes 4194304 | tf_op jit(solution)/shard_map/all_to_all | solution.py:24
  11.2 0.0 copy-done
  11.2 4.8 %collective-permute-start.2 = (bf16[512,1024]{1,0:T(8,128)(2,1)S(1)}, bf16[512,1024]{1,0:T(8,128)(2,1)S(1)}, u32[]{:S(2)}, u32[]{:S(2)}) collective-permute-start(bf16[512,1024]{1,0:T(8,128)(2,1)S(1)} %bitcast.17), channel_id=1, source_target_pairs={{0,4},{1,5},{2,6},{3,7},{4,0},{5,1},{6,2},{7,3},{8,12},{9,13},{10,... | collective-permute-start | bytes 3145736 | tf_op jit(solution)/shard_map/ppermute | solution.py:139
  16.0 2.7 %collective-permute-start.1 = (bf16[512,1024]{1,0:T(8,128)(2,1)S(1)}, bf16[512,1024]{1,0:T(8,128)(2,1)S(1)}, u32[]{:S(2)}, u32[]{:S(2)}) collective-permute-start(bf16[512,1024]{1,0:T(8,128)(2,1)S(1)} %bitcast.18), channel_id=1, source_target_pairs={{0,6},{1,7},{2,4},{3,5},{4,2},{5,3},{6,0},{7,1},{8,14},{9,15},{10,... | collective-permute-start | bytes 3145736 | tf_op jit(solution)/shard_map/ppermute | solution.py:139
  18.7 1.9 %collective-permute-start = (bf16[512,1024]{1,0:T(8,128)(2,1)S(1)}, bf16[512,1024]{1,0:T(8,128)(2,1)}, u32[]{:S(2)}, u32[]{:S(2)}) collective-permute-start(bf16[512,1024]{1,0:T(8,128)(2,1)S(1)} %bitcast.19), channel_id=1, source_target_pairs={{0,2},{1,3},{2,0},{3,1},{4,6},{5,7},{6,4},{7,5},{8,10},{9,11},{10,... | collective-permute-start | bytes 3145736 | tf_op jit(solution)/shard_map/ppermute | solution.py:139
  20.6 12.8 %all-to-all-done = bf16[8,128,1024]{2,1,0:T(8,128)(2,1)} async-done(((bf16[8,128,1024]{2,1,0:T(8,128)(2,1)}), bf16[8,128,1024]{2,1,0:T(8,128)(2,1)}, u32[]{:S(2)}, u32[]{:S(2)}) %all-to-all-start) | async-done | bytes 2097184 | tf_op jit(solution)/shard_map/all_to_all | solution.py:24
  33.4 2.7 %reduce_sum.24 = bf16[128,1024]{1,0:T(8,128)(2,1)} reduce(bf16[8,128,1024]{2,1,0:T(8,128)(2,1)} %all-to-all-done, bf16[]{:T(256)} %constant.34.clone.1), dimensions={0}, to_apply=%region_0.0 | reduce | flops 917504 | bytes 2359298 | tf_op jit(solution)/shard_map/reduce_sum | solution.py:28
  36.1 17.9 %all-to-all-start.1 = ((bf16[8,16,1024]{2,1,0:T(8,128)(2,1)}), bf16[8,16,1024]{2,1,0:T(8,128)(2,1)S(1)}, u32[]{:S(2)}, u32[]{:S(2)}) async-start(bf16[8,16,1024]{2,1,0:T(8,128)(2,1)} %bitcast.11), calls=%async_computation.1 | async-start | bytes 524288 | tf_op jit(solution)/shard_map/all_to_all | solution.py:24
  54.0 0.0 collective-permute-done.2.refs_2_
  54.0 8.1 %collective-permute-done.1.refs_3_ = bf16[512,1024]{1,0:T(8,128)(2,1)S(1)} collective-permute-done((bf16[512,1024]{1,0:T(8,128)(2,1)S(1)}, bf16[512,1024]{1,0:T(8,128)(2,1)S(1)}, u32[]{:S(2)}, u32[]{:S(2)}) %collective-permute-start.1) | collective-permute-done | bytes 1048608 | tf_op jit(solution)/shard_map/ppermute | solution.py:139
  62.1 0.0 collective-permute-done.refs_1_
  62.1 9.4 %all-to-all-done.1 = bf16[8,16,1024]{2,1,0:T(8,128)(2,1)S(1)} async-done(((bf16[8,16,1024]{2,1,0:T(8,128)(2,1)}), bf16[8,16,1024]{2,1,0:T(8,128)(2,1)S(1)}, u32[]{:S(2)}, u32[]{:S(2)}) %all-to-all-start.1) | async-done | bytes 262176 | tf_op jit(solution)/shard_map/all_to_all | solution.py:24
  71.7 27.6 %all_to_all.20 = bf16[32,16,256]{2,1,0:T(8,128)(2,1)S(1)} all-to-all(bf16[32,16,256]{2,1,0:T(8,128)(2,1)S(1)} %bitcast.23), channel_id=1, replica_groups=mesh['x'=4,'z3'=2,'z2'=2,'z1'=2,'z0'=2,'y'=4,'c'=2] {'y','z3','z2','z1'}, dimensions={0} | all-to-all | bytes 524288 | tf_op jit(solution)/shard_map/all_to_all | solution.py:24
  99.3 0.2 broadcast_in_dim.22
  99.5 0.0 copy-start.1
  99.5 31.7 %all_to_all.21.w_ref = bf16[8,4,128,256]{3,2,1,0:T(8,128)(2,1)S(1)} all-to-all(bf16[8,4,128,256]{3,2,1,0:T(8,128)(2,1)S(1)} %broadcast_in_dim.22), channel_id=1, replica_groups=mesh['x'=4,'z3'=2,'z2'=2,'z1'=2,'z0'=2,'y'=4,'c'=2] {'x','z0'}, dimensions={0} | all-to-all | bytes 4194304 | tf_op jit(solution)/shard_map/all_to_all | solution.py:24
  131.2 0.0 copy-done.1
  131.2 3.2 %shard_map.74 = (f32[512,128]{1,0:T(8,128)S(1)}, f32[512,128]{1,0:T(8,128)S(1)}, bf16[512,256]{1,0:T(8,128)(2,1)S(1)}) custom-call(s32[4]{0:T(128)S(1)} %copy-done.1, bf16[8,4,128,256]{3,2,1,0:T(8,128)(2,1)S(1)} %all_to_all.21.w_ref, bf16[512,1024]{1,0:T(8,128)(2,1)S(1)} %bitcast.20, bf16[512,1024]{1,0:T(8,128)(2,1)} %collective-permute-done.refs_1_, ...), custom_call_target="tpu_custom_call" | custom-call | flops 1073741824 | bytes 6291456 | tf_op jit(solution)/shard_map/pallas_call | solution.py:102
  134.4 4.0 %collective-permute-start.3 = (bf16[512,256]{1,0:T(8,128)(2,1)S(1)}, bf16[512,256]{1,0:T(8,128)(2,1)S(1)}, u32[]{:S(2)}, u32[]{:S(2)}) collective-permute-start(bf16[512,256]{1,0:T(8,128)(2,1)S(1)} %get-tuple-element.18), channel_id=1, source_target_pairs={{0,1},{1,0},{2,3},{3,2},{4,5},{5,4},{6,7},{7,6},{8,9},{9,8},{10,11... | collective-permute-start | bytes 786440 | tf_op jit(solution)/shard_map/ppermute | solution.py:139
  138.3 1.1 collective-permute-done.3.got_ref
  139.5 0.9 shard_map.75
  (4 shorter events, 0.1 us)
Async XLA Ops:
  4.8 6.3 %copy-start = (bf16[1,512,1024]{2,1,0:T(8,128)(2,1)S(1)}, bf16[1,512,1024]{2,1,0:T(8,128)(2,1)}, u32[]{:S(2)}) copy-start(bf16[1,512,1024]{2,1,0:T(8,128)(2,1)} %param.12) | copy-start | bytes 3145732
  4.8 28.6 %all-to-all-start = ((bf16[8,128,1024]{2,1,0:T(8,128)(2,1)}), bf16[8,128,1024]{2,1,0:T(8,128)(2,1)}, u32[]{:S(2)}, u32[]{:S(2)}) async-start(bf16[8,128,1024]{2,1,0:T(8,128)(2,1)} %bitcast.21), calls=%async_computation | async-start | bytes 4194304 | tf_op jit(solution)/shard_map/all_to_all | solution.py:24
  11.2 42.8 %collective-permute-start.2 = (bf16[512,1024]{1,0:T(8,128)(2,1)S(1)}, bf16[512,1024]{1,0:T(8,128)(2,1)S(1)}, u32[]{:S(2)}, u32[]{:S(2)}) collective-permute-start(bf16[512,1024]{1,0:T(8,128)(2,1)S(1)} %bitcast.17), channel_id=1, source_target_pairs={{0,4},{1,5},{2,6},{3,7},{4,0},{5,1},{6,2},{7,3},{8,12},{9,13},{10,... | collective-permute-start | bytes 3145736 | tf_op jit(solution)/shard_map/ppermute | solution.py:139
  16.0 46.1 %collective-permute-start.1 = (bf16[512,1024]{1,0:T(8,128)(2,1)S(1)}, bf16[512,1024]{1,0:T(8,128)(2,1)S(1)}, u32[]{:S(2)}, u32[]{:S(2)}) collective-permute-start(bf16[512,1024]{1,0:T(8,128)(2,1)S(1)} %bitcast.18), channel_id=1, source_target_pairs={{0,6},{1,7},{2,4},{3,5},{4,2},{5,3},{6,0},{7,1},{8,14},{9,15},{10,... | collective-permute-start | bytes 3145736 | tf_op jit(solution)/shard_map/ppermute | solution.py:139
  18.7 43.4 %collective-permute-start = (bf16[512,1024]{1,0:T(8,128)(2,1)S(1)}, bf16[512,1024]{1,0:T(8,128)(2,1)}, u32[]{:S(2)}, u32[]{:S(2)}) collective-permute-start(bf16[512,1024]{1,0:T(8,128)(2,1)S(1)} %bitcast.19), channel_id=1, source_target_pairs={{0,2},{1,3},{2,0},{3,1},{4,6},{5,7},{6,4},{7,5},{8,10},{9,11},{10,... | collective-permute-start | bytes 3145736 | tf_op jit(solution)/shard_map/ppermute | solution.py:139
  36.1 35.4 %all-to-all-start.1 = ((bf16[8,16,1024]{2,1,0:T(8,128)(2,1)}), bf16[8,16,1024]{2,1,0:T(8,128)(2,1)S(1)}, u32[]{:S(2)}, u32[]{:S(2)}) async-start(bf16[8,16,1024]{2,1,0:T(8,128)(2,1)} %bitcast.11), calls=%async_computation.1 | async-start | bytes 524288 | tf_op jit(solution)/shard_map/all_to_all | solution.py:24
  99.5 31.7 %copy-start.1 = (s32[4]{0:T(128)S(1)}, s32[4]{0:T(128)}, u32[]{:S(2)}) copy-start(s32[4]{0:T(128)} %pad_add_fusion.place_ref) | copy-start | bytes 52
  134.4 5.1 %collective-permute-start.3 = (bf16[512,256]{1,0:T(8,128)(2,1)S(1)}, bf16[512,256]{1,0:T(8,128)(2,1)S(1)}, u32[]{:S(2)}, u32[]{:S(2)}) collective-permute-start(bf16[512,256]{1,0:T(8,128)(2,1)S(1)} %get-tuple-element.18), channel_id=1, source_target_pairs={{0,1},{1,0},{2,3},{3,2},{4,5},{5,4},{6,7},{7,6},{8,9},{9,8},{10,11... | collective-permute-start | bytes 786440 | tf_op jit(solution)/shard_map/ppermute | solution.py:139

commit v5 on v4

--- a/solution.py
+++ b/solution.py
@@ -28,8 +28,9 @@
     return jnp.sum(blocks.astype(F32), axis=0)
 
 
-def share_kernel(place_ref, x_ref, g_ref, w_ref, theta_ref, momentum_ref, gain_ref, out_ref):
+def share_kernel(x_ref, g_ref, w_ref, theta_ref, momentum_ref, gain_ref, out_ref):
     step = pl.program_id(0)
+    island, fsdp = lax.axis_index(ISLAND), lax.axis_index(FSDP)
     width = x_ref.shape[1]
     term = lax.dot_general(
         x_ref[...], g_ref[...], (((0,), (0,)), ((), ())), preferred_element_type=F32
@@ -37,17 +38,17 @@
     own = (1.0 - STEP) * theta_ref[...] - 0.7 * 0.9 * 0.9 * momentum_ref[...]
     band = []
     for j in range(width // R):
-        here = place_ref[0] == step * (width // R) + j
+        here = island == step * (width // R) + j
         band.append(SHARE * w_ref[:, j * R : (j + 1) * R].astype(F32) + jnp.where(here, own, 0.0))
     band = jnp.concatenate(band, axis=1).T
     gain = jnp.broadcast_to(gain_ref[...], (R, width)).T
     for j in range(out_ref.shape[1] // R):
         piece = (-0.03 * SHARE) * term[:, j * R : (j + 1) * R]
-        piece += jnp.where(place_ref[1] == j, band, 0.0)
+        piece += jnp.where(fsdp == j, band, 0.0)
         out_ref[:, j * R : (j + 1) * R] = (piece * gain).astype(BF16)
 
 
-def share(place, x, g, weight, theta, momentum, gain):
+def share(x, g, weight, theta, momentum, gain):
     tokens, features = x.shape
     keys = g.shape[1]
     width = 4 * R
@@ -56,7 +57,6 @@
         share_kernel,
         grid=(features // width,),
         in_specs=[
-            pl.BlockSpec(memory_space=pltpu.SMEM),
             pl.BlockSpec((tokens, width), lambda i: (0, i)),
             whole(tokens, keys),
             pl.BlockSpec((R, width), lambda i: (0, i)),
@@ -70,23 +70,54 @@
         cost_estimate=pl.CostEstimate(
             flops=2 * tokens * features * keys, bytes_accessed=6 * 2**20, transcendentals=0
         ),
-    )(place, x, g, weight, theta, momentum, gain)
-
-
-def project_kernel(place_ref, w_ref, *refs):
+    )(x, g, weight, theta, momentum, gain)
+
+
+def total_kernel(blocks_ref, out_ref, vmem_ref, sems):
+    parts, size = 4, out_ref.shape[1] // 4
+    copies = []
+    for part in range(parts):
+        rows = pl.ds(part * size, size)
+        copies.append(
+            pltpu.make_async_copy(blocks_ref.at[:, rows], vmem_ref.at[:, rows], sems.at[part])
+        )
+        copies[-1].start()
+    for part in range(parts):
+        copies[part].wait()
+        rows = slice(part * size, (part + 1) * size)
+        block = jnp.sum(vmem_ref[:, rows].astype(F32), axis=0).astype(BF16)
+        for j in range(4):
+            out_ref[j, rows] = block[:, j * 2 * R : (j + 1) * 2 * R]
+
+
+def total_far(blocks):
+    return pl.pallas_call(
+        total_kernel,
+        in_specs=[pl.BlockSpec(memory_space=pl.ANY)],
+        out_specs=pl.BlockSpec(memory_space=pltpu.VMEM),
+        out_shape=jax.ShapeDtypeStruct((4, blocks.shape[1], 2 * R), BF16),
+        scratch_shapes=[pltpu.VMEM(blocks.shape, BF16), pltpu.SemaphoreType.DMA((4,))],
+        compiler_params=pltpu.CompilerParams(vmem_limit_bytes=VMEM),
+        cost_estimate=pl.CostEstimate(
+            flops=blocks.size, bytes_accessed=3 * blocks.size, transcendentals=0
+        ),
+    )(blocks)
+
+
+def project_kernel(w_ref, *refs):
     x_refs, (keep_ref, squares_ref, send_ref) = refs[:4], refs[4:]
+    own, core = lax.axis_index("y"), lax.axis_index("c")
     tokens = keep_ref.shape[0]
     acc = jnp.zeros((tokens, 2 * R), F32)
     for block, x_ref in enumerate(x_refs):
-        weight = w_ref[:, pl.ds(place_ref[2] ^ block, 1)].reshape(-1, 2 * R)
-        acc += jnp.dot(x_ref[...], weight, preferred_element_type=F32)
+        acc += jnp.dot(x_ref[...], w_ref[:, :, pl.ds(own ^ block, 1)].reshape(-1, 2 * R), preferred_element_type=F32)
     squares = jnp.zeros((tokens, R), F32)
     for x_ref in x_refs:
         for j in range(x_ref.shape[1] // R):
             part = x_ref[:, j * R : (j + 1) * R].astype(F32)
             squares += part * part
     squares = jnp.broadcast_to(jnp.sum(squares, axis=1, keepdims=True), (tokens, R))
-    first = place_ref[3] == 0
+    first = core == 0
     keep_ref[...] = jnp.where(first, acc[:, :R], acc[:, R:])
     squares_ref[...] = squares
     high = squares.astype(BF16)
@@ -96,12 +127,12 @@
     send_ref[:, R:] = jnp.where(lane < R // 2, high.astype(F32), low.astype(F32)).astype(BF16)
 
 
-def project(place, weight, blocks):
+def project(weight, blocks):
     tokens, features = blocks[0].shape
     vmem = pl.BlockSpec(memory_space=pltpu.VMEM)
     return pl.pallas_call(
         project_kernel,
-        in_specs=[pl.BlockSpec(memory_space=pltpu.SMEM)] + [vmem] * 5,
+        in_specs=[vmem] * 5,
         out_specs=(vmem,) * 3,
         out_shape=(
             jax.ShapeDtypeStruct((tokens, R), F32),
@@ -114,7 +145,7 @@
             bytes_accessed=8 * (tokens * features + 2 * features * R),
             transcendentals=0,
         ),
-    )(place, weight, *blocks)
+    )(weight, *blocks)
 
 
 def finish_kernel(keep_ref, squares_ref, got_ref, out_ref):
@@ -141,10 +172,7 @@
 
 def per_device(x_saved, grad_keys, inner_weight, outer_weight, outer_momentum, x_next, norm_gain):
     rows, width = outer_weight.shape[0], outer_weight.shape[3]
-    place = jnp.stack([lax.axis_index(axis) for axis in (ISLAND, FSDP, "y", "c")])
-    place = place.astype(jnp.int32)
     term = share(
-        place,
         x_saved[0],
         grad_keys[0],
         inner_weight[0],
@@ -156,15 +184,15 @@
     x_own = x_next[0]
     x_up, x_down, x_far = (swap(x_own, bits) for bits in (2, 6, 4))
     sums = exchange(term.reshape(8, -1, keys), NEAR)
-    fresh = exchange(total(sums).astype(BF16).reshape(8, -1, keys), FAR)
-    fresh, x_up, x_down, x_far = lax.optimization_barrier((fresh, x_up, x_down, x_far))
-    fresh = total(fresh).astype(BF16)
-    depth = fresh.shape[0]
-    pieces = fresh.reshape(depth, 4, 2 * R).transpose(1, 0, 2)
-    pieces = jnp.broadcast_to(pieces[:, None], (4, 8, depth, 2 * R)).reshape(32, depth, 2 * R)
-    mine = exchange(pieces, ("y",) + FAR).reshape(4, 8 * depth, 2 * R)
+    fresh = exchange(total_far(sums).reshape(32, -1, 2 * R), ("y",) + FAR)
+    fresh, x_up, x_down = lax.optimization_barrier((fresh, x_up, x_down))
+    fresh = jnp.sum(fresh.reshape(4, 8, -1, 2 * R).astype(F32), axis=1).astype(BF16)
+    mine = exchange(jnp.broadcast_to(fresh[None], (8, *fresh.shape)), FAR)
+    mine, x_far = lax.optimization_barrier((mine, x_far))
+    mine = mine.reshape(-1, 2 * R)
     weight = exchange(jnp.broadcast_to(mine[None], (8, *mine.shape)), NEAR)
-    keep, squares, send = project(place, weight, (x_own, x_up, x_far, x_down))
+    weight = weight.reshape(8, 8, 4, -1, 2 * R)
+    keep, squares, send = project(weight, (x_own, x_up, x_far, x_down))
     return finish(keep, squares, swap(send, 1))[None]
 
 

time: 141 us -> 137 us (0.972)
  blocking collectives: 59.3 us -> 27.4 us
  starting transfers between devices: 37.6 us -> 52.3 us
  waiting for transfers between devices: 31.5 us -> 46.1 us
  other arithmetic: 3.36 us -> 0.04 us
  Pallas kernels: 8.29 us -> 9.82 us
    all_to_all x2 -> x1, blocking collectives: 59.3 us -> 27.4 us  [exchange(): return lax.all_to_all(blocks, axes, 0, 0)]
    all_to_all x2 -> x3, waiting for transfers between devices: 22.2 us -> 40.6 us  [exchange(): return lax.all_to_all(blocks, axes, 0, 0)]
    all_to_all x2 -> x3, starting transfers between devices: 24.2 us -> 35 us  [exchange(): return lax.all_to_all(blocks, axes, 0, 0)]
    ppermute x4, starting transfers between devices: 13.4 us -> 17.3 us  [swap(): return lax.ppermute(block, TENSOR, [(t, t ^ bits) for t in range(8)])]
    ppermute x4, waiting for transfers between devices: 9.28 us -> 5.44 us  [swap(): return lax.ppermute(block, TENSOR, [(t, t ^ bits) for t in range(8)])]
    reduce_sum x2 -> x1, other arithmetic: 2.77 us -> 0.04 us  [per_device(): jnp.sum(fresh.reshape(4, 8, -1, 2 * R).astype(F32), axis=1).astype(BF16)]
    pallas_call x1 -> x2, Pallas kernels: 3.17 us -> 4.65 us  [the longest x1 3.48 us: project(): pl.pallas_call(project_kernel, in_specs=[vmem] * 5, out_specs=(vmem,) * 3...]
  transfers between devices with their start and end apart: 6 -> 7, of which waited for: 4 -> 5; matrix products, arithmetic and copies ran while one was open for 2% -> 1% of each run, Pallas kernels for 0% -> 1%
where the time goes in v5:
time: 137 us
  starting transfers between devices  52.3 us (38%)
  waiting for transfers between devices  46.1 us (34%)
  blocking collectives  27.4 us (20%)
  Pallas kernels  9.82 us (7%)
    all_to_all x3, waiting for transfers between devices, exchange(): return lax.all_to_all(blocks, axes, 0, 0)  40.6 us
    all_to_all x3, starting transfers between devices, exchange(): return lax.all_to_all(blocks, axes, 0, 0)  35 us
    all_to_all x1, blocking collectives, exchange(): return lax.all_to_all(blocks, axes, 0, 0)  27.4 us
    ppermute x4, starting transfers between devices, swap(): return lax.ppermute(block, TENSOR, [(t, t ^ bits) for t in range(8)])  17.3 us
    ppermute x4, waiting for transfers between devices, swap(): return lax.ppermute(block, TENSOR, [(t, t ^ bits) for t in range(8)])  5.44 us
    pallas_call x1, Pallas kernels, share(): pl.pallas_call(share_kernel, grid=(features // width,), in_specs=[pl.Bloc...  4.29 us
    pallas_call x1, Pallas kernels, project(): pl.pallas_call(project_kernel, in_specs=[vmem] * 5, out_specs=(vmem,) * 3...  3.48 us
  transfers between devices with their start and end apart: 7, of which 5 were waited for; matrix products, arithmetic and copies ran while one was open for 1% of the time, Pallas kernels for 1%

profile of v5, /device:TPU:1, one launch (start us, length us, event | category | flops | bytes accessed | tf_op | source)
XLA Modules:
  0.0 136.6 jit_solution(11500616831470332263)
XLA Ops:
  0.0 4.3 %shard_map.73 = bf16[1024,1024]{1,0:T(8,128)(2,1)} custom-call(bf16[512,1024]{1,0:T(8,128)(2,1)} %bitcast.21, bf16[512,1024]{1,0:T(8,128)(2,1)} %bitcast.22, bf16[128,1024]{1,0:T(8,128)(2,1)} %bitcast.23, f32[128,128]{1,0:T(8,128)} %bitcast.24, f32[128,128]{1,0:T(8,128)} %bitcast.25, f32[1,1024]{1,0:T(1,128)} %bitcast.26), custom_call_target="tpu_custom_call" | custom-call | flops 1073741824 | bytes 6291456 | tf_op jit(solution)/shard_map/pallas_call | solution.py:56
  4.3 0.0 copy-start
  4.3 6.3 %all-to-all-start = ((bf16[8,128,1024]{2,1,0:T(8,128)(2,1)}), bf16[8,128,1024]{2,1,0:T(8,128)(2,1)S(1)}, u32[]{:S(2)}, u32[]{:S(2)}) async-start(bf16[8,128,1024]{2,1,0:T(8,128)(2,1)} %bitcast.19), calls=%async_computation | async-start | bytes 4194304 | tf_op jit(solution)/shard_map/all_to_all | solution.py:24
  10.6 0.0 copy-done
  10.6 4.7 %collective-permute-start.1 = (bf16[512,1024]{1,0:T(8,128)(2,1)S(1)}, bf16[512,1024]{1,0:T(8,128)(2,1)}, u32[]{:S(2)}, u32[]{:S(2)}) collective-permute-start(bf16[512,1024]{1,0:T(8,128)(2,1)S(1)} %bitcast.15), channel_id=1, source_target_pairs={{0,6},{1,7},{2,4},{3,5},{4,2},{5,3},{6,0},{7,1},{8,14},{9,15},{10,... | collective-permute-start | bytes 3145736 | tf_op jit(solution)/shard_map/ppermute | solution.py:170
  15.3 1.9 %collective-permute-start = (bf16[512,1024]{1,0:T(8,128)(2,1)S(1)}, bf16[512,1024]{1,0:T(8,128)(2,1)}, u32[]{:S(2)}, u32[]{:S(2)}) collective-permute-start(bf16[512,1024]{1,0:T(8,128)(2,1)S(1)} %bitcast.16), channel_id=1, source_target_pairs={{0,2},{1,3},{2,0},{3,1},{4,6},{5,7},{6,4},{7,5},{8,10},{9,11},{10,... | collective-permute-start | bytes 3145736 | tf_op jit(solution)/shard_map/ppermute | solution.py:170
  17.2 16.2 %all-to-all-done.blocks_ref = bf16[8,128,1024]{2,1,0:T(8,128)(2,1)S(1)} async-done(((bf16[8,128,1024]{2,1,0:T(8,128)(2,1)}), bf16[8,128,1024]{2,1,0:T(8,128)(2,1)S(1)}, u32[]{:S(2)}, u32[]{:S(2)}) %all-to-all-start) | async-done | bytes 2097184 | tf_op jit(solution)/shard_map/all_to_all | solution.py:24
  33.5 1.2 shard_map.74
  34.6 20.2 %all-to-all-start.1 = ((bf16[32,16,256]{2,1,0:T(8,128)(2,1)}), bf16[32,16,256]{2,1,0:T(8,128)(2,1)S(1)}, u32[]{:S(2)}, u32[]{:S(2)}) async-start(bf16[32,16,256]{2,1,0:T(8,128)(2,1)} %bitcast.7), calls=%async_computation.1 | async-start | bytes 524288 | tf_op jit(solution)/shard_map/all_to_all | solution.py:24
  54.8 4.7 %collective-permute-start.2 = (bf16[512,1024]{1,0:T(8,128)(2,1)S(1)}, bf16[512,1024]{1,0:T(8,128)(2,1)S(1)}, u32[]{:S(2)}, u32[]{:S(2)}) collective-permute-start(bf16[512,1024]{1,0:T(8,128)(2,1)S(1)} %bitcast.17), channel_id=1, source_target_pairs={{0,4},{1,5},{2,6},{3,7},{4,0},{5,1},{6,2},{7,3},{8,12},{9,13},{10,... | collective-permute-start | bytes 3145736 | tf_op jit(solution)/shard_map/ppermute | solution.py:170
  59.5 0.0 collective-permute-done.1.refs_3_
  59.5 0.0 collective-permute-done.refs_1_
  59.5 10.8 %all-to-all-done.1 = bf16[32,16,256]{2,1,0:T(8,128)(2,1)S(1)} async-done(((bf16[32,16,256]{2,1,0:T(8,128)(2,1)}), bf16[32,16,256]{2,1,0:T(8,128)(2,1)S(1)}, u32[]{:S(2)}, u32[]{:S(2)}) %all-to-all-start.1) | async-done | bytes 262176 | tf_op jit(solution)/shard_map/all_to_all | solution.py:24
  70.4 0.7 broadcast_in_dim.20
  71.1 8.5 %all-to-all-start.2 = ((bf16[8,4,16,256]{3,2,1,0:T(8,128)(2,1)}), bf16[8,4,16,256]{3,2,1,0:T(8,128)(2,1)S(1)}, u32[]{:S(2)}, u32[]{:S(2)}) async-start(bf16[8,4,16,256]{3,2,1,0:T(8,128)(2,1)} %broadcast_in_dim.20), calls=%async_computation.2 | async-start | bytes 524288 | tf_op jit(solution)/shard_map/all_to_all | solution.py:24
  79.6 4.3 %collective-permute-done.2.refs_2_ = bf16[512,1024]{1,0:T(8,128)(2,1)S(1)} collective-permute-done((bf16[512,1024]{1,0:T(8,128)(2,1)S(1)}, bf16[512,1024]{1,0:T(8,128)(2,1)S(1)}, u32[]{:S(2)}, u32[]{:S(2)}) %collective-permute-start.2) | collective-permute-done | bytes 1048608 | tf_op jit(solution)/shard_map/ppermute | solution.py:170
  83.9 13.6 %all-to-all-done.2 = bf16[8,4,16,256]{3,2,1,0:T(8,128)(2,1)S(1)} async-done(((bf16[8,4,16,256]{3,2,1,0:T(8,128)(2,1)}), bf16[8,4,16,256]{3,2,1,0:T(8,128)(2,1)S(1)}, u32[]{:S(2)}, u32[]{:S(2)}) %all-to-all-start.2) | async-done | bytes 262176 | tf_op jit(solution)/shard_map/all_to_all | solution.py:24
  97.5 0.1 broadcast_in_dim.22
  97.6 27.4 %all_to_all.20 = bf16[8,512,256]{2,1,0:T(8,128)(2,1)S(1)} all-to-all(bf16[8,512,256]{2,1,0:T(8,128)(2,1)S(1)} %broadcast_in_dim.22), channel_id=1, replica_groups=mesh['x'=4,'z3'=2,'z2'=2,'z1'=2,'z0'=2,'y'=4,'c'=2] {'x','z0'}, dimensions={0} | all-to-all | bytes 4194304 | tf_op jit(solution)/shard_map/all_to_all | solution.py:24
  125.0 3.5 %shard_map.75 = (f32[512,128]{1,0:T(8,128)S(1)}, f32[512,128]{1,0:T(8,128)S(1)}, bf16[512,256]{1,0:T(8,128)(2,1)S(1)}) custom-call(bf16[8,8,4,16,256]{4,3,2,1,0:T(8,128)(2,1)S(1)} %bitcast.14, bf16[512,1024]{1,0:T(8,128)(2,1)S(1)} %bitcast.18, bf16[512,1024]{1,0:T(8,128)(2,1)} %collective-permute-done.refs_1_, ...), custom_call_target="tpu_custom_call" | custom-call | flops 1073741824 | bytes 6291456 | tf_op jit(solution)/shard_map/pallas_call | solution.py:133
  128.5 6.1 %collective-permute-start.3 = (bf16[512,256]{1,0:T(8,128)(2,1)S(1)}, bf16[512,256]{1,0:T(8,128)(2,1)S(1)}, u32[]{:S(2)}, u32[]{:S(2)}) collective-permute-start(bf16[512,256]{1,0:T(8,128)(2,1)S(1)} %get-tuple-element.20), channel_id=1, source_target_pairs={{0,1},{1,0},{2,3},{3,2},{4,5},{5,4},{6,7},{7,6},{8,9},{9,8},{10,11... | collective-permute-start | bytes 786440 | tf_op jit(solution)/shard_map/ppermute | solution.py:170
  134.6 1.1 collective-permute-done.3.got_ref
  135.7 0.9 shard_map.76
  (1 shorter events, 0.0 us)
Async XLA Ops:
  4.3 6.3 %copy-start = (bf16[1,512,1024]{2,1,0:T(8,128)(2,1)S(1)}, bf16[1,512,1024]{2,1,0:T(8,128)(2,1)}, u32[]{:S(2)}) copy-start(bf16[1,512,1024]{2,1,0:T(8,128)(2,1)} %param.12) | copy-start | bytes 3145732
  4.3 29.2 %all-to-all-start = ((bf16[8,128,1024]{2,1,0:T(8,128)(2,1)}), bf16[8,128,1024]{2,1,0:T(8,128)(2,1)S(1)}, u32[]{:S(2)}, u32[]{:S(2)}) async-start(bf16[8,128,1024]{2,1,0:T(8,128)(2,1)} %bitcast.19), calls=%async_computation | async-start | bytes 4194304 | tf_op jit(solution)/shard_map/all_to_all | solution.py:24
  10.6 48.9 %collective-permute-start.1 = (bf16[512,1024]{1,0:T(8,128)(2,1)S(1)}, bf16[512,1024]{1,0:T(8,128)(2,1)}, u32[]{:S(2)}, u32[]{:S(2)}) collective-permute-start(bf16[512,1024]{1,0:T(8,128)(2,1)S(1)} %bitcast.15), channel_id=1, source_target_pairs={{0,6},{1,7},{2,4},{3,5},{4,2},{5,3},{6,0},{7,1},{8,14},{9,15},{10,... | collective-permute-start | bytes 3145736 | tf_op jit(solution)/shard_map/ppermute | solution.py:170
  15.3 44.2 %collective-permute-start = (bf16[512,1024]{1,0:T(8,128)(2,1)S(1)}, bf16[512,1024]{1,0:T(8,128)(2,1)}, u32[]{:S(2)}, u32[]{:S(2)}) collective-permute-start(bf16[512,1024]{1,0:T(8,128)(2,1)S(1)} %bitcast.16), channel_id=1, source_target_pairs={{0,2},{1,3},{2,0},{3,1},{4,6},{5,7},{6,4},{7,5},{8,10},{9,11},{10,... | collective-permute-start | bytes 3145736 | tf_op jit(solution)/shard_map/ppermute | solution.py:170
  34.6 35.7 %all-to-all-start.1 = ((bf16[32,16,256]{2,1,0:T(8,128)(2,1)}), bf16[32,16,256]{2,1,0:T(8,128)(2,1)S(1)}, u32[]{:S(2)}, u32[]{:S(2)}) async-start(bf16[32,16,256]{2,1,0:T(8,128)(2,1)} %bitcast.7), calls=%async_computation.1 | async-start | bytes 524288 | tf_op jit(solution)/shard_map/all_to_all | solution.py:24
  54.8 29.1 %collective-permute-start.2 = (bf16[512,1024]{1,0:T(8,128)(2,1)S(1)}, bf16[512,1024]{1,0:T(8,128)(2,1)S(1)}, u32[]{:S(2)}, u32[]{:S(2)}) collective-permute-start(bf16[512,1024]{1,0:T(8,128)(2,1)S(1)} %bitcast.17), channel_id=1, source_target_pairs={{0,4},{1,5},{2,6},{3,7},{4,0},{5,1},{6,2},{7,3},{8,12},{9,13},{10,... | collective-permute-start | bytes 3145736 | tf_op jit(solution)/shard_map/ppermute | solution.py:170
  71.1 26.4 %all-to-all-start.2 = ((bf16[8,4,16,256]{3,2,1,0:T(8,128)(2,1)}), bf16[8,4,16,256]{3,2,1,0:T(8,128)(2,1)S(1)}, u32[]{:S(2)}, u32[]{:S(2)}) async-start(bf16[8,4,16,256]{3,2,1,0:T(8,128)(2,1)} %broadcast_in_dim.20), calls=%async_computation.2 | async-start | bytes 524288 | tf_op jit(solution)/shard_map/all_to_all | solution.py:24
  128.5 7.3 %collective-permute-start.3 = (bf16[512,256]{1,0:T(8,128)(2,1)S(1)}, bf16[512,256]{1,0:T(8,128)(2,1)S(1)}, u32[]{:S(2)}, u32[]{:S(2)}) collective-permute-start(bf16[512,256]{1,0:T(8,128)(2,1)S(1)} %get-tuple-element.20), channel_id=1, source_target_pairs={{0,1},{1,0},{2,3},{3,2},{4,5},{5,4},{6,7},{7,6},{8,9},{9,8},{10,11... | collective-permute-start | bytes 786440 | tf_op jit(solution)/shard_map/ppermute | solution.py:170

commit v6 on v5

--- a/solution.py
+++ b/solution.py
@@ -74,7 +74,7 @@
 
 
 def total_kernel(blocks_ref, out_ref, vmem_ref, sems):
-    parts, size = 4, out_ref.shape[1] // 4
+    parts, size = 4, out_ref.shape[0] * 4
     copies = []
     for part in range(parts):
         rows = pl.ds(part * size, size)
@@ -86,8 +86,10 @@
         copies[part].wait()
         rows = slice(part * size, (part + 1) * size)
         block = jnp.sum(vmem_ref[:, rows].astype(F32), axis=0).astype(BF16)
-        for j in range(4):
-            out_ref[j, rows] = block[:, j * 2 * R : (j + 1) * 2 * R]
+        for i in range(size // 16):
+            for j in range(4):
+                piece = block[i * 16 : (i + 1) * 16, j * 2 * R : (j + 1) * 2 * R]
+                out_ref[part * (size // 16) + i, j] = piece
 
 
 def total_far(blocks):
@@ -95,7 +97,7 @@
         total_kernel,
         in_specs=[pl.BlockSpec(memory_space=pl.ANY)],
         out_specs=pl.BlockSpec(memory_space=pltpu.VMEM),
-        out_shape=jax.ShapeDtypeStruct((4, blocks.shape[1], 2 * R), BF16),
+        out_shape=jax.ShapeDtypeStruct((blocks.shape[1] // 16, 4, 16, 2 * R), BF16),
         scratch_shapes=[pltpu.VMEM(blocks.shape, BF16), pltpu.SemaphoreType.DMA((4,))],
         compiler_params=pltpu.CompilerParams(vmem_limit_bytes=VMEM),
         cost_estimate=pl.CostEstimate(
@@ -104,22 +106,45 @@
     )(blocks)
 
 
-def project_kernel(w_ref, *refs):
-    x_refs, (keep_ref, squares_ref, send_ref) = refs[:4], refs[4:]
+def squares_kernel(*refs):
+    x_refs, out_ref = refs[:4], refs[4]
+
+    @pl.loop(0, out_ref.shape[0] // 64)
+    def _(i):
+        rows = pl.ds(pl.multiple_of(i * 64, 64), 64)
+        squares = jnp.zeros((64, R), F32)
+        for x_ref in x_refs:
+            for j in range(x_ref.shape[1] // R):
+                part = x_ref[rows, j * R : (j + 1) * R].astype(F32)
+                squares += part * part
+        out_ref[rows, :] = jnp.broadcast_to(jnp.sum(squares, axis=1, keepdims=True), (64, R))
+
+
+def squares_of(blocks):
+    tokens, features = blocks[0].shape
+    vmem = pl.BlockSpec(memory_space=pltpu.VMEM)
+    return pl.pallas_call(
+        squares_kernel,
+        in_specs=[vmem] * 4,
+        out_specs=vmem,
+        out_shape=jax.ShapeDtypeStruct((tokens, R), F32),
+        compiler_params=pltpu.CompilerParams(vmem_limit_bytes=VMEM),
+        cost_estimate=pl.CostEstimate(
+            flops=8 * tokens * features, bytes_accessed=8 * tokens * features, transcendentals=0
+        ),
+    )(*blocks)
+
+
+def project_kernel(w_ref, squares_ref, *refs):
+    x_refs, (keep_ref, send_ref) = refs[:4], refs[4:]
+    squares = squares_ref[...]
     own, core = lax.axis_index("y"), lax.axis_index("c")
     tokens = keep_ref.shape[0]
     acc = jnp.zeros((tokens, 2 * R), F32)
     for block, x_ref in enumerate(x_refs):
         acc += jnp.dot(x_ref[...], w_ref[:, :, pl.ds(own ^ block, 1)].reshape(-1, 2 * R), preferred_element_type=F32)
-    squares = jnp.zeros((tokens, R), F32)
-    for x_ref in x_refs:
-        for j in range(x_ref.shape[1] // R):
-            part = x_ref[:, j * R : (j + 1) * R].astype(F32)
-            squares += part * part
-    squares = jnp.broadcast_to(jnp.sum(squares, axis=1, keepdims=True), (tokens, R))
     first = core == 0
     keep_ref[...] = jnp.where(first, acc[:, :R], acc[:, R:])
-    squares_ref[...] = squares
     high = squares.astype(BF16)
     low = (squares - high.astype(F32)).astype(BF16)
     lane = lax.broadcasted_iota(jnp.int32, (tokens, R), 1)
@@ -127,15 +152,14 @@
     send_ref[:, R:] = jnp.where(lane < R // 2, high.astype(F32), low.astype(F32)).astype(BF16)
 
 
-def project(weight, blocks):
+def project(weight, squares, blocks):
     tokens, features = blocks[0].shape
     vmem = pl.BlockSpec(memory_space=pltpu.VMEM)
     return pl.pallas_call(
         project_kernel,
-        in_specs=[vmem] * 5,
-        out_specs=(vmem,) * 3,
+        in_specs=[vmem] * 6,
+        out_specs=(vmem,) * 2,
         out_shape=(
-            jax.ShapeDtypeStruct((tokens, R), F32),
             jax.ShapeDtypeStruct((tokens, R), F32),
             jax.ShapeDtypeStruct((tokens, 2 * R), BF16),
         ),
@@ -145,7 +169,7 @@
             bytes_accessed=8 * (tokens * features + 2 * features * R),
             transcendentals=0,
         ),
-    )(weight, *blocks)
+    )(weight, squares, *blocks)
 
 
 def finish_kernel(keep_ref, squares_ref, got_ref, out_ref):
@@ -184,15 +208,17 @@
     x_own = x_next[0]
     x_up, x_down, x_far = (swap(x_own, bits) for bits in (2, 6, 4))
     sums = exchange(term.reshape(8, -1, keys), NEAR)
-    fresh = exchange(total_far(sums).reshape(32, -1, 2 * R), ("y",) + FAR)
+    fresh = exchange(total_far(sums).reshape(32, -1, 2 * R), FAR + ("y",))
     fresh, x_up, x_down = lax.optimization_barrier((fresh, x_up, x_down))
-    fresh = jnp.sum(fresh.reshape(4, 8, -1, 2 * R).astype(F32), axis=1).astype(BF16)
+    fresh = jnp.sum(fresh.reshape(8, 4, -1, 2 * R).astype(F32), axis=0).astype(BF16)
     mine = exchange(jnp.broadcast_to(fresh[None], (8, *fresh.shape)), FAR)
-    mine, x_far = lax.optimization_barrier((mine, x_far))
+    blocks = (x_own, x_up, x_far, x_down)
+    squares = squares_of(blocks)
+    mine, x_far, squares = lax.optimization_barrier((mine, x_far, squares))
     mine = mine.reshape(-1, 2 * R)
     weight = exchange(jnp.broadcast_to(mine[None], (8, *mine.shape)), NEAR)
     weight = weight.reshape(8, 8, 4, -1, 2 * R)
-    keep, squares, send = project(weight, (x_own, x_up, x_far, x_down))
+    keep, send = project(weight, squares, (x_own, x_up, x_far, x_down))
     return finish(keep, squares, swap(send, 1))[None]
 
 

time: 137 us -> 135 us (0.985)
  waiting for transfers between devices: 46.1 us -> 42.7 us
  Pallas kernels: 9.82 us -> 12.2 us
  starting transfers between devices: 52.3 us -> 50.8 us
    all_to_all x3, waiting for transfers between devices: 40.6 us -> 37.1 us  [exchange(): return lax.all_to_all(blocks, axes, 0, 0)]
    all_to_all x3, starting transfers between devices: 35 us -> 31.6 us  [exchange(): return lax.all_to_all(blocks, axes, 0, 0)]
    pallas_call x1 -> x2, Pallas kernels: 3.48 us -> 5.92 us  [the longest x1 3.06 us: squares_of(): pl.pallas_call(squares_kernel, in_specs=[vmem] * 4, out_specs=vmem, out_s...]
    ppermute x4, starting transfers between devices: 17.3 us -> 19.2 us  [swap(): return lax.ppermute(block, TENSOR, [(t, t ^ bits) for t in range(8)])]
  transfers between devices with their start and end apart: 7 -> 7, of which waited for: 5 -> 5; matrix products, arithmetic and copies ran while one was open for 1% -> 1% of each run, Pallas kernels for 1% -> 3%
where the time goes in v6:
time: 135 us
  starting transfers between devices  50.8 us (38%)
  waiting for transfers between devices  42.7 us (32%)
  blocking collectives  27.9 us (21%)
  Pallas kernels  12.2 us (9%)
    all_to_all x3, waiting for transfers between devices, exchange(): return lax.all_to_all(blocks, axes, 0, 0)  37.1 us
    all_to_all x3, starting transfers between devices, exchange(): return lax.all_to_all(blocks, axes, 0, 0)  31.6 us
    all_to_all x1, blocking collectives, exchange(): return lax.all_to_all(blocks, axes, 0, 0)  27.9 us
    ppermute x4, starting transfers between devices, swap(): return lax.ppermute(block, TENSOR, [(t, t ^ bits) for t in range(8)])  19.2 us
    ppermute x4, waiting for transfers between devices, swap(): return lax.ppermute(block, TENSOR, [(t, t ^ bits) for t in range(8)])  5.66 us
    pallas_call x1, Pallas kernels, share(): pl.pallas_call(share_kernel, grid=(features // width,), in_specs=[pl.Bloc...  4.29 us
    pallas_call x1, Pallas kernels, squares_of(): pl.pallas_call(squares_kernel, in_specs=[vmem] * 4, out_specs=vmem, out_s...  3.06 us
    pallas_call x1, Pallas kernels, project(): pl.pallas_call(project_kernel, in_specs=[vmem] * 6, out_specs=(vmem,) * 2...  2.85 us
  transfers between devices with their start and end apart: 7, of which 5 were waited for; matrix products, arithmetic and copies ran while one was open for 1% of the time, Pallas kernels for 3%

profile of v6, /device:TPU:1, one launch (start us, length us, event | category | flops | bytes accessed | tf_op | source)
XLA Modules:
  0.0 134.6 jit_solution(7999079736446471022)
XLA Ops:
  0.0 4.3 %shard_map.73 = bf16[1024,1024]{1,0:T(8,128)(2,1)} custom-call(bf16[512,1024]{1,0:T(8,128)(2,1)} %bitcast.22, bf16[512,1024]{1,0:T(8,128)(2,1)} %bitcast.23, bf16[128,1024]{1,0:T(8,128)(2,1)} %bitcast.24, f32[128,128]{1,0:T(8,128)} %bitcast.25, f32[128,128]{1,0:T(8,128)} %bitcast.26, f32[1,1024]{1,0:T(1,128)} %bitcast.27), custom_call_target="tpu_custom_call" | custom-call | flops 1073741824 | bytes 6291456 | tf_op jit(solution)/shard_map/pallas_call | solution.py:56
  4.3 0.0 copy-start
  4.3 6.3 %all-to-all-start = ((bf16[8,128,1024]{2,1,0:T(8,128)(2,1)}), bf16[8,128,1024]{2,1,0:T(8,128)(2,1)S(1)}, u32[]{:S(2)}, u32[]{:S(2)}) async-start(bf16[8,128,1024]{2,1,0:T(8,128)(2,1)} %bitcast.19), calls=%async_computation | async-start | bytes 4194304 | tf_op jit(solution)/shard_map/all_to_all | solution.py:24
  10.6 0.0 copy-done
  10.6 4.7 %collective-permute-start.1 = (bf16[512,1024]{1,0:T(8,128)(2,1)S(1)}, bf16[512,1024]{1,0:T(8,128)(2,1)}, u32[]{:S(2)}, u32[]{:S(2)}) collective-permute-start(bf16[512,1024]{1,0:T(8,128)(2,1)S(1)} %bitcast.14), channel_id=1, source_target_pairs={{0,6},{1,7},{2,4},{3,5},{4,2},{5,3},{6,0},{7,1},{8,14},{9,15},{10,... | collective-permute-start | bytes 3145736 | tf_op jit(solution)/shard_map/ppermute | solution.py:194
  15.3 1.9 %collective-permute-start = (bf16[512,1024]{1,0:T(8,128)(2,1)S(1)}, bf16[512,1024]{1,0:T(8,128)(2,1)}, u32[]{:S(2)}, u32[]{:S(2)}) collective-permute-start(bf16[512,1024]{1,0:T(8,128)(2,1)S(1)} %bitcast.15), channel_id=1, source_target_pairs={{0,2},{1,3},{2,0},{3,1},{4,6},{5,7},{6,4},{7,5},{8,10},{9,11},{10,... | collective-permute-start | bytes 3145736 | tf_op jit(solution)/shard_map/ppermute | solution.py:194
  17.2 16.2 %all-to-all-done.blocks_ref = bf16[8,128,1024]{2,1,0:T(8,128)(2,1)S(1)} async-done(((bf16[8,128,1024]{2,1,0:T(8,128)(2,1)}), bf16[8,128,1024]{2,1,0:T(8,128)(2,1)S(1)}, u32[]{:S(2)}, u32[]{:S(2)}) %all-to-all-start) | async-done | bytes 2097184 | tf_op jit(solution)/shard_map/all_to_all | solution.py:24
  33.5 1.2 shard_map.74
  34.6 20.2 %all-to-all-start.1 = ((bf16[32,16,256]{2,1,0:T(8,128)(2,1)}), bf16[32,16,256]{2,1,0:T(8,128)(2,1)S(1)}, u32[]{:S(2)}, u32[]{:S(2)}) async-start(bf16[32,16,256]{2,1,0:T(8,128)(2,1)} %bitcast.7), calls=%async_computation.1 | async-start | bytes 524288 | tf_op jit(solution)/shard_map/all_to_all | solution.py:24
  54.8 4.6 %collective-permute-start.2 = (bf16[512,1024]{1,0:T(8,128)(2,1)S(1)}, bf16[512,1024]{1,0:T(8,128)(2,1)S(1)}, u32[]{:S(2)}, u32[]{:S(2)}) collective-permute-start(bf16[512,1024]{1,0:T(8,128)(2,1)S(1)} %bitcast.16), channel_id=1, source_target_pairs={{0,4},{1,5},{2,6},{3,7},{4,0},{5,1},{6,2},{7,3},{8,12},{9,13},{10,... | collective-permute-start | bytes 3145736 | tf_op jit(solution)/shard_map/ppermute | solution.py:194
  59.5 0.0 collective-permute-done.1.refs_3_
  59.5 0.0 collective-permute-done.refs_1_
  59.5 14.4 %all-to-all-done.1 = bf16[32,16,256]{2,1,0:T(8,128)(2,1)S(1)} async-done(((bf16[32,16,256]{2,1,0:T(8,128)(2,1)}), bf16[32,16,256]{2,1,0:T(8,128)(2,1)S(1)}, u32[]{:S(2)}, u32[]{:S(2)}) %all-to-all-start.1) | async-done | bytes 262176 | tf_op jit(solution)/shard_map/all_to_all | solution.py:24
  74.0 0.7 broadcast_in_dim.20
  74.7 5.1 %all-to-all-start.2 = ((bf16[8,4,16,256]{3,2,1,0:T(8,128)(2,1)}), bf16[8,4,16,256]{3,2,1,0:T(8,128)(2,1)S(1)}, u32[]{:S(2)}, u32[]{:S(2)}) async-start(bf16[8,4,16,256]{3,2,1,0:T(8,128)(2,1)} %broadcast_in_dim.20), calls=%async_computation.2 | async-start | bytes 524288 | tf_op jit(solution)/shard_map/all_to_all | solution.py:24
  79.8 4.5 %collective-permute-done.2.refs_2_ = bf16[512,1024]{1,0:T(8,128)(2,1)S(1)} collective-permute-done((bf16[512,1024]{1,0:T(8,128)(2,1)S(1)}, bf16[512,1024]{1,0:T(8,128)(2,1)S(1)}, u32[]{:S(2)}, u32[]{:S(2)}) %collective-permute-start.2) | collective-permute-done | bytes 1048608 | tf_op jit(solution)/shard_map/ppermute | solution.py:194
  84.3 3.1 %shard_map.75.squares_ref = f32[512,128]{1,0:T(8,128)S(1)} custom-call(bf16[512,1024]{1,0:T(8,128)(2,1)S(1)} %bitcast.17, bf16[512,1024]{1,0:T(8,128)(2,1)} %collective-permute-done.refs_1_, bf16[512,1024]{1,0:T(8,128)(2,1)S(1)} %collective-permute-done.2.refs_2_, bf16[512,1024]{1,0:T(8,128)(2,1)} %collective-permute-done.1.refs_3_), custom_call_target="tpu_custom_call" | custom-call | flops 4194304 | bytes 4194304 | tf_op jit(solution)/shard_map/pallas_call | solution.py:126
  87.4 6.4 %all-to-all-done.2 = bf16[8,4,16,256]{3,2,1,0:T(8,128)(2,1)S(1)} async-done(((bf16[8,4,16,256]{3,2,1,0:T(8,128)(2,1)}), bf16[8,4,16,256]{3,2,1,0:T(8,128)(2,1)S(1)}, u32[]{:S(2)}, u32[]{:S(2)}) %all-to-all-start.2) | async-done | bytes 262176 | tf_op jit(solution)/shard_map/all_to_all | solution.py:24
  93.8 0.1 broadcast_in_dim.22
  93.9 27.9 %all_to_all.20 = bf16[8,512,256]{2,1,0:T(8,128)(2,1)S(1)} all-to-all(bf16[8,512,256]{2,1,0:T(8,128)(2,1)S(1)} %broadcast_in_dim.22), channel_id=1, replica_groups=mesh['x'=4,'z3'=2,'z2'=2,'z1'=2,'z0'=2,'y'=4,'c'=2] {'x','z0'}, dimensions={0} | all-to-all | bytes 4194304 | tf_op jit(solution)/shard_map/all_to_all | solution.py:24
  121.8 2.9 %shard_map.76 = (f32[512,128]{1,0:T(8,128)S(1)}, bf16[512,256]{1,0:T(8,128)(2,1)S(1)}) custom-call(bf16[8,8,4,16,256]{4,3,2,1,0:T(8,128)(2,1)S(1)} %bitcast.13, f32[512,128]{1,0:T(8,128)S(1)} %shard_map.75.squares_ref, bf16[512,1024]{1,0:T(8,128)(2,1)S(1)} %bitcast.18, bf16[512,1024]{1,0:T(8,128)(2,1)} %collective-permute-done.refs_1_, ...), custom_call_target="tpu_custom_call" | custom-call | flops 1073741824 | bytes 6291456 | tf_op jit(solution)/shard_map/pallas_call | solution.py:158
  124.6 7.9 %collective-permute-start.3 = (bf16[512,256]{1,0:T(8,128)(2,1)S(1)}, bf16[512,256]{1,0:T(8,128)(2,1)S(1)}, u32[]{:S(2)}, u32[]{:S(2)}) collective-permute-start(bf16[512,256]{1,0:T(8,128)(2,1)S(1)} %get-tuple-element.20), channel_id=1, source_target_pairs={{0,1},{1,0},{2,3},{3,2},{4,5},{5,4},{6,7},{7,6},{8,9},{9,8},{10,11... | collective-permute-start | bytes 786440 | tf_op jit(solution)/shard_map/ppermute | solution.py:194
  132.6 1.1 collective-permute-done.3.got_ref
  133.7 0.9 shard_map.77
  (1 shorter events, 0.0 us)
Async XLA Ops:
  4.3 6.3 %copy-start = (bf16[1,512,1024]{2,1,0:T(8,128)(2,1)S(1)}, bf16[1,512,1024]{2,1,0:T(8,128)(2,1)}, u32[]{:S(2)}) copy-start(bf16[1,512,1024]{2,1,0:T(8,128)(2,1)} %param.12) | copy-start | bytes 3145732
  4.3 29.2 %all-to-all-start = ((bf16[8,128,1024]{2,1,0:T(8,128)(2,1)}), bf16[8,128,1024]{2,1,0:T(8,128)(2,1)S(1)}, u32[]{:S(2)}, u32[]{:S(2)}) async-start(bf16[8,128,1024]{2,1,0:T(8,128)(2,1)} %bitcast.19), calls=%async_computation | async-start | bytes 4194304 | tf_op jit(solution)/shard_map/all_to_all | solution.py:24
  10.6 48.8 %collective-permute-start.1 = (bf16[512,1024]{1,0:T(8,128)(2,1)S(1)}, bf16[512,1024]{1,0:T(8,128)(2,1)}, u32[]{:S(2)}, u32[]{:S(2)}) collective-permute-start(bf16[512,1024]{1,0:T(8,128)(2,1)S(1)} %bitcast.14), channel_id=1, source_target_pairs={{0,6},{1,7},{2,4},{3,5},{4,2},{5,3},{6,0},{7,1},{8,14},{9,15},{10,... | collective-permute-start | bytes 3145736 | tf_op jit(solution)/shard_map/ppermute | solution.py:194
  15.3 44.2 %collective-permute-start = (bf16[512,1024]{1,0:T(8,128)(2,1)S(1)}, bf16[512,1024]{1,0:T(8,128)(2,1)}, u32[]{:S(2)}, u32[]{:S(2)}) collective-permute-start(bf16[512,1024]{1,0:T(8,128)(2,1)S(1)} %bitcast.15), channel_id=1, source_target_pairs={{0,2},{1,3},{2,0},{3,1},{4,6},{5,7},{6,4},{7,5},{8,10},{9,11},{10,... | collective-permute-start | bytes 3145736 | tf_op jit(solution)/shard_map/ppermute | solution.py:194
  34.6 39.3 %all-to-all-start.1 = ((bf16[32,16,256]{2,1,0:T(8,128)(2,1)}), bf16[32,16,256]{2,1,0:T(8,128)(2,1)S(1)}, u32[]{:S(2)}, u32[]{:S(2)}) async-start(bf16[32,16,256]{2,1,0:T(8,128)(2,1)} %bitcast.7), calls=%async_computation.1 | async-start | bytes 524288 | tf_op jit(solution)/shard_map/all_to_all | solution.py:24
  54.8 29.5 %collective-permute-start.2 = (bf16[512,1024]{1,0:T(8,128)(2,1)S(1)}, bf16[512,1024]{1,0:T(8,128)(2,1)S(1)}, u32[]{:S(2)}, u32[]{:S(2)}) collective-permute-start(bf16[512,1024]{1,0:T(8,128)(2,1)S(1)} %bitcast.16), channel_id=1, source_target_pairs={{0,4},{1,5},{2,6},{3,7},{4,0},{5,1},{6,2},{7,3},{8,12},{9,13},{10,... | collective-permute-start | bytes 3145736 | tf_op jit(solution)/shard_map/ppermute | solution.py:194
  74.7 19.1 %all-to-all-start.2 = ((bf16[8,4,16,256]{3,2,1,0:T(8,128)(2,1)}), bf16[8,4,16,256]{3,2,1,0:T(8,128)(2,1)S(1)}, u32[]{:S(2)}, u32[]{:S(2)}) async-start(bf16[8,4,16,256]{3,2,1,0:T(8,128)(2,1)} %broadcast_in_dim.20), calls=%async_computation.2 | async-start | bytes 524288 | tf_op jit(solution)/shard_map/all_to_all | solution.py:24
  124.6 9.1 %collective-permute-start.3 = (bf16[512,256]{1,0:T(8,128)(2,1)S(1)}, bf16[512,256]{1,0:T(8,128)(2,1)S(1)}, u32[]{:S(2)}, u32[]{:S(2)}) collective-permute-start(bf16[512,256]{1,0:T(8,128)(2,1)S(1)} %get-tuple-element.20), channel_id=1, source_target_pairs={{0,1},{1,0},{2,3},{3,2},{4,5},{5,4},{6,7},{7,6},{8,9},{9,8},{10,11... | collective-permute-start | bytes 786440 | tf_op jit(solution)/shard_map/ppermute | solution.py:194

commit v7 on v6

--- a/solution.py
+++ b/solution.py
@@ -73,32 +73,20 @@
     )(x, g, weight, theta, momentum, gain)
 
 
-def total_kernel(blocks_ref, out_ref, vmem_ref, sems):
-    parts, size = 4, out_ref.shape[0] * 4
-    copies = []
-    for part in range(parts):
-        rows = pl.ds(part * size, size)
-        copies.append(
-            pltpu.make_async_copy(blocks_ref.at[:, rows], vmem_ref.at[:, rows], sems.at[part])
-        )
-        copies[-1].start()
-    for part in range(parts):
-        copies[part].wait()
-        rows = slice(part * size, (part + 1) * size)
-        block = jnp.sum(vmem_ref[:, rows].astype(F32), axis=0).astype(BF16)
-        for i in range(size // 16):
-            for j in range(4):
-                piece = block[i * 16 : (i + 1) * 16, j * 2 * R : (j + 1) * 2 * R]
-                out_ref[part * (size // 16) + i, j] = piece
+def total_kernel(blocks_ref, out_ref):
+    for i in range(out_ref.shape[0]):
+        rows = slice(i * 16, (i + 1) * 16)
+        block = jnp.sum(blocks_ref[:, rows].astype(F32), axis=0).astype(BF16)
+        for j in range(4):
+            out_ref[i, j] = block[:, j * 2 * R : (j + 1) * 2 * R]
 
 
 def total_far(blocks):
     return pl.pallas_call(
         total_kernel,
-        in_specs=[pl.BlockSpec(memory_space=pl.ANY)],
+        in_specs=[pl.BlockSpec(memory_space=pltpu.VMEM)],
         out_specs=pl.BlockSpec(memory_space=pltpu.VMEM),
         out_shape=jax.ShapeDtypeStruct((blocks.shape[1] // 16, 4, 16, 2 * R), BF16),
-        scratch_shapes=[pltpu.VMEM(blocks.shape, BF16), pltpu.SemaphoreType.DMA((4,))],
         compiler_params=pltpu.CompilerParams(vmem_limit_bytes=VMEM),
         cost_estimate=pl.CostEstimate(
             flops=blocks.size, bytes_accessed=3 * blocks.size, transcendentals=0

time: 135 us -> 135 us (level)
  no operation moved by 1% of the time
where the time goes in v7:
time: 135 us; the launch traced here: 134 us
  starting transfers between devices  50.8 us (38%)
  waiting for transfers between devices  42.7 us (32%)
  blocking collectives  27.9 us (21%)
  Pallas kernels  12 us (9%)
    all_to_all x3, waiting for transfers between devices, exchange(): return lax.all_to_all(blocks, axes, 0, 0)  37.1 us
    all_to_all x3, starting transfers between devices, exchange(): return lax.all_to_all(blocks, axes, 0, 0)  31.6 us
    all_to_all x1, blocking collectives, exchange(): return lax.all_to_all(blocks, axes, 0, 0)  27.9 us
    ppermute x4, starting transfers between devices, swap(): return lax.ppermute(block, TENSOR, [(t, t ^ bits) for t in range(8)])  19.2 us
    ppermute x4, waiting for transfers between devices, swap(): return lax.ppermute(block, TENSOR, [(t, t ^ bits) for t in range(8)])  5.66 us
    pallas_call x1, Pallas kernels, share(): pl.pallas_call(share_kernel, grid=(features // width,), in_specs=[pl.Bloc...  4.29 us
    pallas_call x1, Pallas kernels, squares_of(): pl.pallas_call(squares_kernel, in_specs=[vmem] * 4, out_specs=vmem, out_s...  3.06 us
    pallas_call x1, Pallas kernels, project(): pl.pallas_call(project_kernel, in_specs=[vmem] * 6, out_specs=(vmem,) * 2...  2.85 us
  transfers between devices with their start and end apart: 7, of which 5 were waited for; matrix products, arithmetic and copies ran while one was open for 1% of the time, Pallas kernels for 3%

profile of v7, /device:TPU:1, one launch (start us, length us, event | category | flops | bytes accessed | tf_op | source)
XLA Modules:
  0.0 134.4 jit_solution(11293121792441829424)
XLA Ops:
  0.0 4.3 %shard_map.73 = bf16[1024,1024]{1,0:T(8,128)(2,1)} custom-call(bf16[512,1024]{1,0:T(8,128)(2,1)} %bitcast.22, bf16[512,1024]{1,0:T(8,128)(2,1)} %bitcast.23, bf16[128,1024]{1,0:T(8,128)(2,1)} %bitcast.24, f32[128,128]{1,0:T(8,128)} %bitcast.25, f32[128,128]{1,0:T(8,128)} %bitcast.26, f32[1,1024]{1,0:T(1,128)} %bitcast.27), custom_call_target="tpu_custom_call" | custom-call | flops 1073741824 | bytes 6291456 | tf_op jit(solution)/shard_map/pallas_call | solution.py:56
  4.3 0.0 copy-start
  4.3 6.3 %all-to-all-start = ((bf16[8,128,1024]{2,1,0:T(8,128)(2,1)}), bf16[8,128,1024]{2,1,0:T(8,128)(2,1)S(1)}, u32[]{:S(2)}, u32[]{:S(2)}) async-start(bf16[8,128,1024]{2,1,0:T(8,128)(2,1)} %bitcast.19), calls=%async_computation | async-start | bytes 4194304 | tf_op jit(solution)/shard_map/all_to_all | solution.py:24
  10.6 0.0 copy-done
  10.6 4.7 %collective-permute-start.1 = (bf16[512,1024]{1,0:T(8,128)(2,1)S(1)}, bf16[512,1024]{1,0:T(8,128)(2,1)}, u32[]{:S(2)}, u32[]{:S(2)}) collective-permute-start(bf16[512,1024]{1,0:T(8,128)(2,1)S(1)} %bitcast.14), channel_id=1, source_target_pairs={{0,6},{1,7},{2,4},{3,5},{4,2},{5,3},{6,0},{7,1},{8,14},{9,15},{10,... | collective-permute-start | bytes 3145736 | tf_op jit(solution)/shard_map/ppermute | solution.py:182
  15.3 1.9 %collective-permute-start = (bf16[512,1024]{1,0:T(8,128)(2,1)S(1)}, bf16[512,1024]{1,0:T(8,128)(2,1)}, u32[]{:S(2)}, u32[]{:S(2)}) collective-permute-start(bf16[512,1024]{1,0:T(8,128)(2,1)S(1)} %bitcast.15), channel_id=1, source_target_pairs={{0,2},{1,3},{2,0},{3,1},{4,6},{5,7},{6,4},{7,5},{8,10},{9,11},{10,... | collective-permute-start | bytes 3145736 | tf_op jit(solution)/shard_map/ppermute | solution.py:182
  17.2 16.2 %all-to-all-done.blocks_ref = bf16[8,128,1024]{2,1,0:T(8,128)(2,1)S(1)} async-done(((bf16[8,128,1024]{2,1,0:T(8,128)(2,1)}), bf16[8,128,1024]{2,1,0:T(8,128)(2,1)S(1)}, u32[]{:S(2)}, u32[]{:S(2)}) %all-to-all-start) | async-done | bytes 2097184 | tf_op jit(solution)/shard_map/all_to_all | solution.py:24
  33.5 1.0 shard_map.74
  34.4 20.2 %all-to-all-start.1 = ((bf16[32,16,256]{2,1,0:T(8,128)(2,1)}), bf16[32,16,256]{2,1,0:T(8,128)(2,1)S(1)}, u32[]{:S(2)}, u32[]{:S(2)}) async-start(bf16[32,16,256]{2,1,0:T(8,128)(2,1)} %bitcast.7), calls=%async_computation.1 | async-start | bytes 524288 | tf_op jit(solution)/shard_map/all_to_all | solution.py:24
  54.6 4.6 %collective-permute-start.2 = (bf16[512,1024]{1,0:T(8,128)(2,1)S(1)}, bf16[512,1024]{1,0:T(8,128)(2,1)S(1)}, u32[]{:S(2)}, u32[]{:S(2)}) collective-permute-start(bf16[512,1024]{1,0:T(8,128)(2,1)S(1)} %bitcast.16), channel_id=1, source_target_pairs={{0,4},{1,5},{2,6},{3,7},{4,0},{5,1},{6,2},{7,3},{8,12},{9,13},{10,... | collective-permute-start | bytes 3145736 | tf_op jit(solution)/shard_map/ppermute | solution.py:182
  59.3 0.0 collective-permute-done.1.refs_3_
  59.3 0.0 collective-permute-done.refs_1_
  59.3 14.4 %all-to-all-done.1 = bf16[32,16,256]{2,1,0:T(8,128)(2,1)S(1)} async-done(((bf16[32,16,256]{2,1,0:T(8,128)(2,1)}), bf16[32,16,256]{2,1,0:T(8,128)(2,1)S(1)}, u32[]{:S(2)}, u32[]{:S(2)}) %all-to-all-start.1) | async-done | bytes 262176 | tf_op jit(solution)/shard_map/all_to_all | solution.py:24
  73.7 0.7 broadcast_in_dim.20
  74.5 5.1 %all-to-all-start.2 = ((bf16[8,4,16,256]{3,2,1,0:T(8,128)(2,1)}), bf16[8,4,16,256]{3,2,1,0:T(8,128)(2,1)S(1)}, u32[]{:S(2)}, u32[]{:S(2)}) async-start(bf16[8,4,16,256]{3,2,1,0:T(8,128)(2,1)} %broadcast_in_dim.20), calls=%async_computation.2 | async-start | bytes 524288 | tf_op jit(solution)/shard_map/all_to_all | solution.py:24
  79.6 4.5 %collective-permute-done.2.refs_2_ = bf16[512,1024]{1,0:T(8,128)(2,1)S(1)} collective-permute-done((bf16[512,1024]{1,0:T(8,128)(2,1)S(1)}, bf16[512,1024]{1,0:T(8,128)(2,1)S(1)}, u32[]{:S(2)}, u32[]{:S(2)}) %collective-permute-start.2) | collective-permute-done | bytes 1048608 | tf_op jit(solution)/shard_map/ppermute | solution.py:182
  84.1 3.1 %shard_map.75.squares_ref = f32[512,128]{1,0:T(8,128)S(1)} custom-call(bf16[512,1024]{1,0:T(8,128)(2,1)S(1)} %bitcast.17, bf16[512,1024]{1,0:T(8,128)(2,1)} %collective-permute-done.refs_1_, bf16[512,1024]{1,0:T(8,128)(2,1)S(1)} %collective-permute-done.2.refs_2_, bf16[512,1024]{1,0:T(8,128)(2,1)} %collective-permute-done.1.refs_3_), custom_call_target="tpu_custom_call" | custom-call | flops 4194304 | bytes 4194304 | tf_op jit(solution)/shard_map/pallas_call | solution.py:114
  87.1 6.4 %all-to-all-done.2 = bf16[8,4,16,256]{3,2,1,0:T(8,128)(2,1)S(1)} async-done(((bf16[8,4,16,256]{3,2,1,0:T(8,128)(2,1)}), bf16[8,4,16,256]{3,2,1,0:T(8,128)(2,1)S(1)}, u32[]{:S(2)}, u32[]{:S(2)}) %all-to-all-start.2) | async-done | bytes 262176 | tf_op jit(solution)/shard_map/all_to_all | solution.py:24
  93.6 0.1 broadcast_in_dim.22
  93.7 27.9 %all_to_all.20 = bf16[8,512,256]{2,1,0:T(8,128)(2,1)S(1)} all-to-all(bf16[8,512,256]{2,1,0:T(8,128)(2,1)S(1)} %broadcast_in_dim.22), channel_id=1, replica_groups=mesh['x'=4,'z3'=2,'z2'=2,'z1'=2,'z0'=2,'y'=4,'c'=2] {'x','z0'}, dimensions={0} | all-to-all | bytes 4194304 | tf_op jit(solution)/shard_map/all_to_all | solution.py:24
  121.6 2.9 %shard_map.76 = (f32[512,128]{1,0:T(8,128)S(1)}, bf16[512,256]{1,0:T(8,128)(2,1)S(1)}) custom-call(bf16[8,8,4,16,256]{4,3,2,1,0:T(8,128)(2,1)S(1)} %bitcast.13, f32[512,128]{1,0:T(8,128)S(1)} %shard_map.75.squares_ref, bf16[512,1024]{1,0:T(8,128)(2,1)S(1)} %bitcast.18, bf16[512,1024]{1,0:T(8,128)(2,1)} %collective-permute-done.refs_1_, ...), custom_call_target="tpu_custom_call" | custom-call | flops 1073741824 | bytes 6291456 | tf_op jit(solution)/shard_map/pallas_call | solution.py:146
  124.4 7.9 %collective-permute-start.3 = (bf16[512,256]{1,0:T(8,128)(2,1)S(1)}, bf16[512,256]{1,0:T(8,128)(2,1)S(1)}, u32[]{:S(2)}, u32[]{:S(2)}) collective-permute-start(bf16[512,256]{1,0:T(8,128)(2,1)S(1)} %get-tuple-element.20), channel_id=1, source_target_pairs={{0,1},{1,0},{2,3},{3,2},{4,5},{5,4},{6,7},{7,6},{8,9},{9,8},{10,11... | collective-permute-start | bytes 786440 | tf_op jit(solution)/shard_map/ppermute | solution.py:182
  132.4 1.1 collective-permute-done.3.got_ref
  133.5 0.9 shard_map.77
  (1 shorter events, 0.0 us)
Async XLA Ops:
  4.3 6.3 %copy-start = (bf16[1,512,1024]{2,1,0:T(8,128)(2,1)S(1)}, bf16[1,512,1024]{2,1,0:T(8,128)(2,1)}, u32[]{:S(2)}) copy-start(bf16[1,512,1024]{2,1,0:T(8,128)(2,1)} %param.12) | copy-start | bytes 3145732
  4.3 29.2 %all-to-all-start = ((bf16[8,128,1024]{2,1,0:T(8,128)(2,1)}), bf16[8,128,1024]{2,1,0:T(8,128)(2,1)S(1)}, u32[]{:S(2)}, u32[]{:S(2)}) async-start(bf16[8,128,1024]{2,1,0:T(8,128)(2,1)} %bitcast.19), calls=%async_computation | async-start | bytes 4194304 | tf_op jit(solution)/shard_map/all_to_all | solution.py:24
  10.6 48.6 %collective-permute-start.1 = (bf16[512,1024]{1,0:T(8,128)(2,1)S(1)}, bf16[512,1024]{1,0:T(8,128)(2,1)}, u32[]{:S(2)}, u32[]{:S(2)}) collective-permute-start(bf16[512,1024]{1,0:T(8,128)(2,1)S(1)} %bitcast.14), channel_id=1, source_target_pairs={{0,6},{1,7},{2,4},{3,5},{4,2},{5,3},{6,0},{7,1},{8,14},{9,15},{10,... | collective-permute-start | bytes 3145736 | tf_op jit(solution)/shard_map/ppermute | solution.py:182
  15.3 44.0 %collective-permute-start = (bf16[512,1024]{1,0:T(8,128)(2,1)S(1)}, bf16[512,1024]{1,0:T(8,128)(2,1)}, u32[]{:S(2)}, u32[]{:S(2)}) collective-permute-start(bf16[512,1024]{1,0:T(8,128)(2,1)S(1)} %bitcast.15), channel_id=1, source_target_pairs={{0,2},{1,3},{2,0},{3,1},{4,6},{5,7},{6,4},{7,5},{8,10},{9,11},{10,... | collective-permute-start | bytes 3145736 | tf_op jit(solution)/shard_map/ppermute | solution.py:182
  34.4 39.3 %all-to-all-start.1 = ((bf16[32,16,256]{2,1,0:T(8,128)(2,1)}), bf16[32,16,256]{2,1,0:T(8,128)(2,1)S(1)}, u32[]{:S(2)}, u32[]{:S(2)}) async-start(bf16[32,16,256]{2,1,0:T(8,128)(2,1)} %bitcast.7), calls=%async_computation.1 | async-start | bytes 524288 | tf_op jit(solution)/shard_map/all_to_all | solution.py:24
  54.6 29.5 %collective-permute-start.2 = (bf16[512,1024]{1,0:T(8,128)(2,1)S(1)}, bf16[512,1024]{1,0:T(8,128)(2,1)S(1)}, u32[]{:S(2)}, u32[]{:S(2)}) collective-permute-start(bf16[512,1024]{1,0:T(8,128)(2,1)S(1)} %bitcast.16), channel_id=1, source_target_pairs={{0,4},{1,5},{2,6},{3,7},{4,0},{5,1},{6,2},{7,3},{8,12},{9,13},{10,... | collective-permute-start | bytes 3145736 | tf_op jit(solution)/shard_map/ppermute | solution.py:182
  74.5 19.1 %all-to-all-start.2 = ((bf16[8,4,16,256]{3,2,1,0:T(8,128)(2,1)}), bf16[8,4,16,256]{3,2,1,0:T(8,128)(2,1)S(1)}, u32[]{:S(2)}, u32[]{:S(2)}) async-start(bf16[8,4,16,256]{3,2,1,0:T(8,128)(2,1)} %broadcast_in_dim.20), calls=%async_computation.2 | async-start | bytes 524288 | tf_op jit(solution)/shard_map/all_to_all | solution.py:24
  124.4 9.1 %collective-permute-start.3 = (bf16[512,256]{1,0:T(8,128)(2,1)S(1)}, bf16[512,256]{1,0:T(8,128)(2,1)S(1)}, u32[]{:S(2)}, u32[]{:S(2)}) collective-permute-start(bf16[512,256]{1,0:T(8,128)(2,1)S(1)} %get-tuple-element.20), channel_id=1, source_target_pairs={{0,1},{1,0},{2,3},{3,2},{4,5},{5,4},{6,7},{7,6},{8,9},{9,8},{10,11... | collective-permute-start | bytes 786440 | tf_op jit(solution)/shard_map/ppermute | solution.py:182

commit v8 on v7

--- a/solution.py
+++ b/solution.py
@@ -28,7 +28,7 @@
     return jnp.sum(blocks.astype(F32), axis=0)
 
 
-def share_kernel(x_ref, g_ref, w_ref, theta_ref, momentum_ref, gain_ref, out_ref):
+def share_kernel(x_ref, g_ref, w_ref, theta_ref, momentum_ref, gain_ref, out_ref, held, sems):
     step = pl.program_id(0)
     island, fsdp = lax.axis_index(ISLAND), lax.axis_index(FSDP)
     width = x_ref.shape[1]
@@ -42,10 +42,29 @@
         band.append(SHARE * w_ref[:, j * R : (j + 1) * R].astype(F32) + jnp.where(here, own, 0.0))
     band = jnp.concatenate(band, axis=1).T
     gain = jnp.broadcast_to(gain_ref[...], (R, width)).T
-    for j in range(out_ref.shape[1] // R):
-        piece = (-0.03 * SHARE) * term[:, j * R : (j + 1) * R]
-        piece += jnp.where(fsdp == j, band, 0.0)
-        out_ref[:, j * R : (j + 1) * R] = (piece * gain).astype(BF16)
+    chunk = width // 2
+    steps = out_ref.shape[0] // width
+    copies = []
+    for at in range(2 * steps):
+        rows = pl.ds(at * chunk, chunk)
+        copies.append(pltpu.make_async_copy(held.at[rows], out_ref.at[rows], sems.at[at]))
+    for at in range(2):
+        rows = slice(at * chunk, (at + 1) * chunk)
+        place = pl.ds(pl.multiple_of(step * width + at * chunk, chunk), chunk)
+        for j in range(out_ref.shape[1] // R):
+            piece = (-0.03 * SHARE) * term[rows, j * R : (j + 1) * R]
+            piece += jnp.where(fsdp == j, band[rows], 0.0)
+            held[place, j * R : (j + 1) * R] = (piece * gain[rows]).astype(BF16)
+        for here in range(steps):
+
+            @pl.when(step == here)
+            def _():
+                copies[2 * here + at].start()
+
+    @pl.when(step == steps - 1)
+    def _():
+        for copy in copies:
+            copy.wait()
 
 
 def share(x, g, weight, theta, momentum, gain):
@@ -64,8 +83,12 @@
             whole(R, R),
             pl.BlockSpec((1, width), lambda i: (0, i)),
         ],
-        out_specs=pl.BlockSpec((width, keys), lambda i: (i, 0)),
+        out_specs=pl.BlockSpec(memory_space=pl.ANY),
         out_shape=jax.ShapeDtypeStruct((features, keys), BF16),
+        scratch_shapes=[
+            pltpu.VMEM((features, keys), BF16),
+            pltpu.SemaphoreType.DMA((2 * features // width,)),
+        ],
         compiler_params=pltpu.CompilerParams(vmem_limit_bytes=60 * 2**20),
         cost_estimate=pl.CostEstimate(
             flops=2 * tokens * features * keys, bytes_accessed=6 * 2**20, transcendentals=0

time: 135 us -> 135 us (level)
  no operation moved by 1% of the time
where the time goes in v8:
time: 135 us; the launch traced here: 134 us
  starting transfers between devices  50.8 us (38%)
  waiting for transfers between devices  42.7 us (32%)
  blocking collectives  27.9 us (21%)
  Pallas kernels  12 us (9%)
    all_to_all x3, waiting for transfers between devices, exchange(): return lax.all_to_all(blocks, axes, 0, 0)  37.1 us
    all_to_all x3, starting transfers between devices, exchange(): return lax.all_to_all(blocks, axes, 0, 0)  31.6 us
    all_to_all x1, blocking collectives, exchange(): return lax.all_to_all(blocks, axes, 0, 0)  27.9 us
    ppermute x4, starting transfers between devices, swap(): return lax.ppermute(block, TENSOR, [(t, t ^ bits) for t in range(8)])  19.1 us
    ppermute x4, waiting for transfers between devices, swap(): return lax.ppermute(block, TENSOR, [(t, t ^ bits) for t in range(8)])  5.66 us
    pallas_call x1, Pallas kernels, share(): pl.pallas_call(share_kernel, grid=(features // width,), in_specs=[pl.Bloc...  4.25 us
    pallas_call x1, Pallas kernels, squares_of(): pl.pallas_call(squares_kernel, in_specs=[vmem] * 4, out_specs=vmem, out_s...  3.06 us
    pallas_call x1, Pallas kernels, project(): pl.pallas_call(project_kernel, in_specs=[vmem] * 6, out_specs=(vmem,) * 2...  2.85 us
  transfers between devices with their start and end apart: 7, of which 5 were waited for; matrix products, arithmetic and copies ran while one was open for 1% of the time, Pallas kernels for 3%

profile of v8, /device:TPU:1, one launch (start us, length us, event | category | flops | bytes accessed | tf_op | source)
XLA Modules:
  0.0 134.4 jit_solution(15009258071539233178)
XLA Ops:
  0.0 4.3 %shard_map.73 = bf16[1024,1024]{1,0:T(8,128)(2,1)} custom-call(bf16[512,1024]{1,0:T(8,128)(2,1)} %bitcast.22, bf16[512,1024]{1,0:T(8,128)(2,1)} %bitcast.23, bf16[128,1024]{1,0:T(8,128)(2,1)} %bitcast.24, f32[128,128]{1,0:T(8,128)} %bitcast.25, f32[128,128]{1,0:T(8,128)} %bitcast.26, f32[1,1024]{1,0:T(1,128)} %bitcast.27), custom_call_target="tpu_custom_call" | custom-call | flops 1073741824 | bytes 6291456 | tf_op jit(solution)/shard_map/pallas_call | solution.py:75
  4.3 0.0 copy-start
  4.3 6.3 %all-to-all-start = ((bf16[8,128,1024]{2,1,0:T(8,128)(2,1)}), bf16[8,128,1024]{2,1,0:T(8,128)(2,1)S(1)}, u32[]{:S(2)}, u32[]{:S(2)}) async-start(bf16[8,128,1024]{2,1,0:T(8,128)(2,1)} %bitcast.19), calls=%async_computation | async-start | bytes 4194304 | tf_op jit(solution)/shard_map/all_to_all | solution.py:24
  10.6 0.0 copy-done
  10.6 4.6 %collective-permute-start.1 = (bf16[512,1024]{1,0:T(8,128)(2,1)S(1)}, bf16[512,1024]{1,0:T(8,128)(2,1)}, u32[]{:S(2)}, u32[]{:S(2)}) collective-permute-start(bf16[512,1024]{1,0:T(8,128)(2,1)S(1)} %bitcast.14), channel_id=1, source_target_pairs={{0,6},{1,7},{2,4},{3,5},{4,2},{5,3},{6,0},{7,1},{8,14},{9,15},{10,... | collective-permute-start | bytes 3145736 | tf_op jit(solution)/shard_map/ppermute | solution.py:205
  15.3 1.9 %collective-permute-start = (bf16[512,1024]{1,0:T(8,128)(2,1)S(1)}, bf16[512,1024]{1,0:T(8,128)(2,1)}, u32[]{:S(2)}, u32[]{:S(2)}) collective-permute-start(bf16[512,1024]{1,0:T(8,128)(2,1)S(1)} %bitcast.15), channel_id=1, source_target_pairs={{0,2},{1,3},{2,0},{3,1},{4,6},{5,7},{6,4},{7,5},{8,10},{9,11},{10,... | collective-permute-start | bytes 3145736 | tf_op jit(solution)/shard_map/ppermute | solution.py:205
  17.2 16.2 %all-to-all-done.blocks_ref = bf16[8,128,1024]{2,1,0:T(8,128)(2,1)S(1)} async-done(((bf16[8,128,1024]{2,1,0:T(8,128)(2,1)}), bf16[8,128,1024]{2,1,0:T(8,128)(2,1)S(1)}, u32[]{:S(2)}, u32[]{:S(2)}) %all-to-all-start) | async-done | bytes 2097184 | tf_op jit(solution)/shard_map/all_to_all | solution.py:24
  33.5 1.0 shard_map.74
  34.4 20.2 %all-to-all-start.1 = ((bf16[32,16,256]{2,1,0:T(8,128)(2,1)}), bf16[32,16,256]{2,1,0:T(8,128)(2,1)S(1)}, u32[]{:S(2)}, u32[]{:S(2)}) async-start(bf16[32,16,256]{2,1,0:T(8,128)(2,1)} %bitcast.7), calls=%async_computation.1 | async-start | bytes 524288 | tf_op jit(solution)/shard_map/all_to_all | solution.py:24
  54.6 4.6 %collective-permute-start.2 = (bf16[512,1024]{1,0:T(8,128)(2,1)S(1)}, bf16[512,1024]{1,0:T(8,128)(2,1)S(1)}, u32[]{:S(2)}, u32[]{:S(2)}) collective-permute-start(bf16[512,1024]{1,0:T(8,128)(2,1)S(1)} %bitcast.16), channel_id=1, source_target_pairs={{0,4},{1,5},{2,6},{3,7},{4,0},{5,1},{6,2},{7,3},{8,12},{9,13},{10,... | collective-permute-start | bytes 3145736 | tf_op jit(solution)/shard_map/ppermute | solution.py:205
  59.3 0.0 collective-permute-done.1.refs_3_
  59.3 0.0 collective-permute-done.refs_1_
  59.3 14.4 %all-to-all-done.1 = bf16[32,16,256]{2,1,0:T(8,128)(2,1)S(1)} async-done(((bf16[32,16,256]{2,1,0:T(8,128)(2,1)}), bf16[32,16,256]{2,1,0:T(8,128)(2,1)S(1)}, u32[]{:S(2)}, u32[]{:S(2)}) %all-to-all-start.1) | async-done | bytes 262176 | tf_op jit(solution)/shard_map/all_to_all | solution.py:24
  73.7 0.7 broadcast_in_dim.20
  74.5 5.1 %all-to-all-start.2 = ((bf16[8,4,16,256]{3,2,1,0:T(8,128)(2,1)}), bf16[8,4,16,256]{3,2,1,0:T(8,128)(2,1)S(1)}, u32[]{:S(2)}, u32[]{:S(2)}) async-start(bf16[8,4,16,256]{3,2,1,0:T(8,128)(2,1)} %broadcast_in_dim.20), calls=%async_computation.2 | async-start | bytes 524288 | tf_op jit(solution)/shard_map/all_to_all | solution.py:24
  79.6 4.5 %collective-permute-done.2.refs_2_ = bf16[512,1024]{1,0:T(8,128)(2,1)S(1)} collective-permute-done((bf16[512,1024]{1,0:T(8,128)(2,1)S(1)}, bf16[512,1024]{1,0:T(8,128)(2,1)S(1)}, u32[]{:S(2)}, u32[]{:S(2)}) %collective-permute-start.2) | collective-permute-done | bytes 1048608 | tf_op jit(solution)/shard_map/ppermute | solution.py:205
  84.1 3.1 %shard_map.75.squares_ref = f32[512,128]{1,0:T(8,128)S(1)} custom-call(bf16[512,1024]{1,0:T(8,128)(2,1)S(1)} %bitcast.17, bf16[512,1024]{1,0:T(8,128)(2,1)} %collective-permute-done.refs_1_, bf16[512,1024]{1,0:T(8,128)(2,1)S(1)} %collective-permute-done.2.refs_2_, bf16[512,1024]{1,0:T(8,128)(2,1)} %collective-permute-done.1.refs_3_), custom_call_target="tpu_custom_call" | custom-call | flops 4194304 | bytes 4194304 | tf_op jit(solution)/shard_map/pallas_call | solution.py:137
  87.1 6.4 %all-to-all-done.2 = bf16[8,4,16,256]{3,2,1,0:T(8,128)(2,1)S(1)} async-done(((bf16[8,4,16,256]{3,2,1,0:T(8,128)(2,1)}), bf16[8,4,16,256]{3,2,1,0:T(8,128)(2,1)S(1)}, u32[]{:S(2)}, u32[]{:S(2)}) %all-to-all-start.2) | async-done | bytes 262176 | tf_op jit(solution)/shard_map/all_to_all | solution.py:24
  93.6 0.1 broadcast_in_dim.22
  93.7 27.9 %all_to_all.20 = bf16[8,512,256]{2,1,0:T(8,128)(2,1)S(1)} all-to-all(bf16[8,512,256]{2,1,0:T(8,128)(2,1)S(1)} %broadcast_in_dim.22), channel_id=1, replica_groups=mesh['x'=4,'z3'=2,'z2'=2,'z1'=2,'z0'=2,'y'=4,'c'=2] {'x','z0'}, dimensions={0} | all-to-all | bytes 4194304 | tf_op jit(solution)/shard_map/all_to_all | solution.py:24
  121.6 2.9 %shard_map.76 = (f32[512,128]{1,0:T(8,128)S(1)}, bf16[512,256]{1,0:T(8,128)(2,1)S(1)}) custom-call(bf16[8,8,4,16,256]{4,3,2,1,0:T(8,128)(2,1)S(1)} %bitcast.13, f32[512,128]{1,0:T(8,128)S(1)} %shard_map.75.squares_ref, bf16[512,1024]{1,0:T(8,128)(2,1)S(1)} %bitcast.18, bf16[512,1024]{1,0:T(8,128)(2,1)} %collective-permute-done.refs_1_, ...), custom_call_target="tpu_custom_call" | custom-call | flops 1073741824 | bytes 6291456 | tf_op jit(solution)/shard_map/pallas_call | solution.py:169
  124.4 7.9 %collective-permute-start.3 = (bf16[512,256]{1,0:T(8,128)(2,1)S(1)}, bf16[512,256]{1,0:T(8,128)(2,1)S(1)}, u32[]{:S(2)}, u32[]{:S(2)}) collective-permute-start(bf16[512,256]{1,0:T(8,128)(2,1)S(1)} %get-tuple-element.20), channel_id=1, source_target_pairs={{0,1},{1,0},{2,3},{3,2},{4,5},{5,4},{6,7},{7,6},{8,9},{9,8},{10,11... | collective-permute-start | bytes 786440 | tf_op jit(solution)/shard_map/ppermute | solution.py:205
  132.4 1.1 collective-permute-done.3.got_ref
  133.5 0.9 shard_map.77
  (1 shorter events, 0.0 us)
Async XLA Ops:
  4.3 6.4 %copy-start = (bf16[1,512,1024]{2,1,0:T(8,128)(2,1)S(1)}, bf16[1,512,1024]{2,1,0:T(8,128)(2,1)}, u32[]{:S(2)}) copy-start(bf16[1,512,1024]{2,1,0:T(8,128)(2,1)} %param.12) | copy-start | bytes 3145732
  4.3 29.2 %all-to-all-start = ((bf16[8,128,1024]{2,1,0:T(8,128)(2,1)}), bf16[8,128,1024]{2,1,0:T(8,128)(2,1)S(1)}, u32[]{:S(2)}, u32[]{:S(2)}) async-start(bf16[8,128,1024]{2,1,0:T(8,128)(2,1)} %bitcast.19), calls=%async_computation | async-start | bytes 4194304 | tf_op jit(solution)/shard_map/all_to_all | solution.py:24
  10.6 48.6 %collective-permute-start.1 = (bf16[512,1024]{1,0:T(8,128)(2,1)S(1)}, bf16[512,1024]{1,0:T(8,128)(2,1)}, u32[]{:S(2)}, u32[]{:S(2)}) collective-permute-start(bf16[512,1024]{1,0:T(8,128)(2,1)S(1)} %bitcast.14), channel_id=1, source_target_pairs={{0,6},{1,7},{2,4},{3,5},{4,2},{5,3},{6,0},{7,1},{8,14},{9,15},{10,... | collective-permute-start | bytes 3145736 | tf_op jit(solution)/shard_map/ppermute | solution.py:205
  15.3 44.0 %collective-permute-start = (bf16[512,1024]{1,0:T(8,128)(2,1)S(1)}, bf16[512,1024]{1,0:T(8,128)(2,1)}, u32[]{:S(2)}, u32[]{:S(2)}) collective-permute-start(bf16[512,1024]{1,0:T(8,128)(2,1)S(1)} %bitcast.15), channel_id=1, source_target_pairs={{0,2},{1,3},{2,0},{3,1},{4,6},{5,7},{6,4},{7,5},{8,10},{9,11},{10,... | collective-permute-start | bytes 3145736 | tf_op jit(solution)/shard_map/ppermute | solution.py:205
  34.4 39.3 %all-to-all-start.1 = ((bf16[32,16,256]{2,1,0:T(8,128)(2,1)}), bf16[32,16,256]{2,1,0:T(8,128)(2,1)S(1)}, u32[]{:S(2)}, u32[]{:S(2)}) async-start(bf16[32,16,256]{2,1,0:T(8,128)(2,1)} %bitcast.7), calls=%async_computation.1 | async-start | bytes 524288 | tf_op jit(solution)/shard_map/all_to_all | solution.py:24
  54.6 29.5 %collective-permute-start.2 = (bf16[512,1024]{1,0:T(8,128)(2,1)S(1)}, bf16[512,1024]{1,0:T(8,128)(2,1)S(1)}, u32[]{:S(2)}, u32[]{:S(2)}) collective-permute-start(bf16[512,1024]{1,0:T(8,128)(2,1)S(1)} %bitcast.16), channel_id=1, source_target_pairs={{0,4},{1,5},{2,6},{3,7},{4,0},{5,1},{6,2},{7,3},{8,12},{9,13},{10,... | collective-permute-start | bytes 3145736 | tf_op jit(solution)/shard_map/ppermute | solution.py:205
  74.5 19.1 %all-to-all-start.2 = ((bf16[8,4,16,256]{3,2,1,0:T(8,128)(2,1)}), bf16[8,4,16,256]{3,2,1,0:T(8,128)(2,1)S(1)}, u32[]{:S(2)}, u32[]{:S(2)}) async-start(bf16[8,4,16,256]{3,2,1,0:T(8,128)(2,1)} %broadcast_in_dim.20), calls=%async_computation.2 | async-start | bytes 524288 | tf_op jit(solution)/shard_map/all_to_all | solution.py:24
  124.4 9.1 %collective-permute-start.3 = (bf16[512,256]{1,0:T(8,128)(2,1)S(1)}, bf16[512,256]{1,0:T(8,128)(2,1)S(1)}, u32[]{:S(2)}, u32[]{:S(2)}) collective-permute-start(bf16[512,256]{1,0:T(8,128)(2,1)S(1)} %get-tuple-element.20), channel_id=1, source_target_pairs={{0,1},{1,0},{2,3},{3,2},{4,5},{5,4},{6,7},{7,6},{8,9},{9,8},{10,11... | collective-permute-start | bytes 786440 | tf_op jit(solution)/shard_map/ppermute | solution.py:205

commit v9 on v7

--- a/solution.py
+++ b/solution.py
@@ -17,7 +17,7 @@
 STEP = 0.7 * 1.9
 SHARE = STEP / ISLANDS
 F32, BF16 = jnp.float32, jnp.bfloat16
-VMEM = 16 * 2**20
+VMEM = 12 * 2**20
 
 
 def exchange(blocks, axes):
@@ -197,12 +197,12 @@
     x_up, x_down, x_far = (swap(x_own, bits) for bits in (2, 6, 4))
     sums = exchange(term.reshape(8, -1, keys), NEAR)
     fresh = exchange(total_far(sums).reshape(32, -1, 2 * R), FAR + ("y",))
-    fresh, x_up, x_down = lax.optimization_barrier((fresh, x_up, x_down))
+    fresh, x_far = lax.optimization_barrier((fresh, x_far))
     fresh = jnp.sum(fresh.reshape(8, 4, -1, 2 * R).astype(F32), axis=0).astype(BF16)
     mine = exchange(jnp.broadcast_to(fresh[None], (8, *fresh.shape)), FAR)
     blocks = (x_own, x_up, x_far, x_down)
     squares = squares_of(blocks)
-    mine, x_far, squares = lax.optimization_barrier((mine, x_far, squares))
+    mine, squares = lax.optimization_barrier((mine, squares))
     mine = mine.reshape(-1, 2 * R)
     weight = exchange(jnp.broadcast_to(mine[None], (8, *mine.shape)), NEAR)
     weight = weight.reshape(8, 8, 4, -1, 2 * R)

time: 135 us -> 136 us (level)
    ppermute x4, waiting for transfers between devices: 5.66 us -> 7.15 us  [swap(): return lax.ppermute(block, TENSOR, [(t, t ^ bits) for t in range(8)])]
  transfers between devices with their start and end apart: 7 -> 7, of which waited for: 5 -> 6; matrix products, arithmetic and copies ran while one was open for 1% -> 1% of each run, Pallas kernels for 3% -> 3%
where the time goes in v9:
time: 136 us; the launch traced here: 135 us
  starting transfers between devices  50.9 us (37%)
  waiting for transfers between devices  43.4 us (32%)
  blocking collectives  27.4 us (20%)
  Pallas kernels  11.4 us (8%)
  local copies, waits for them, and re-layouts  1.81 us (1%)
    all_to_all x3, waiting for transfers between devices, exchange(): return lax.all_to_all(blocks, axes, 0, 0)  36.2 us
    all_to_all x3, starting transfers between devices, exchange(): return lax.all_to_all(blocks, axes, 0, 0)  31.4 us
    all_to_all x1, blocking collectives, exchange(): return lax.all_to_all(blocks, axes, 0, 0)  27.4 us
    ppermute x4, starting transfers between devices, swap(): return lax.ppermute(block, TENSOR, [(t, t ^ bits) for t in range(8)])  19.5 us
    ppermute x4, waiting for transfers between devices, swap(): return lax.ppermute(block, TENSOR, [(t, t ^ bits) for t in range(8)])  7.15 us
    pallas_call x1, Pallas kernels, share(): pl.pallas_call(share_kernel, grid=(features // width,), in_specs=[pl.Bloc...  4.29 us
    pallas_call x1, Pallas kernels, squares_of(): pl.pallas_call(squares_kernel, in_specs=[vmem] * 4, out_specs=vmem, out_s...  2.75 us
  transfers between devices with their start and end apart: 7, of which 6 were waited for; matrix products, arithmetic and copies ran while one was open for 1% of the time, Pallas kernels for 3%

profile of v9, /device:TPU:1, one launch (start us, length us, event | category | flops | bytes accessed | tf_op | source)
XLA Modules:
  0.0 135.0 jit_solution(12602598613603627738)
XLA Ops:
  0.0 4.3 %shard_map.73 = bf16[1024,1024]{1,0:T(8,128)(2,1)} custom-call(bf16[512,1024]{1,0:T(8,128)(2,1)} %bitcast.21, bf16[512,1024]{1,0:T(8,128)(2,1)} %bitcast.22, bf16[128,1024]{1,0:T(8,128)(2,1)} %bitcast.23, f32[128,128]{1,0:T(8,128)} %bitcast.24, f32[128,128]{1,0:T(8,128)} %bitcast.25, f32[1,1024]{1,0:T(1,128)} %bitcast.26), custom_call_target="tpu_custom_call" | custom-call | flops 1073741824 | bytes 6291456 | tf_op jit(solution)/shard_map/pallas_call | solution.py:56
  4.3 0.0 copy-start
  4.3 6.3 %all-to-all-start = ((bf16[8,128,1024]{2,1,0:T(8,128)(2,1)}), bf16[8,128,1024]{2,1,0:T(8,128)(2,1)S(1)}, u32[]{:S(2)}, u32[]{:S(2)}) async-start(bf16[8,128,1024]{2,1,0:T(8,128)(2,1)} %bitcast.19), calls=%async_computation | async-start | bytes 4194304 | tf_op jit(solution)/shard_map/all_to_all | solution.py:24
  10.6 0.0 copy-done
  10.6 4.8 %collective-permute-start = (bf16[512,1024]{1,0:T(8,128)(2,1)S(1)}, bf16[512,1024]{1,0:T(8,128)(2,1)}, u32[]{:S(2)}, u32[]{:S(2)}) collective-permute-start(bf16[512,1024]{1,0:T(8,128)(2,1)S(1)} %bitcast.14), channel_id=1, source_target_pairs={{0,4},{1,5},{2,6},{3,7},{4,0},{5,1},{6,2},{7,3},{8,12},{9,13},{10,... | collective-permute-start | bytes 3145736 | tf_op jit(solution)/shard_map/ppermute | solution.py:182
  15.5 18.1 %all-to-all-done.blocks_ref = bf16[8,128,1024]{2,1,0:T(8,128)(2,1)S(1)} async-done(((bf16[8,128,1024]{2,1,0:T(8,128)(2,1)}), bf16[8,128,1024]{2,1,0:T(8,128)(2,1)S(1)}, u32[]{:S(2)}, u32[]{:S(2)}) %all-to-all-start) | async-done | bytes 2097184 | tf_op jit(solution)/shard_map/all_to_all | solution.py:24
  33.6 1.0 shard_map.74
  34.5 20.1 %all-to-all-start.1 = ((bf16[32,16,256]{2,1,0:T(8,128)(2,1)}), bf16[32,16,256]{2,1,0:T(8,128)(2,1)S(1)}, u32[]{:S(2)}, u32[]{:S(2)}) async-start(bf16[32,16,256]{2,1,0:T(8,128)(2,1)} %bitcast.7), calls=%async_computation.1 | async-start | bytes 524288 | tf_op jit(solution)/shard_map/all_to_all | solution.py:24
  54.6 4.3 %collective-permute-start.2 = (bf16[512,1024]{1,0:T(8,128)(2,1)S(1)}, bf16[512,1024]{1,0:T(8,128)(2,1)S(1)}, u32[]{:S(2)}, u32[]{:S(2)}) collective-permute-start(bf16[512,1024]{1,0:T(8,128)(2,1)S(1)} %bitcast.15), channel_id=1, source_target_pairs={{0,6},{1,7},{2,4},{3,5},{4,2},{5,3},{6,0},{7,1},{8,14},{9,15},{10,... | collective-permute-start | bytes 3145736 | tf_op jit(solution)/shard_map/ppermute | solution.py:182
  59.0 1.9 %collective-permute-start.1 = (bf16[512,1024]{1,0:T(8,128)(2,1)S(1)}, bf16[512,1024]{1,0:T(8,128)(2,1)S(1)}, u32[]{:S(2)}, u32[]{:S(2)}) collective-permute-start(bf16[512,1024]{1,0:T(8,128)(2,1)S(1)} %bitcast.16), channel_id=1, source_target_pairs={{0,2},{1,3},{2,0},{3,1},{4,6},{5,7},{6,4},{7,5},{8,10},{9,11},{10,... | collective-permute-start | bytes 3145736 | tf_op jit(solution)/shard_map/ppermute | solution.py:182
  60.9 0.0 collective-permute-done.refs_2_
  60.9 12.8 %all-to-all-done.1 = bf16[32,16,256]{2,1,0:T(8,128)(2,1)S(1)} async-done(((bf16[32,16,256]{2,1,0:T(8,128)(2,1)}), bf16[32,16,256]{2,1,0:T(8,128)(2,1)S(1)}, u32[]{:S(2)}, u32[]{:S(2)}) %all-to-all-start.1) | async-done | bytes 262176 | tf_op jit(solution)/shard_map/all_to_all | solution.py:24
  73.7 0.7 broadcast_in_dim.20
  74.5 5.0 %all-to-all-start.2 = ((bf16[8,4,16,256]{3,2,1,0:T(8,128)(2,1)}), bf16[8,4,16,256]{3,2,1,0:T(8,128)(2,1)}, u32[]{:S(2)}, u32[]{:S(2)}) async-start(bf16[8,4,16,256]{3,2,1,0:T(8,128)(2,1)} %broadcast_in_dim.20), calls=%async_computation.2 | async-start | bytes 524288 | tf_op jit(solution)/shard_map/all_to_all | solution.py:24
  79.4 4.0 %collective-permute-done.2.refs_3_ = bf16[512,1024]{1,0:T(8,128)(2,1)S(1)} collective-permute-done((bf16[512,1024]{1,0:T(8,128)(2,1)S(1)}, bf16[512,1024]{1,0:T(8,128)(2,1)S(1)}, u32[]{:S(2)}, u32[]{:S(2)}) %collective-permute-start.2) | collective-permute-done | bytes 1048608 | tf_op jit(solution)/shard_map/ppermute | solution.py:182
  83.4 2.1 %collective-permute-done.1.refs_1_ = bf16[512,1024]{1,0:T(8,128)(2,1)S(1)} collective-permute-done((bf16[512,1024]{1,0:T(8,128)(2,1)S(1)}, bf16[512,1024]{1,0:T(8,128)(2,1)S(1)}, u32[]{:S(2)}, u32[]{:S(2)}) %collective-permute-start.1) | collective-permute-done | bytes 1048608 | tf_op jit(solution)/shard_map/ppermute | solution.py:182
  85.4 2.7 %shard_map.75.squares_ref = f32[512,128]{1,0:T(8,128)S(1)} custom-call(bf16[512,1024]{1,0:T(8,128)(2,1)S(1)} %bitcast.17, bf16[512,1024]{1,0:T(8,128)(2,1)S(1)} %collective-permute-done.1.refs_1_, bf16[512,1024]{1,0:T(8,128)(2,1)} %collective-permute-done.refs_2_, bf16[512,1024]{1,0:T(8,128)(2,1)S(1)} %collective-permute-done.2.refs_3_), custom_call_target="tpu_custom_call" | custom-call | flops 4194304 | bytes 4194304 | tf_op jit(solution)/shard_map/pallas_call | solution.py:114
  88.2 5.3 %all-to-all-done.2 = bf16[8,4,16,256]{3,2,1,0:T(8,128)(2,1)} async-done(((bf16[8,4,16,256]{3,2,1,0:T(8,128)(2,1)}), bf16[8,4,16,256]{3,2,1,0:T(8,128)(2,1)}, u32[]{:S(2)}, u32[]{:S(2)}) %all-to-all-start.2) | async-done | bytes 262176 | tf_op jit(solution)/shard_map/all_to_all | solution.py:24
  93.5 1.1 broadcast_in_dim.22
  94.6 27.4 %all_to_all.20 = bf16[8,512,256]{2,1,0:T(8,128)(2,1)S(1)} all-to-all(bf16[8,512,256]{2,1,0:T(8,128)(2,1)S(1)} %broadcast_in_dim.22), channel_id=1, replica_groups=mesh['x'=4,'z3'=2,'z2'=2,'z1'=2,'z0'=2,'y'=4,'c'=2] {'x','z0'}, dimensions={0} | all-to-all | bytes 4194304 | tf_op jit(solution)/shard_map/all_to_all | solution.py:24
  122.0 2.5 %shard_map.76 = (f32[512,128]{1,0:T(8,128)S(1)}, bf16[512,256]{1,0:T(8,128)(2,1)S(1)}) custom-call(bf16[8,8,4,16,256]{4,3,2,1,0:T(8,128)(2,1)S(1)} %bitcast.13, f32[512,128]{1,0:T(8,128)S(1)} %shard_map.75.squares_ref, bf16[512,1024]{1,0:T(8,128)(2,1)S(1)} %bitcast.18, bf16[512,1024]{1,0:T(8,128)(2,1)S(1)} %collective-permute-done.1.refs_1_, ...), custom_call_target="tpu_custom_call" | custom-call | flops 1073741824 | bytes 6291456 | tf_op jit(solution)/shard_map/pallas_call | solution.py:146
  124.6 8.4 %collective-permute-start.3 = (bf16[512,256]{1,0:T(8,128)(2,1)S(1)}, bf16[512,256]{1,0:T(8,128)(2,1)S(1)}, u32[]{:S(2)}, u32[]{:S(2)}) collective-permute-start(bf16[512,256]{1,0:T(8,128)(2,1)S(1)} %get-tuple-element.16), channel_id=1, source_target_pairs={{0,1},{1,0},{2,3},{3,2},{4,5},{5,4},{6,7},{7,6},{8,9},{9,8},{10,11... | collective-permute-start | bytes 786440 | tf_op jit(solution)/shard_map/ppermute | solution.py:182
  133.0 1.1 collective-permute-done.3.got_ref
  134.2 0.9 shard_map.77
  (1 shorter events, 0.0 us)
Async XLA Ops:
  4.3 6.3 %copy-start = (bf16[1,512,1024]{2,1,0:T(8,128)(2,1)S(1)}, bf16[1,512,1024]{2,1,0:T(8,128)(2,1)}, u32[]{:S(2)}) copy-start(bf16[1,512,1024]{2,1,0:T(8,128)(2,1)} %param.12) | copy-start | bytes 3145732
  4.3 29.3 %all-to-all-start = ((bf16[8,128,1024]{2,1,0:T(8,128)(2,1)}), bf16[8,128,1024]{2,1,0:T(8,128)(2,1)S(1)}, u32[]{:S(2)}, u32[]{:S(2)}) async-start(bf16[8,128,1024]{2,1,0:T(8,128)(2,1)} %bitcast.19), calls=%async_computation | async-start | bytes 4194304 | tf_op jit(solution)/shard_map/all_to_all | solution.py:24
  10.6 50.3 %collective-permute-start = (bf16[512,1024]{1,0:T(8,128)(2,1)S(1)}, bf16[512,1024]{1,0:T(8,128)(2,1)}, u32[]{:S(2)}, u32[]{:S(2)}) collective-permute-start(bf16[512,1024]{1,0:T(8,128)(2,1)S(1)} %bitcast.14), channel_id=1, source_target_pairs={{0,4},{1,5},{2,6},{3,7},{4,0},{5,1},{6,2},{7,3},{8,12},{9,13},{10,... | collective-permute-start | bytes 3145736 | tf_op jit(solution)/shard_map/ppermute | solution.py:182
  34.5 39.2 %all-to-all-start.1 = ((bf16[32,16,256]{2,1,0:T(8,128)(2,1)}), bf16[32,16,256]{2,1,0:T(8,128)(2,1)S(1)}, u32[]{:S(2)}, u32[]{:S(2)}) async-start(bf16[32,16,256]{2,1,0:T(8,128)(2,1)} %bitcast.7), calls=%async_computation.1 | async-start | bytes 524288 | tf_op jit(solution)/shard_map/all_to_all | solution.py:24
  54.6 28.8 %collective-permute-start.2 = (bf16[512,1024]{1,0:T(8,128)(2,1)S(1)}, bf16[512,1024]{1,0:T(8,128)(2,1)S(1)}, u32[]{:S(2)}, u32[]{:S(2)}) collective-permute-start(bf16[512,1024]{1,0:T(8,128)(2,1)S(1)} %bitcast.15), channel_id=1, source_target_pairs={{0,6},{1,7},{2,4},{3,5},{4,2},{5,3},{6,0},{7,1},{8,14},{9,15},{10,... | collective-permute-start | bytes 3145736 | tf_op jit(solution)/shard_map/ppermute | solution.py:182
  59.0 26.5 %collective-permute-start.1 = (bf16[512,1024]{1,0:T(8,128)(2,1)S(1)}, bf16[512,1024]{1,0:T(8,128)(2,1)S(1)}, u32[]{:S(2)}, u32[]{:S(2)}) collective-permute-start(bf16[512,1024]{1,0:T(8,128)(2,1)S(1)} %bitcast.16), channel_id=1, source_target_pairs={{0,2},{1,3},{2,0},{3,1},{4,6},{5,7},{6,4},{7,5},{8,10},{9,11},{10,... | collective-permute-start | bytes 3145736 | tf_op jit(solution)/shard_map/ppermute | solution.py:182
  74.5 19.1 %all-to-all-start.2 = ((bf16[8,4,16,256]{3,2,1,0:T(8,128)(2,1)}), bf16[8,4,16,256]{3,2,1,0:T(8,128)(2,1)}, u32[]{:S(2)}, u32[]{:S(2)}) async-start(bf16[8,4,16,256]{3,2,1,0:T(8,128)(2,1)} %broadcast_in_dim.20), calls=%async_computation.2 | async-start | bytes 524288 | tf_op jit(solution)/shard_map/all_to_all | solution.py:24
  124.6 9.6 %collective-permute-start.3 = (bf16[512,256]{1,0:T(8,128)(2,1)S(1)}, bf16[512,256]{1,0:T(8,128)(2,1)S(1)}, u32[]{:S(2)}, u32[]{:S(2)}) collective-permute-start(bf16[512,256]{1,0:T(8,128)(2,1)S(1)} %get-tuple-element.16), channel_id=1, source_target_pairs={{0,1},{1,0},{2,3},{3,2},{4,5},{5,4},{6,7},{7,6},{8,9},{9,8},{10,11... | collective-permute-start | bytes 786440 | tf_op jit(solution)/shard_map/ppermute | solution.py:182

commit v10 on v7

--- a/solution.py
+++ b/solution.py
@@ -207,7 +207,9 @@
     weight = exchange(jnp.broadcast_to(mine[None], (8, *mine.shape)), NEAR)
     weight = weight.reshape(8, 8, 4, -1, 2 * R)
     keep, send = project(weight, squares, (x_own, x_up, x_far, x_down))
-    return finish(keep, squares, swap(send, 1))[None]
+    got = swap(send, 1).astype(F32)
+    scale = lax.rsqrt((squares[:, :1] + got[:, R : R + 1] + got[:, -1:]) / D + 1e-05)
+    return ((keep + got[:, :R]) * scale).astype(BF16)[None]
 
 
 def solution(mesh):

time: 135 us -> 135 us (level)
  no operation moved by 1% of the time
where the time goes in v10:
time: 135 us
  starting transfers between devices  50.8 us (38%)
  waiting for transfers between devices  42.7 us (32%)
  blocking collectives  27.9 us (21%)
  Pallas kernels  11.2 us (8%)
    all_to_all x3, waiting for transfers between devices, exchange(): return lax.all_to_all(blocks, axes, 0, 0)  37.1 us
    all_to_all x3, starting transfers between devices, exchange(): return lax.all_to_all(blocks, axes, 0, 0)  31.6 us
    all_to_all x1, blocking collectives, exchange(): return lax.all_to_all(blocks, axes, 0, 0)  27.9 us
    ppermute x4, starting transfers between devices, swap(): return lax.ppermute(block, TENSOR, [(t, t ^ bits) for t in range(8)])  19.2 us
    ppermute x4, waiting for transfers between devices, swap(): return lax.ppermute(block, TENSOR, [(t, t ^ bits) for t in range(8)])  5.65 us
    pallas_call x1, Pallas kernels, share(): pl.pallas_call(share_kernel, grid=(features // width,), in_specs=[pl.Bloc...  4.31 us
    pallas_call x1, Pallas kernels, squares_of(): pl.pallas_call(squares_kernel, in_specs=[vmem] * 4, out_specs=vmem, out_s...  3.06 us
    pallas_call x1, Pallas kernels, project(): pl.pallas_call(project_kernel, in_specs=[vmem] * 6, out_specs=(vmem,) * 2...  2.85 us
  transfers between devices with their start and end apart: 7, of which 5 were waited for; matrix products, arithmetic and copies ran while one was open for 1% of the time, Pallas kernels for 3%

profile of v10, /device:TPU:1, one launch (start us, length us, event | category | flops | bytes accessed | tf_op | source)
XLA Modules:
  0.0 134.6 jit_solution(707447717072491603)
XLA Ops:
  0.0 4.3 %shard_map.73 = bf16[1024,1024]{1,0:T(8,128)(2,1)} custom-call(bf16[512,1024]{1,0:T(8,128)(2,1)} %bitcast.23, bf16[512,1024]{1,0:T(8,128)(2,1)} %bitcast.24, bf16[128,1024]{1,0:T(8,128)(2,1)} %bitcast.25, f32[128,128]{1,0:T(8,128)} %bitcast.26, f32[128,128]{1,0:T(8,128)} %bitcast.27, f32[1,1024]{1,0:T(1,128)} %bitcast.28), custom_call_target="tpu_custom_call" | custom-call | flops 1073741824 | bytes 6291456 | tf_op jit(solution)/shard_map/pallas_call | solution.py:56
  4.3 0.0 copy-start
  4.3 6.3 %all-to-all-start = ((bf16[8,128,1024]{2,1,0:T(8,128)(2,1)}), bf16[8,128,1024]{2,1,0:T(8,128)(2,1)S(1)}, u32[]{:S(2)}, u32[]{:S(2)}) async-start(bf16[8,128,1024]{2,1,0:T(8,128)(2,1)} %bitcast.20), calls=%async_computation | async-start | bytes 4194304 | tf_op jit(solution)/shard_map/all_to_all | solution.py:24
  10.6 0.0 copy-done
  10.6 4.7 %collective-permute-start.1 = (bf16[512,1024]{1,0:T(8,128)(2,1)S(1)}, bf16[512,1024]{1,0:T(8,128)(2,1)}, u32[]{:S(2)}, u32[]{:S(2)}) collective-permute-start(bf16[512,1024]{1,0:T(8,128)(2,1)S(1)} %bitcast.15), channel_id=1, source_target_pairs={{0,6},{1,7},{2,4},{3,5},{4,2},{5,3},{6,0},{7,1},{8,14},{9,15},{10,... | collective-permute-start | bytes 3145736 | tf_op jit(solution)/shard_map/ppermute | solution.py:182
  15.3 1.9 %collective-permute-start = (bf16[512,1024]{1,0:T(8,128)(2,1)S(1)}, bf16[512,1024]{1,0:T(8,128)(2,1)}, u32[]{:S(2)}, u32[]{:S(2)}) collective-permute-start(bf16[512,1024]{1,0:T(8,128)(2,1)S(1)} %bitcast.16), channel_id=1, source_target_pairs={{0,2},{1,3},{2,0},{3,1},{4,6},{5,7},{6,4},{7,5},{8,10},{9,11},{10,... | collective-permute-start | bytes 3145736 | tf_op jit(solution)/shard_map/ppermute | solution.py:182
  17.2 16.2 %all-to-all-done.blocks_ref = bf16[8,128,1024]{2,1,0:T(8,128)(2,1)S(1)} async-done(((bf16[8,128,1024]{2,1,0:T(8,128)(2,1)}), bf16[8,128,1024]{2,1,0:T(8,128)(2,1)S(1)}, u32[]{:S(2)}, u32[]{:S(2)}) %all-to-all-start) | async-done | bytes 2097184 | tf_op jit(solution)/shard_map/all_to_all | solution.py:24
  33.5 1.0 shard_map.74
  34.4 20.2 %all-to-all-start.1 = ((bf16[32,16,256]{2,1,0:T(8,128)(2,1)}), bf16[32,16,256]{2,1,0:T(8,128)(2,1)S(1)}, u32[]{:S(2)}, u32[]{:S(2)}) async-start(bf16[32,16,256]{2,1,0:T(8,128)(2,1)} %bitcast.7), calls=%async_computation.1 | async-start | bytes 524288 | tf_op jit(solution)/shard_map/all_to_all | solution.py:24
  54.6 4.6 %collective-permute-start.2 = (bf16[512,1024]{1,0:T(8,128)(2,1)S(1)}, bf16[512,1024]{1,0:T(8,128)(2,1)S(1)}, u32[]{:S(2)}, u32[]{:S(2)}) collective-permute-start(bf16[512,1024]{1,0:T(8,128)(2,1)S(1)} %bitcast.17), channel_id=1, source_target_pairs={{0,4},{1,5},{2,6},{3,7},{4,0},{5,1},{6,2},{7,3},{8,12},{9,13},{10,... | collective-permute-start | bytes 3145736 | tf_op jit(solution)/shard_map/ppermute | solution.py:182
  59.3 0.0 collective-permute-done.1.refs_3_
  59.3 0.0 collective-permute-done.refs_1_
  59.3 14.4 %all-to-all-done.1 = bf16[32,16,256]{2,1,0:T(8,128)(2,1)S(1)} async-done(((bf16[32,16,256]{2,1,0:T(8,128)(2,1)}), bf16[32,16,256]{2,1,0:T(8,128)(2,1)S(1)}, u32[]{:S(2)}, u32[]{:S(2)}) %all-to-all-start.1) | async-done | bytes 262176 | tf_op jit(solution)/shard_map/all_to_all | solution.py:24
  73.8 0.7 broadcast_in_dim.20
  74.5 5.1 %all-to-all-start.2 = ((bf16[8,4,16,256]{3,2,1,0:T(8,128)(2,1)}), bf16[8,4,16,256]{3,2,1,0:T(8,128)(2,1)S(1)}, u32[]{:S(2)}, u32[]{:S(2)}) async-start(bf16[8,4,16,256]{3,2,1,0:T(8,128)(2,1)} %broadcast_in_dim.20), calls=%async_computation.2 | async-start | bytes 524288 | tf_op jit(solution)/shard_map/all_to_all | solution.py:24
  79.6 4.5 %collective-permute-done.2.refs_2_ = bf16[512,1024]{1,0:T(8,128)(2,1)S(1)} collective-permute-done((bf16[512,1024]{1,0:T(8,128)(2,1)S(1)}, bf16[512,1024]{1,0:T(8,128)(2,1)S(1)}, u32[]{:S(2)}, u32[]{:S(2)}) %collective-permute-start.2) | collective-permute-done | bytes 1048608 | tf_op jit(solution)/shard_map/ppermute | solution.py:182
  84.1 3.1 %shard_map.75.squares_ref = f32[512,128]{1,0:T(8,128)S(1)} custom-call(bf16[512,1024]{1,0:T(8,128)(2,1)S(1)} %bitcast.18, bf16[512,1024]{1,0:T(8,128)(2,1)} %collective-permute-done.refs_1_, bf16[512,1024]{1,0:T(8,128)(2,1)S(1)} %collective-permute-done.2.refs_2_, bf16[512,1024]{1,0:T(8,128)(2,1)} %collective-permute-done.1.refs_3_), custom_call_target="tpu_custom_call" | custom-call | flops 4194304 | bytes 4194304 | tf_op jit(solution)/shard_map/pallas_call | solution.py:114
  87.2 6.4 %all-to-all-done.2 = bf16[8,4,16,256]{3,2,1,0:T(8,128)(2,1)S(1)} async-done(((bf16[8,4,16,256]{3,2,1,0:T(8,128)(2,1)}), bf16[8,4,16,256]{3,2,1,0:T(8,128)(2,1)S(1)}, u32[]{:S(2)}, u32[]{:S(2)}) %all-to-all-start.2) | async-done | bytes 262176 | tf_op jit(solution)/shard_map/all_to_all | solution.py:24
  93.6 0.1 broadcast_in_dim.22
  93.7 27.9 %all_to_all.20 = bf16[8,512,256]{2,1,0:T(8,128)(2,1)S(1)} all-to-all(bf16[8,512,256]{2,1,0:T(8,128)(2,1)S(1)} %broadcast_in_dim.22), channel_id=1, replica_groups=mesh['x'=4,'z3'=2,'z2'=2,'z1'=2,'z0'=2,'y'=4,'c'=2] {'x','z0'}, dimensions={0} | all-to-all | bytes 4194304 | tf_op jit(solution)/shard_map/all_to_all | solution.py:24
  121.6 2.9 %shard_map.76 = (f32[512,128]{1,0:T(8,128)S(1)}, bf16[512,256]{1,0:T(8,128)(2,1)S(1)}) custom-call(bf16[8,8,4,16,256]{4,3,2,1,0:T(8,128)(2,1)S(1)} %bitcast.14, f32[512,128]{1,0:T(8,128)S(1)} %shard_map.75.squares_ref, bf16[512,1024]{1,0:T(8,128)(2,1)S(1)} %bitcast.19, bf16[512,1024]{1,0:T(8,128)(2,1)} %collective-permute-done.refs_1_, ...), custom_call_target="tpu_custom_call" | custom-call | flops 1073741824 | bytes 6291456 | tf_op jit(solution)/shard_map/pallas_call | solution.py:146
  124.4 7.9 %collective-permute-start.3 = (bf16[512,256]{1,0:T(8,128)(2,1)S(1)}, bf16[512,256]{1,0:T(8,128)(2,1)S(1)}, u32[]{:S(2)}, u32[]{:S(2)}) collective-permute-start(bf16[512,256]{1,0:T(8,128)(2,1)S(1)} %get-tuple-element.20), channel_id=1, source_target_pairs={{0,1},{1,0},{2,3},{3,2},{4,5},{5,4},{6,7},{7,6},{8,9},{9,8},{10,11... | collective-permute-start | bytes 786440 | tf_op jit(solution)/shard_map/ppermute | solution.py:182
  132.4 1.1 collective-permute-done.3
  133.6 0.2 fusion.3
  133.8 0.8 fusion.6
  (2 shorter events, 0.1 us)
Async XLA Ops:
  4.3 6.3 %copy-start = (bf16[1,512,1024]{2,1,0:T(8,128)(2,1)S(1)}, bf16[1,512,1024]{2,1,0:T(8,128)(2,1)}, u32[]{:S(2)}) copy-start(bf16[1,512,1024]{2,1,0:T(8,128)(2,1)} %param.12) | copy-start | bytes 3145732
  4.3 29.2 %all-to-all-start = ((bf16[8,128,1024]{2,1,0:T(8,128)(2,1)}), bf16[8,128,1024]{2,1,0:T(8,128)(2,1)S(1)}, u32[]{:S(2)}, u32[]{:S(2)}) async-start(bf16[8,128,1024]{2,1,0:T(8,128)(2,1)} %bitcast.20), calls=%async_computation | async-start | bytes 4194304 | tf_op jit(solution)/shard_map/all_to_all | solution.py:24
  10.6 48.6 %collective-permute-start.1 = (bf16[512,1024]{1,0:T(8,128)(2,1)S(1)}, bf16[512,1024]{1,0:T(8,128)(2,1)}, u32[]{:S(2)}, u32[]{:S(2)}) collective-permute-start(bf16[512,1024]{1,0:T(8,128)(2,1)S(1)} %bitcast.15), channel_id=1, source_target_pairs={{0,6},{1,7},{2,4},{3,5},{4,2},{5,3},{6,0},{7,1},{8,14},{9,15},{10,... | collective-permute-start | bytes 3145736 | tf_op jit(solution)/shard_map/ppermute | solution.py:182
  15.3 44.0 %collective-permute-start = (bf16[512,1024]{1,0:T(8,128)(2,1)S(1)}, bf16[512,1024]{1,0:T(8,128)(2,1)}, u32[]{:S(2)}, u32[]{:S(2)}) collective-permute-start(bf16[512,1024]{1,0:T(8,128)(2,1)S(1)} %bitcast.16), channel_id=1, source_target_pairs={{0,2},{1,3},{2,0},{3,1},{4,6},{5,7},{6,4},{7,5},{8,10},{9,11},{10,... | collective-permute-start | bytes 3145736 | tf_op jit(solution)/shard_map/ppermute | solution.py:182
  34.4 39.3 %all-to-all-start.1 = ((bf16[32,16,256]{2,1,0:T(8,128)(2,1)}), bf16[32,16,256]{2,1,0:T(8,128)(2,1)S(1)}, u32[]{:S(2)}, u32[]{:S(2)}) async-start(bf16[32,16,256]{2,1,0:T(8,128)(2,1)} %bitcast.7), calls=%async_computation.1 | async-start | bytes 524288 | tf_op jit(solution)/shard_map/all_to_all | solution.py:24
  54.6 29.5 %collective-permute-start.2 = (bf16[512,1024]{1,0:T(8,128)(2,1)S(1)}, bf16[512,1024]{1,0:T(8,128)(2,1)S(1)}, u32[]{:S(2)}, u32[]{:S(2)}) collective-permute-start(bf16[512,1024]{1,0:T(8,128)(2,1)S(1)} %bitcast.17), channel_id=1, source_target_pairs={{0,4},{1,5},{2,6},{3,7},{4,0},{5,1},{6,2},{7,3},{8,12},{9,13},{10,... | collective-permute-start | bytes 3145736 | tf_op jit(solution)/shard_map/ppermute | solution.py:182
  74.5 19.1 %all-to-all-start.2 = ((bf16[8,4,16,256]{3,2,1,0:T(8,128)(2,1)}), bf16[8,4,16,256]{3,2,1,0:T(8,128)(2,1)S(1)}, u32[]{:S(2)}, u32[]{:S(2)}) async-start(bf16[8,4,16,256]{3,2,1,0:T(8,128)(2,1)} %broadcast_in_dim.20), calls=%async_computation.2 | async-start | bytes 524288 | tf_op jit(solution)/shard_map/all_to_all | solution.py:24
  124.4 9.1 %collective-permute-start.3 = (bf16[512,256]{1,0:T(8,128)(2,1)S(1)}, bf16[512,256]{1,0:T(8,128)(2,1)S(1)}, u32[]{:S(2)}, u32[]{:S(2)}) collective-permute-start(bf16[512,256]{1,0:T(8,128)(2,1)S(1)} %get-tuple-element.20), channel_id=1, source_target_pairs={{0,1},{1,0},{2,3},{3,2},{4,5},{5,4},{6,7},{7,6},{8,9},{9,8},{10,11... | collective-permute-start | bytes 786440 | tf_op jit(solution)/shard_map/ppermute | solution.py:182
